TPU v7x, 32 devices: a whole 2x2x4 slice. The times are simulated.
32 devices in a mesh: groups: 2 (over x), dp: 2 (over core), tensor: 8 (over z, y).
Axes of the slice: x: 2, y: 2, z: 4, core: 2. Of those that a mesh axis runs over, the one named last changes fastest.
Arguments:
- tokens: bfloat16 [1024, 8192], P(('groups', 'dp'), 'tensor'), parts along dimension 0, may hold values from -6 to 6
- cotangent: bfloat16 [1024, 8192], P(('groups', 'dp'), 'tensor'), parts along dimension 0, may hold values from -6 to 6
- gate_weight: bfloat16 [8192, 14336], P(None, 'tensor'), may hold values from -0.09375 to 0.09375
- up_weight: bfloat16 [8192, 14336], P(None, 'tensor'), may hold values from -0.0625 to 0.0625
- down_matrix_frozen: bfloat16 [14336, 8192], P('tensor'), may hold values from -0.046875 to 0.046875
- adapter_a: bfloat16 [32, 14336, 64], P('groups', 'tensor'), parts along dimension 0, may hold values from -0.046875 to 0.046875
- adapter_b: bfloat16 [32, 64, 8192], P('groups', None, 'tensor'), parts along dimension 0, may hold values from -0.75 to 0.75
- tenant: int32 [8], P(('groups', 'dp')), parts along dimension 0, may hold values from 0 to 15
- ranks: int32 [32], P('groups'), parts along dimension 0, may hold values from 8 to 64
Outputs:
- grad_input: bfloat16 [1024, 8192], P(('groups', 'dp'), 'tensor'), parts along dimension 0
- grad_a: float32 [32, 14336, 64], P('groups', 'tensor'), parts along dimension 0
- grad_b: float32 [32, 64, 8192], P('groups', None, 'tensor'), parts along dimension 0
There are 2 independent parts, one for each index of `groups`. A program takes and returns all parts, laid end to end along the dimension named above; an argument that names none is the same for every part. Nothing has to cross between parts.
Inputs may be any that keep to these rules, and one draw needn't show every extreme that they name: Each tenant's adapter uses only its first ranks[t] of 64 rank columns; blocks are labelled independently, so tenants hold uneven numbers of blocks. Every block of 128 tokens belongs to one tenant.
All inputs are finite; a program needn't handle non-finite values.
Results may differ from a plain program's by a relative error of at most 0.0065.
Values may be sent and summed in bfloat16 or wider, within the bound.
No kernel may reach another device: no remote copies, remote signals or barrier semaphores. Data moves between devices by JAX's collectives and lax.ppermute only.
A program may use at most 256 MiB of HBM per device.

v0:
```python
import jax
import jax.numpy as jnp
from jax import lax
from jax.sharding import PartitionSpec as P

adapter_alpha_factor = 32.0


def contract_trailing_axis(left, right):
    return lax.dot_general(
        left, right, (((1,), (1,)), ((), ())), preferred_element_type=jnp.float32
    )


def local(
    tokens,
    cotangent,
    gate_weight,
    up_weight,
    down_matrix_frozen,
    adapter_a,
    adapter_b,
    tenant,
    ranks,
):
    row_number_total = tokens.shape[0]
    block_count = tenant.shape[0]
    block_len = row_number_total // block_count
    rank_width = adapter_a.shape[2]
    tenant_count = adapter_a.shape[0]
    hidden_shard_slice = gate_weight.shape[1]
    shard_piece = lax.all_gather(tokens, "tensor", axis=1, tiled=True)
    gate_pre = jnp.dot(shard_piece, gate_weight, preferred_element_type=jnp.float32)
    up_pre = jnp.dot(shard_piece, up_weight, preferred_element_type=jnp.float32)
    sigma_gate = jax.nn.sigmoid(gate_pre)
    activated = gate_pre * sigma_gate
    hidden = (activated * up_pre).astype(jnp.bfloat16)
    mask_table = (
        lax.broadcasted_iota(jnp.int32, (tenant_count, rank_width), 1) < ranks[:, None]
    ).astype(jnp.float32)
    tenant_scale_lookup = adapter_alpha_factor / ranks.astype(jnp.float32)
    onehot = (
        tenant[:, None] == lax.broadcasted_iota(jnp.int32, (block_count, tenant_count), 1)
    ).astype(jnp.float32)
    block_mask = jnp.dot(onehot, mask_table, precision=lax.Precision.HIGHEST)
    block_scale = jnp.dot(onehot, tenant_scale_lookup, precision=lax.Precision.HIGHEST)
    hid_blocks = hidden.reshape(block_count, block_len, hidden_shard_slice)
    cot_blocks = cotangent.reshape(block_count, block_len, cotangent.shape[1])
    selected_down_adapter = adapter_a[tenant]
    b_chosen = adapter_b[tenant]
    low_part = jnp.einsum(
        "bnf,bfr->bnr", hid_blocks, selected_down_adapter, preferred_element_type=jnp.float32
    )
    back_part = jnp.einsum("bnd,brd->bnr", cot_blocks, b_chosen, preferred_element_type=jnp.float32)
    low_part = low_part * block_mask[:, None, :]
    back_part = back_part * block_mask[:, None, :]
    low_sum, back_sum = lax.psum((low_part, back_part), "tensor")
    low_bf = low_sum.astype(jnp.bfloat16)
    backward_half_precision = (back_sum * block_scale[:, None, None]).astype(jnp.bfloat16)
    adapter_gradient_term = jnp.einsum(
        "gpl,gdl->gpd",
        backward_half_precision,
        selected_down_adapter,
        preferred_element_type=jnp.float32,
    )
    adapter_gradient_term = adapter_gradient_term.reshape(row_number_total, hidden_shard_slice)
    hidden_gradient = adapter_gradient_term + contract_trailing_axis(
        lax.all_gather(cotangent, "tensor", axis=1, tiled=True), down_matrix_frozen
    )
    block_a = jnp.einsum(
        "bnf,bnr->bfr", hid_blocks, backward_half_precision, preferred_element_type=jnp.float32
    )
    grad_a_part = jnp.einsum("bt,bfr->tfr", onehot, block_a, precision=lax.Precision.HIGHEST)
    block_b = jnp.einsum("bnr,bnd->brd", low_bf, cot_blocks, preferred_element_type=jnp.float32)
    grad_b_part = jnp.einsum("bt,brd->trd", onehot, block_b, precision=lax.Precision.HIGHEST)
    grad_b_part = grad_b_part * tenant_scale_lookup[:, None, None]
    grad_a, grad_b = (
        lax.psum(grad_a_part.astype(jnp.bfloat16), "dp").astype(jnp.float32),
        lax.psum(grad_b_part.astype(jnp.bfloat16), "dp").astype(jnp.float32),
    )
    grad_gate = (
        hidden_gradient * up_pre * sigma_gate * (1.0 + gate_pre * (1.0 - sigma_gate))
    ).astype(jnp.bfloat16)
    grad_up = (hidden_gradient * activated).astype(jnp.bfloat16)
    input_term = contract_trailing_axis(grad_gate, gate_weight) + contract_trailing_axis(
        grad_up, up_weight
    )
    grad_input = lax.psum_scatter(input_term, "tensor", scatter_dimension=1, tiled=True).astype(
        jnp.bfloat16
    )
    return (grad_input, grad_a, grad_b)


def solution(mesh):
    return jax.shard_map(
        local,
        mesh=mesh,
        in_specs=(
            P(("groups", "dp"), "tensor"),
            P(("groups", "dp"), "tensor"),
            P(None, "tensor"),
            P(None, "tensor"),
            P("tensor", None),
            P("groups", "tensor", None),
            P("groups", None, "tensor"),
            P(("groups", "dp")),
            P("groups"),
        ),
        out_specs=(
            P(("groups", "dp"), "tensor"),
            P("groups", "tensor", None),
            P("groups", None, "tensor"),
        ),
        check_vma=False,
    )
```

profile of v0, /device:TPU:0, one launch (start us, length us, event | category | flops | bytes accessed | tf_op | source)
XLA Modules:
  0.0 456.8 jit_solution(11939597452084389677)
XLA Ops:
  7.2 0.0 all-reduce.4.cloned.1.call-start
  7.2 0.8 compare_select_fusion
  8.0 0.9 fusion.9
  8.9 0.6 gather_fusion
  9.5 2.0 fusion.1
  11.5 0.0 all-gather.5.cloned.1.call-start
  11.5 0.7 all-gather.5.cloned.1.call-update
  12.2 0.0 all-gather.3.cloned.1.call-start
  12.3 0.7 all-gather.3.cloned.1.call-update
  13.0 0.0 all-reduce.6.cloned.1.call-start
  13.0 2.6 gather_fusion.1
  15.7 0.2 convolution_bitcast_fusion
  15.8 67.3 %all-reduce.4.cloned.1.call-done = f32[2,128,64]{1,2,0:T(8,128)} async-done(((f32[2,128,64]{1,2,0:T(8,128)}), f32[2,128,64]{1,2,0:T(8,128)}) %all-reduce.4.cloned.1.call-update) | async-done | bytes 65552 | tf_op jit(solution)/shard_map/psum | solution.py:57
  83.2 1.3 fusion.21
  84.5 74.2 %all-gather.5.cloned.1.call-done = bf16[256,8192]{1,0:T(8,128)(2,1)} async-done(((bf16[256,1024]{1,0:T(8,128)(2,1)}), bf16[256,8192]{1,0:T(8,128)(2,1)}) %all-gather.5.cloned.1.call-update) | async-done | bytes 4194320 | tf_op jit(solution)/shard_map/all_gather | solution.py:32
  158.7 19.5 %fusion.22 = f32[256,1792]{1,0:T(8,128)S(1)} fusion(bf16[256,8192]{1,0:T(8,128)(2,1)} %all-gather.5.cloned.1.call-done, bf16[8192,1792]{1,0:T(8,128)(2,1)} %param.11), kind=kOutput, calls=%fused_computation.40 | convolution fusion | flops 7516192768 | bytes 35389440 | tf_op jit(solution)/shard_map/dot_general | solution.py:33
  178.2 15.8 %multiply_convert_fusion.1 = (bf16[256,1792]{1,0:T(8,128)(2,1)S(1)}, f32[256,1792]{1,0:T(8,128)}) fusion(f32[256,1792]{1,0:T(8,128)S(1)} %fusion.22, bf16[256,8192]{1,0:T(8,128)(2,1)S(1)} %copy-done.7, bf16[8192,1792]{1,0:T(8,128)(2,1)} %param.12), kind=kOutput, calls=%fused_computation.6 | convolution fusion | flops 7518945280 | bytes 38141952 | tf_op jit(solution)/shard_map/dot_general | solution.py:34
  194.0 0.9 copy-done.4
  194.9 0.4 convolution_multiply_fusion
  195.3 38.3 %psum.30 = bf16[2,128,64]{2,1,0:T(8,128)(2,1)S(1)} all-reduce(f32[2,128,64]{2,1,0:T(8,128)S(1)} %convolution_multiply_fusion), channel_id=1, replica_groups=mesh['groups'=2,'dp'=2,'tensor'=8] {'tensor'}, use_global_device_ids=true, to_apply=%region_3.0 | all-reduce | flops 16384 | bytes 98304 | tf_op jit(solution)/shard_map/psum | solution.py:57
  233.6 0.3 fusion.23
  233.9 1.5 fusion.20
  235.4 3.5 multiply_convert_fusion
  238.9 5.1 %convolution_convert_fusion = bf16[16,1792,64]{1,0,2:T(8,128)(2,1)} fusion(f32[2,1792,64]{1,2,0:T(8,128)S(1)} %fusion.20, s32[2]{0:T(128)S(1)} %copy-done.6), kind=kOutput, calls=%fused_computation.4 | convolution fusion | flops 45875232 | bytes 4587528 | tf_op jit(solution)/shard_map/bt,bfr->tfr/dot_general | solution.py:73
  244.0 0.0 reduce-scatter.2.cloned.1.call-start
  244.1 17.9 %convolution_add_fusion.1 = f32[256,1792]{1,0:T(8,128)} fusion(f32[256,1792]{1,0:T(8,128)S(1)} %bitcast.33, bf16[256,8192]{1,0:T(8,128)(2,1)} %all-gather.3.cloned.1.call-done, bf16[1792,8192]{1,0:T(8,128)(2,1)} %param.13), kind=kOutput, calls=%fused_computation.5 | convolution fusion | flops 7516651520 | bytes 37224448 | tf_op jit(solution)/shard_map/dot_general | solution.py:10
  262.0 20.1 %fusion.2 = f32[256,8192]{1,0:T(8,128)} fusion(bf16[8192,1792]{1,0:T(8,128)(2,1)} %param.11, f32[256,1792]{1,0:T(8,128)} %copy-done.9, f32[256,1792]{1,0:T(8,128)} %convolution_add_fusion.1, f32[256,1792]{1,0:T(8,128)} %get-tuple-element.9), kind=kOutput, calls=%fused_computation.15 | convolution fusion | flops 7520780288 | bytes 43253760 | tf_op jit(solution)/shard_map/dot_general | solution.py:10
  282.2 19.3 %convolution_add_fusion = f32[256,8192]{1,0:T(8,128)} fusion(f32[256,8192]{1,0:T(8,128)} %fusion.2, bf16[8192,1792]{1,0:T(8,128)(2,1)} %param.12, f32[256,1792]{1,0:T(8,128)} %convolution_add_fusion.1, f32[256,1792]{1,0:T(8,128)S(1)} %copy-done.10), kind=kOutput, calls=%fused_computation.2 | convolution fusion | flops 7521042432 | bytes 49807360 | tf_op jit(solution)/shard_map/dot_general | solution.py:10
  301.5 6.5 %copy.12 = f32[16,1792,64]{1,2,0:T(8,128)} copy(bf16[16,1792,64]{1,0,2:T(8,128)(2,1)} %get-tuple-element.6) | data formatting | bytes 11010048
  308.1 3.2 copy.13
  311.3 136.8 %reduce-scatter.2.cloned.1.call-done = f32[256,1024]{1,0:T(8,128)} async-done(((f32[256,8192]{1,0:T(8,128)}), f32[256,1024]{1,0:T(8,128)}) %reduce-scatter.2.cloned.1.call-update) | async-done | bytes 1048592 | tf_op jit(solution)/shard_map/reduce_scatter | solution.py:88
  448.1 2.1 convert_element_type.39
  (28 shorter events, 0.2 us)
Async XLA Ops:
  7.2 1.7 copy-start
  7.2 76.0 %all-reduce.4.cloned.1.call-start = ((), (), s32[]{:S(2)}) async-start(), calls=%async_computation.1 | async-start | bytes 131072 | tf_op jit(solution)/shard_map/psum | solution.py:57
  8.9 6.7 %copy-start.8 = (s32[16]{0:T(128)S(1)}, s32[16]{0:T(128)}, u32[]{:S(2)}) copy-start(s32[16]{0:T(128)} %param.17) | copy-start | bytes 196
  8.9 6.8 %copy-start.6 = (s32[2]{0:T(128)S(1)}, s32[2]{0:T(128)}, u32[]{:S(2)}) copy-start(s32[2]{0:T(128)} %param.16) | copy-start | bytes 28
  11.5 147.2 %all-gather.5.cloned.1.call-start = ((), (), s32[]{:S(2)}) async-start(), calls=%async_computation.3 | async-start | bytes 4718592 | tf_op jit(solution)/shard_map/all_gather | solution.py:32
  12.2 231.9 %all-gather.3.cloned.1.call-start = ((), (), s32[]{:S(2)}) async-start(), calls=%async_computation.2 | async-start | bytes 4718592 | tf_op jit(solution)/shard_map/all_gather | solution.py:68
  13.0 288.6 %all-reduce.6.cloned.1.call-start = ((), (), s32[]{:S(2)}) async-start(), calls=%async_computation.5 | async-start | bytes 11534336 | tf_op jit(solution)/shard_map/psum | solution.py:78
  158.7 19.5 %copy-start.7 = (bf16[256,8192]{1,0:T(8,128)(2,1)S(1)}, bf16[256,8192]{1,0:T(8,128)(2,1)}, u32[]{:S(2)}) copy-start(bf16[256,8192]{1,0:T(8,128)(2,1)} %all-gather.5.cloned.1.call-done) | copy-start | bytes 12582916
  178.2 15.8 %copy-start.9 = (f32[256,1792]{1,0:T(8,128)}, f32[256,1792]{1,0:T(8,128)S(1)}, u32[]{:S(2)}) copy-start(f32[256,1792]{1,0:T(8,128)S(1)} %fusion.22) | copy-start | bytes 5505028
  178.2 55.4 %copy-start.2 = (bf16[256,1024]{1,0:T(8,128)(2,1)S(1)}, bf16[256,1024]{1,0:T(8,128)(2,1)}, u32[]{:S(2)}) copy-start(bf16[256,1024]{1,0:T(8,128)(2,1)} %param.10) | copy-start | bytes 1572868
  194.0 0.9 copy-start.4
  194.0 39.9 %copy-start.5 = (f32[2,128,64]{1,2,0:T(8,128)S(1)}, f32[2,128,64]{1,2,0:T(8,128)}, u32[]{:S(2)}) copy-start(f32[2,128,64]{1,2,0:T(8,128)} %all-reduce.4.cloned.1.call-done) | copy-start | bytes 196612
  244.0 204.1 %reduce-scatter.2.cloned.1.call-start = ((), (), s32[]{:S(2)}) async-start(), calls=%async_computation.4 | async-start | bytes 9437184 | tf_op jit(solution)/shard_map/reduce_scatter | solution.py:88
  262.0 20.1 %copy-start.10 = (f32[256,1792]{1,0:T(8,128)S(1)}, f32[256,1792]{1,0:T(8,128)}, u32[]{:S(2)}) copy-start(f32[256,1792]{1,0:T(8,128)} %copy-done.9) | copy-start | bytes 5505028
  301.5 6.5 %copy-start.3 = (bf16[16,64,1024]{2,0,1:T(8,128)(2,1)S(1)}, bf16[16,64,1024]{2,0,1:T(8,128)(2,1)}, u32[]{:S(2)}) copy-start(bf16[16,64,1024]{2,0,1:T(8,128)(2,1)} %get-tuple-element.7) | copy-start | bytes 6291460
  308.1 142.2 %copy-start.1 = (bf16[16,64,1024]{2,1,0:T(8,128)(2,1)S(1)}, bf16[16,64,1024]{2,1,0:T(8,128)(2,1)}, u32[]{:S(2)}) copy-start(bf16[16,64,1024]{2,1,0:T(8,128)(2,1)} %param.15) | copy-start | bytes 6291460
Sparse Core Ops, SparseCore 0:
  12.0 71.1 all-reduce.3
  85.4 73.3 all-gather.4
  160.9 76.2 all-gather.2
  244.1 28.2 all-reduce.5
  301.6 146.4 reduce-scatter.1
where the time goes:
time: 457 us
  waiting for transfers between devices  280 us (61%)
  matrix products  108 us (24%)
  blocking collectives  38.3 us (8%)
  local copies, waits for them, and re-layouts  13.9 us (3%)
  between operations  13.9 us (3%)
    reduce_scatter x1, waiting for transfers between devices, local(): lax.psum_scatter(input_term, 'tensor', scatter_dimension=1, tiled=True)  137 us
    all_gather x1, waiting for transfers between devices, local(): shard_piece = lax.all_gather(tokens, 'tensor', axis=1, tiled=True)  74.2 us
    psum x1, waiting for transfers between devices, local(): low_sum, back_sum = lax.psum((low_part, back_part), 'tensor')  67.3 us
    dot_general x3, matrix products, contract_trailing_axis(): lax.dot_general(left, right, (((1,), (1,)), ((), ())), preferred_element_...  57.4 us
    psum x1, blocking collectives, local(): low_sum, back_sum = lax.psum((low_part, back_part), 'tensor')  38.3 us
    dot_general x1, matrix products, local(): jnp.dot(shard_piece, gate_weight, preferred_element_type=jnp.float32)  19.5 us
    dot_general x1, matrix products, local(): up_pre = jnp.dot(shard_piece, up_weight, preferred_element_type=jnp.float32)  15.8 us
    unnamed x24, local copies, waits for them, and re-layouts  10.7 us
  transfers between devices with their start and end apart: 5, of which 3 were waited for; matrix products, arithmetic and copies ran while one was open for 26% of the time, Pallas kernels for 0%

commit v1 on v0

--- a/solution.py
+++ b/solution.py
@@ -1,18 +1,587 @@
+import functools
+
 import jax
 import jax.numpy as jnp
 from jax import lax
+from jax.experimental import pallas as pl
+from jax.experimental.pallas import tpu as pltpu
 from jax.sharding import PartitionSpec as P
 
 adapter_alpha_factor = 32.0
+f32 = jnp.float32
+bf16 = jnp.bfloat16
+together = lax.optimization_barrier
+
+RING_PLAN = (
+    ("T10", "T00"),
+    ("C10", "C00"),
+    ("T20", "T10"),
+    ("C20", "C10"),
+    ("T30", "T20"),
+    ("C30", "C20"),
+    ("C21", "C11"),
+)
+PAIR_PLAN = (
+    ("T01", "T00"),
+    ("C01", "C00"),
+    ("T11", "T10"),
+    ("C11", "C10"),
+    ("T21", "T20"),
+    ("T31", "T30"),
+    ("C31", "C30"),
+)
+RING, PAIR = 4, 2
 
 
 def contract_trailing_axis(left, right):
     return lax.dot_general(
-        left, right, (((1,), (1,)), ((), ())), preferred_element_type=jnp.float32
-    )
-
-
-def local(
+        left, right, (((1,), (1,)), ((), ())), preferred_element_type=f32
+    )
+
+
+ANYWHERE = pl.BlockSpec(memory_space=pl.ANY)
+NEAR = pl.BlockSpec(memory_space=pltpu.VMEM)
+SCALARS = pl.BlockSpec(memory_space=pltpu.SMEM)
+MARK = jax.ShapeDtypeStruct((8, 128), f32)
+
+
+def cost(flops, weights):
+    return pl.CostEstimate(flops=flops, bytes_accessed=weights, transcendentals=0)
+
+
+def in_hbm(value):
+    return pltpu.with_memory_space_constraint(value, pltpu.HBM)
+
+
+def call(body, name, mark, scalars, far, out_shape, scratch, vmem, estimate):
+    def marked(*refs):
+        refs, (mark_ref, *scratch_refs) = refs[1 : ends + 1], refs[ends + 1 :]
+        mark_ref[...] = jnp.zeros_like(mark_ref)
+        body(*refs, *scratch_refs)
+
+    ends = len(scalars) + len(far) + len(out_shape)
+    return pl.pallas_call(
+        marked,
+        in_specs=[ANYWHERE] + [SCALARS] * len(scalars) + [ANYWHERE] * len(far),
+        out_specs=[ANYWHERE] * len(out_shape) + [NEAR],
+        out_shape=[*out_shape, MARK],
+        scratch_shapes=scratch,
+        compiler_params=pltpu.CompilerParams(vmem_limit_bytes=vmem << 20),
+        cost_estimate=estimate,
+        name=name,
+    )(mark, *scalars, *far)
+
+
+def at(index, size):
+    return pl.ds(pl.multiple_of(index * size, size), size)
+
+
+class Flow:
+    def __init__(self, far, close, sems, out=False):
+        self.far, self.close, self.sems, self.out = far, close, sems, out
+        self.slots = sems.shape[0]
+
+    def copy(self, n):
+        ends = (self.close(n), self.far(n)) if self.out else (self.far(n), self.close(n))
+        return pltpu.make_async_copy(*ends, self.sems.at[lax.rem(n, self.slots)])
+
+    def start(self, n):
+        self.copy(n).start()
+
+    def wait(self, n):
+        self.copy(n).wait()
+
+
+def tiles(steps, inward, *phases):
+    most = max([f.slots for f in inward])
+    for n in range(most):
+        for f in inward:
+            if n < min(f.slots, steps):
+                f.start(n)
+    share = steps // len(phases)
+    for p, (outward, compute) in enumerate(phases):
+
+        def step(k, carry, base=p * share, outward=outward, compute=compute):
+            n = base + k
+            for f in inward:
+                f.wait(n)
+            for f in outward:
+
+                @pl.when(k >= f.slots)
+                def _():
+                    f.wait(k - f.slots)
+
+            compute(n, [f.close(n) for f in inward], [f.close(k) for f in outward])
+            for f in outward:
+                f.start(k)
+            for f in inward:
+
+                @pl.when(n + f.slots < steps)
+                def _():
+                    f.start(n + f.slots)
+
+            return carry
+
+        lax.fori_loop(0, share, step, 0)
+    for outward, _ in phases:
+        for f in outward:
+            for k in range(max(0, share - f.slots), share):
+                f.wait(k)
+
+
+def buffers(slots, *shapes):
+    out = []
+    for shape, dtype in shapes:
+        out += [pltpu.VMEM((slots, *shape), dtype), pltpu.SemaphoreType.DMA((slots,))]
+    return out
+
+
+def flows(fars, scratch, out=False):
+    made = []
+    for i, far in enumerate(fars):
+        buffer, sems = scratch[2 * i : 2 * i + 2]
+        made.append(Flow(far, lambda n, b=buffer: b.at[lax.rem(n, b.shape[0])], sems, out))
+    return made
+
+
+class Refs:
+    def __init__(self, refs):
+        self.refs = list(refs)
+
+    def __call__(self, count):
+        got, self.refs = self.refs[:count], self.refs[count:]
+        return got
+
+
+def gate_up(mark, chunks, places, gate, up, sums, low=None, tile=256, slots=3):
+    count = len(chunks)
+    rows, depth = chunks[0].shape
+    hid = gate.shape[1]
+    blocks = 0 if low is None else low[0].shape[0]
+    length = 0 if low is None else rows // blocks
+    rank = 0 if low is None else low[1].shape[1]
+    scalars = [places] + ([] if low is None else [low[0]])
+    far = [*chunks, in_hbm(gate), in_hbm(up)] + ([] if sums is None else [in_hbm(t) for t in sums])
+    far += [] if low is None else [low[1]]
+    types = [f32, f32] if low is None else [f32, f32, bf16]
+    outs = [pltpu.HBM((rows, hid), t) for t in types]
+    if low is not None:
+        outs += [jax.ShapeDtypeStruct((blocks, length, rank), f32)]
+    scratch = buffers(1, *[((rows, depth), bf16)] * count)
+    scratch += buffers(slots, *[((depth, tile), bf16)] * (2 * count))
+    scratch += buffers(slots, *[((rows, tile), f32)] * (0 if sums is None else 2))
+    scratch += buffers(2, *[((rank, tile), bf16)] * blocks)
+    scratch += buffers(2, *[((rows, tile), t) for t in types])
+    scratch += [] if low is None else buffers(1, ((blocks, length, rank), f32))
+
+    def body(*refs):
+        take = Refs(refs)
+        (where,) = take(1)
+        label = take(1)[0] if low is not None else None
+        x_far = take(count)
+        weights = take(2)
+        sums_far = take(0 if sums is None else 2)
+        adapter = take(0 if low is None else 1)
+        out_far = take(len(types))
+        low_far = take(0 if low is None else 1)
+        x = flows([lambda n, r=r: r for r in x_far], take(2 * count))
+        w = flows(
+            [
+                lambda n, r=r, c=c: r.at[at(where[c], depth), at(n, tile)]
+                for r in weights
+                for c in range(count)
+            ],
+            take(4 * count),
+        )
+        w += flows([lambda n, r=r: r.at[:, at(n, tile)] for r in sums_far], take(2 * len(sums_far)))
+        w += flows(
+            [lambda n, b=b: adapter[0].at[label[b], :, at(n, tile)] for b in range(blocks)],
+            take(2 * blocks),
+        )
+        o = flows([lambda n, r=r: r.at[:, at(n, tile)] for r in out_far], take(2 * len(out_far)), True)
+        l = flows([lambda n, r=r: r for r in low_far], take(2 * len(low_far)), True)
+        for f in x:
+            f.start(0)
+        for f in l:
+            f.close(0)[...] = jnp.zeros((blocks, length, rank), f32)
+
+        def compute(n, got, put):
+            @pl.when(n == 0)
+            def _():
+                for f in x:
+                    f.wait(0)
+
+            found = []
+            for which in range(2):
+                total = None if sums is None else got[2 * count + which][...]
+                for c in range(count):
+                    term = jnp.dot(
+                        x[c].close(0)[...], got[which * count + c][...], preferred_element_type=f32
+                    )
+                    total = term if total is None else total + term
+                found.append(total)
+            if low is None:
+                put[0][...], put[1][...] = found
+                return
+            gate_pre, up_pre = found
+            sigma = jax.nn.sigmoid(gate_pre)
+            act = gate_pre * sigma
+            put[0][...] = act
+            put[1][...] = up_pre * sigma * (1.0 + gate_pre * (1.0 - sigma))
+            hidden = (act * up_pre).astype(bf16)
+            put[2][...] = hidden
+            for b in range(blocks):
+                l[0].close(0)[b] += contract_trailing_axis(
+                    hidden[b * length : (b + 1) * length], got[len(got) - blocks + b][...]
+                )
+
+        tiles(hid // tile, w, (o, compute))
+        for f in l:
+            f.start(0)
+            f.wait(0)
+
+    work = count * rows * depth * hid
+    estimate = cost(4 * work, 4 * work // rows)
+    return call(body, "gate_up", mark, scalars, far, outs, scratch, 32, estimate)
+
+
+def down_back(mark, chunks, rows, places, down, total, last=None, tile=256, slots=4):
+    count = len(chunks)
+    depth = chunks[0].shape[1]
+    hid = down.shape[0]
+    blocks = 0 if last is None else last[0].shape[0]
+    length = 0 if last is None else rows // blocks
+    rank = 0 if last is None else last[1].shape[1]
+    scalars = [places] + ([] if last is None else [last[0]])
+    far = [*chunks, in_hbm(down)] + ([] if total is None else [in_hbm(total)])
+    far += [] if last is None else [*last[1:3], in_hbm(last[3]), in_hbm(last[4])]
+    types = [f32] if last is None else [bf16, bf16]
+    scratch = buffers(1, *[((rows, depth), bf16)] * count)
+    scratch += buffers(slots, *[((tile, depth), bf16)] * count)
+    scratch += [] if total is None else buffers(slots, ((rows, tile), f32))
+    if last is not None:
+        scratch += buffers(1, ((blocks, length, rank), bf16))
+        scratch += buffers(slots, *[((rank, tile), bf16)] * blocks)
+        scratch += buffers(slots, *[((rows, tile), f32)] * 2)
+    scratch += buffers(2, *[((rows, tile), t) for t in types])
+
+    def body(*refs):
+        take = Refs(refs)
+        (where,) = take(1)
+        label = take(1)[0] if last is not None else None
+        x_far = take(count)
+        (weight,) = take(1)
+        total_far = take(0 if total is None else 1)
+        adapter, back_far = take(0 if last is None else 2) or (None, None)
+        factors = take(0 if last is None else 2)
+        out_far = take(len(types))
+        x = flows([lambda n, r=r: r.at[0:rows] for r in x_far], take(2 * count))
+        w = flows(
+            [lambda n, c=c: weight.at[at(n, tile), at(where[c], depth)] for c in range(count)],
+            take(2 * count),
+        )
+        w += flows([lambda n, r=r: r.at[:, at(n, tile)] for r in total_far], take(2 * len(total_far)))
+        if last is not None:
+            x += flows([lambda n: back_far], take(2))
+        w += flows(
+            [lambda n, b=b: adapter.at[label[b], :, at(n, tile)] for b in range(blocks)],
+            take(2 * blocks),
+        )
+        w += flows([lambda n, r=r: r.at[:, at(n, tile)] for r in factors], take(2 * len(factors)))
+        o = flows([lambda n, r=r: r.at[:, at(n, tile)] for r in out_far], take(2 * len(out_far)), True)
+        for f in x:
+            f.start(0)
+
+        def compute(n, got, put):
+            @pl.when(n == 0)
+            def _():
+                for f in x:
+                    f.wait(0)
+
+            value = None if total is None else got[count][...]
+            for c in range(count):
+                term = contract_trailing_axis(x[c].close(0)[...], got[c][...])
+                value = term if value is None else value + term
+            if last is None:
+                put[0][...] = value
+                return
+            *adapters, act, slope = got[len(got) - blocks - 2 :]
+            for b in range(blocks):
+                span = slice(b * length, (b + 1) * length)
+                grad = value[span] + jnp.dot(
+                    x[count].close(0)[b], adapters[b][...], preferred_element_type=f32
+                )
+                put[0][span] = (grad * slope[span]).astype(bf16)
+                put[1][span] = (grad * act[span]).astype(bf16)
+
+        tiles(hid // tile, w, (o, compute))
+
+    if last is None:
+        outs = [pltpu.HBM((rows, hid), f32)]
+    else:
+        outs = [jax.ShapeDtypeStruct((rows, hid), bf16)] * 2
+    work = count * rows * depth * hid
+    estimate = cost(2 * work, 2 * work // rows)
+    return call(body, "down_back", mark, scalars, far, outs, scratch, 24, estimate)
+
+
+def input_parts(mark, places, grads, gate, up, width, dtypes, tile=256, slots=4):
+    rows, hid = grads[0].shape
+    count = len(dtypes)
+    share = width // tile
+    scratch = buffers(1, *[((rows, hid), bf16)] * 2)
+    scratch += buffers(slots, *[((tile, hid), bf16)] * 2)
+    scratch += buffers(2, *[((rows, tile), t) for t in dtypes])
+
+    def body(*refs):
+        take = Refs(refs)
+        (where,) = take(1)
+        x_far, weights, out_far = take(2), take(2), take(count)
+
+        def tile_at(n):
+            return at(where[lax.div(n, share)] * share + lax.rem(n, share), tile)
+
+        x = flows([lambda n, r=r: r for r in x_far], take(4))
+        w = flows([lambda n, r=r: r.at[tile_at(n), :] for r in weights], take(4))
+        o = flows([lambda n, r=r: r.at[:, at(n, tile)] for r in out_far], take(2 * count), True)
+        for f in x:
+            f.start(0)
+
+        def compute(n, got, put):
+            @pl.when(n == 0)
+            def _():
+                for f in x:
+                    f.wait(0)
+
+            put[0][...] = (
+                contract_trailing_axis(x[0].close(0)[...], got[0][...])
+                + contract_trailing_axis(x[1].close(0)[...], got[1][...])
+            ).astype(put[0].dtype)
+
+        tiles(count * share, w, *[([f], compute) for f in o])
+
+    outs = [jax.ShapeDtypeStruct((rows, width), t) for t in dtypes]
+    work = count * rows * width * hid
+    estimate = cost(4 * work, 4 * work // rows)
+    far = [*grads, in_hbm(gate), in_hbm(up)]
+    return call(body, "input_parts", mark, [places], far, outs, scratch, 16, estimate)
+
+
+def block_products(left, right):
+    blocks, length, rank = left.shape
+    width = right.shape[1]
+
+    def body(l, r, out):
+        out[0] = lax.dot_general(
+            l[0], r[...], (((0,), (0,)), ((), ())), preferred_element_type=f32
+        ).astype(bf16)
+
+    return pl.pallas_call(
+        body,
+        grid=(blocks,),
+        in_specs=[
+            pl.BlockSpec((1, length, rank), lambda b: (b, 0, 0)),
+            pl.BlockSpec((length, width), lambda b: (b, 0)),
+        ],
+        out_specs=pl.BlockSpec((1, rank, width), lambda b: (b, 0, 0)),
+        out_shape=jax.ShapeDtypeStruct((blocks, rank, width), bf16),
+        compiler_params=pltpu.CompilerParams(vmem_limit_bytes=16 << 20),
+        cost_estimate=cost(2 * blocks * length * rank * width, left.size * 2 + right.size * 2),
+        name="block_products",
+    )(left, right)
+
+
+def by_tenant(labels, scales, parts, tenants, at_once=4):
+    count, rank, width = parts.shape
+
+    def body(labels_ref, scales_ref, parts_ref, out):
+        first = pl.program_id(0) * at_once
+        out[...] = jnp.zeros_like(out)
+        for c in range(count):
+            offset = labels_ref[c] - first
+
+            @pl.when((offset >= 0) & (offset < at_once))
+            def _():
+                out[offset] += scales_ref[c] * parts_ref[c].astype(f32)
+
+    return pl.pallas_call(
+        body,
+        grid=(tenants // at_once,),
+        in_specs=[SCALARS, SCALARS, pl.BlockSpec((count, rank, width), lambda t: (0, 0, 0))],
+        out_specs=pl.BlockSpec((at_once, rank, width), lambda t: (t, 0, 0)),
+        out_shape=jax.ShapeDtypeStruct((tenants, rank, width), f32),
+        compiler_params=pltpu.CompilerParams(vmem_limit_bytes=16 << 20),
+        cost_estimate=cost(0, 4 * tenants * rank * width),
+        name="by_tenant",
+    )(labels, scales, parts)
+
+
+def ringed(
+    tokens,
+    cotangent,
+    gate_weight,
+    up_weight,
+    down_matrix_frozen,
+    adapter_a,
+    adapter_b,
+    tenant,
+    ranks,
+):
+    rows, depth = tokens.shape
+    blocks = tenant.shape[0]
+    length = rows // blocks
+    tenants, _, rank = adapter_a.shape
+    devices = RING * PAIR
+    me = lax.axis_index("tensor")
+    along, across = me // PAIR, me % PAIR
+    first_core = lax.axis_index("dp") == 0
+
+    def place(k, j):
+        return ((along + RING - k) % RING) * PAIR + (across + j) % PAIR
+
+    def places(names):
+        return jnp.stack([place(int(n[1]), int(n[2])) for n in names]).astype(jnp.int32)
+
+    def ring_on(value):
+        return lax.ppermute(value, "tensor", [(i, (i + PAIR) % devices) for i in range(devices)])
+
+    def swap(value, bit=1):
+        return lax.ppermute(value, "tensor", [(i, i ^ bit) for i in range(devices)])
+
+    def other_core(value):
+        return lax.ppermute(value, "dp", [(0, 1), (1, 0)])
+
+    def both_cores(own, other):
+        return jnp.where(
+            first_core, jnp.concatenate([own, other]), jnp.concatenate([other, own])
+        )
+
+    adapter = adapter_a.transpose(0, 2, 1)
+    ranks_of = ranks[tenant]
+    mask = (lax.broadcasted_iota(jnp.int32, (blocks, 1, rank), 2) < ranks_of[:, None, None]).astype(f32)
+    scales = adapter_alpha_factor / ranks.astype(f32)
+    scale_of = scales[tenant]
+
+    cot_blocks = cotangent.reshape(blocks, length, depth)
+    back = jnp.einsum("bnd,brd->bnr", cot_blocks, adapter_b[tenant], preferred_element_type=f32)
+    back = (back * mask).astype(bf16).reshape(rows * rank // depth, depth)
+
+    held = {"T00": tokens, "C00": jnp.concatenate([cotangent, back])}
+    slots = []
+    mark = jnp.zeros(MARK.shape, MARK.dtype)
+
+    def passed(*values):
+        nonlocal mark
+        *values, mark = together((*values, mark))
+        return values
+
+    def start(i):
+        sent = []
+        for plan, send, side in ((RING_PLAN, ring_on, 0), (PAIR_PLAN, swap, 1)):
+            name, source = plan[i]
+            value = held[source]
+            if i >= 2:
+                gate = slots[i - 2][side]
+                if gate == source:
+                    (value,) = passed(value)
+                else:
+                    value, held[gate] = passed(value, held[gate])
+            held[name] = send(value)
+            sent.append(name)
+        slots.append(sent)
+
+    def landed(i):
+        names = slots[i]
+        for n, v in zip(names, passed(*[held[n] for n in names])):
+            held[n] = v
+
+    def add_up(names, sums, low=None):
+        nonlocal mark
+        chunks = [held[n] for n in names]
+        *out, mark = gate_up(mark, chunks, places(names), gate_weight, up_weight, sums, low)
+        return out
+
+    def add_down(names, total, last=None):
+        nonlocal mark
+        chunks = [held[n] for n in names]
+        *out, mark = down_back(mark, chunks, rows, places(names), down_matrix_frozen, total, last)
+        return out
+
+    start(0)
+    start(1)
+    landed(0)
+    labels = both_cores(tenant, other_core(tenant))
+    label_scales = scales[labels]
+    start(2)
+    sums = add_up(["T00", "T10", "T01"], None)
+    landed(1)
+    start(3)
+    (total,) = add_down(["C00", "C10", "C01"], None)
+    landed(2)
+    start(4)
+    sums = add_up(["T20", "T11"], sums)
+    landed(3)
+    start(5)
+    (total,) = add_down(["C20", "C11"], total)
+    landed(4)
+    start(6)
+    sums = add_up(["T30", "T21"], sums)
+    landed(5)
+    act, slope, hidden, low = add_up(["T31"], sums, (tenant, adapter))
+    low = low * mask
+    got_low = swap(low)
+    landed(6)
+    back = sum(held[f"C{k}{j}"][rows:].astype(f32) for k in range(RING) for j in range(PAIR))
+    back = back.reshape(blocks, length, rank)
+    back = (back * scale_of[:, None, None]).astype(bf16)
+    low, got_low = passed(low, got_low)
+    low = low + got_low
+    got_low = swap(low, PAIR)
+    grads = add_down(["C30", "C21", "C31"], total, (tenant, adapter, back, act, slope))
+
+    def parts(blocks_of, dtypes):
+        nonlocal mark
+        where = jnp.stack([place(k, j) for k, j in blocks_of]).astype(jnp.int32)
+        *out, mark = input_parts(mark, where, grads, gate_weight, up_weight, depth, dtypes)
+        return out
+
+    def add(*terms):
+        return sum(t.astype(f32) for t in terms).astype(bf16)
+
+    (out0,) = parts([(1, 1)], [bf16])
+    low, got_low = passed(low, got_low)
+    low = low + got_low
+    got_low = swap(low, 2 * PAIR)
+    got0 = swap(out0)
+    own0, out1 = parts([(1, 0), (2, 1)], [f32, bf16])
+    got1 = swap(out1)
+    got0, got_low = passed(got0, got_low)
+    ring0 = ring_on(add(got0, own0))
+    hidden, back = passed(hidden, back)
+    block_a = block_products(back, hidden)
+    other_a = other_core(block_a)
+    (block_a,) = passed(block_a)
+    own1, out2 = parts([(2, 0), (3, 1)], [f32, bf16])
+    got2 = swap(out2)
+    ring0, got1 = passed(ring0, got1)
+    ring1 = ring_on(add(ring0, got1, own1))
+    own2, out3 = parts([(3, 0), (0, 1)], [f32, bf16])
+    got3 = swap(out3)
+    ring1, got2 = passed(ring1, got2)
+    ring2 = ring_on(add(ring1, got2, own2))
+    (own3,) = parts([(0, 0)], [f32])
+
+    low = (low + got_low).astype(bf16)
+    low, block_a, other_a = passed(low, block_a, other_a)
+    block_b = block_products(low, cotangent)
+    other_b = other_core(block_b)
+    ones = jnp.ones_like(label_scales)
+    grad_a = by_tenant(labels, ones, both_cores(block_a, other_a), tenants)
+    grad_b = by_tenant(labels, label_scales, both_cores(block_b, other_b), tenants)
+    return add(ring2, got3, own3), grad_a.transpose(0, 2, 1), grad_b
+
+
+def gathered(
     tokens,
     cotangent,
     gate_weight,
@@ -92,6 +661,8 @@
 
 
 def solution(mesh):
+    sizes = mesh.shape
+    local = ringed if (sizes["tensor"], sizes["dp"]) == (RING * PAIR, 2) else gathered
     return jax.shard_map(
         local,
         mesh=mesh,

time: 457 us -> 188 us (0.41)
  waiting for transfers between devices: 280 us -> 30.4 us
  Pallas kernels: 0 us -> 108 us
  matrix products: 108 us -> 1.42 us
  blocking collectives: 38.3 us -> 0 us
  starting transfers between devices: 0.2 us -> 28.9 us
  between operations: 13.9 us -> 1.07 us
    reduce_scatter x1 -> x0, waiting for transfers between devices: 137 us -> none  [local(): lax.psum_scatter(input_term, 'tensor', scatter_dimension=1, tiled=True)]
    pallas_call x0 -> x16, Pallas kernels: none -> 108 us  [the longest x12 99.4 us: call(): pl.pallas_call(marked, in_specs=[ANYWHERE] + [SCALARS] * len(scalars) + [...]
    dot_general x14 -> x1, matrix products: 108 us -> 1.42 us  [ringed(): jnp.einsum('bnd,brd->bnr', cot_blocks, adapter_b[tenant], preferred_eleme...]
    all_gather x2 -> x0, waiting for transfers between devices: 74.2 us -> none  [the longest x1 74.2 us: local(): shard_piece = lax.all_gather(tokens, 'tensor', axis=1, tiled=True)]
    psum x2 -> x0, waiting for transfers between devices: 67.3 us -> none  [the longest x1 67.3 us: local(): low_sum, back_sum = lax.psum((low_part, back_part), 'tensor')]
    psum x1 -> x0, blocking collectives: 38.3 us -> none  [local(): low_sum, back_sum = lax.psum((low_part, back_part), 'tensor')]
    ppermute x0 -> x27, waiting for transfers between devices: none -> 30.4 us  [the longest x10 21.2 us: ring_on(): lax.ppermute(value, 'tensor', [(i, (i + PAIR) % devices) for i in range(d...]
    ppermute x0 -> x27, starting transfers between devices: none -> 28.9 us  [the longest x14 15.5 us: swap(): return lax.ppermute(value, 'tensor', [(i, i ^ bit) for i in range(devices)])]
  transfers between devices with their start and end apart: 5 -> 27, of which waited for: 3 -> 9; matrix products, arithmetic and copies ran while one was open for 26% -> 5% of each run, Pallas kernels for 0% -> 58%
where the time goes in v1:
time: 188 us; the launch traced here: 187 us
  Pallas kernels  108 us (57%)
  waiting for transfers between devices  30.4 us (16%)
  starting transfers between devices  28.9 us (15%)
  local copies, waits for them, and re-layouts  12.2 us (6%)
  other arithmetic  5.46 us (3%)
    pallas_call x12, Pallas kernels, call(): pl.pallas_call(marked, in_specs=[ANYWHERE] + [SCALARS] * len(scalars) + [...  99.4 us
    ppermute x10, waiting for transfers between devices, ring_on(): lax.ppermute(value, 'tensor', [(i, (i + PAIR) % devices) for i in range(d...  21.2 us
    ppermute x14, starting transfers between devices, swap(): return lax.ppermute(value, 'tensor', [(i, i ^ bit) for i in range(devices)])  15.5 us
    ppermute x10, starting transfers between devices, ring_on(): lax.ppermute(value, 'tensor', [(i, (i + PAIR) % devices) for i in range(d...  13.1 us
    ppermute x14, waiting for transfers between devices, swap(): return lax.ppermute(value, 'tensor', [(i, i ^ bit) for i in range(devices)])  9.19 us
    unnamed x37, local copies, waits for them, and re-layouts  8.08 us
    pallas_call x2, Pallas kernels, by_tenant(): pl.pallas_call(body, grid=(tenants // at_once,), in_specs=[SCALARS, SCALA...  7.29 us
    convert_element_type x4, other arithmetic, add(): return sum((t.astype(f32) for t in terms)).astype(bf16)  3.76 us
  transfers between devices with their start and end apart: 27, of which 9 were waited for; matrix products, arithmetic and copies ran while one was open for 5% of the time, Pallas kernels for 58%

profile of v1, /device:TPU:0, one launch (start us, length us, event | category | flops | bytes accessed | tf_op | source)
XLA Modules:
  0.0 187.2 jit_solution(9381703316956432166)
XLA Ops:
  0.7 3.1 %collective-permute-start.2 = (bf16[256,1024]{1,0:T(8,128)(2,1)}, bf16[256,1024]{1,0:T(8,128)(2,1)}, u32[]{:S(2)}, u32[]{:S(2)}) collective-permute-start(bf16[256,1024]{1,0:T(8,128)(2,1)} %refs_2_.3), channel_id=1, source_target_pairs={{0,2},{1,3},{2,4},{3,5},{4,6},{5,7},{6,0},{7,1},{8,10},{9,11},{10,... | collective-permute-start | bytes 1572872 | tf_op jit(solution)/shard_map/ppermute | solution.py:446
  10.3 1.6 collective-permute-start
  12.6 6.2 %collective-permute-done.2.refs_3_ = bf16[256,1024]{1,0:T(8,128)(2,1)} collective-permute-done((bf16[256,1024]{1,0:T(8,128)(2,1)}, bf16[256,1024]{1,0:T(8,128)(2,1)}, u32[]{:S(2)}, u32[]{:S(2)}) %collective-permute-start.2) | collective-permute-done | bytes 524320 | tf_op jit(solution)/shard_map/ppermute | solution.py:446
  18.9 1.6 collective-permute-start.6
  22.0 12.4 %gate_up.4 = (f32[256,1792]{1,0:T(8,128)}, f32[256,1792]{1,0:T(8,128)}, f32[8,128]{1,0:T(8,128)S(1)}) custom-call(f32[8,128]{1,0:T(8,128)S(1)} %broadcast_in_dim.5.refs_0_, s32[3]{0:T(128)S(1)} %pad_add_fusion.refs_1_, bf16[256,1024]{1,0:T(8,128)(2,1)S(1)} %copy-done.15, bf16[256,1024]{1,0:T(8,128)(2,1)} %collective-permute-done.2.refs_3_, ...), custom_call_target="tpu_custom_call" | custom-call | flops 5637144576 | bytes 22020096 | tf_op jit(solution)/shard_map/gate_up/pallas_call | solution.py:63
  34.4 1.6 collective-permute-start.4
  36.6 7.5 %down_back.3 = (f32[256,1792]{1,0:T(8,128)}, f32[8,128]{1,0:T(8,128)S(1)}) custom-call(f32[8,128]{1,0:T(8,128)S(1)} %get-tuple-element.121.refs_0_, s32[3]{0:T(128)S(1)} %pad_add_fusion.refs_1_, bf16[272,1024]{1,0:T(8,128)(2,1)S(1)} %constant_dynamic-update-slice_fusion.refs_2_, bf16[272,1024]{1,0:T(8,128)(2,1)S(1)} %collective-permute-done.refs_3_, ...), custom_call_target="tpu_custom_call" | custom-call | flops 2818572288 | bytes 11010048 | tf_op jit(solution)/shard_map/down_back/pallas_call | solution.py:63
  45.9 10.1 %gate_up.5 = (f32[256,1792]{1,0:T(8,128)}, f32[256,1792]{1,0:T(8,128)}, f32[8,128]{1,0:T(8,128)S(1)}) custom-call(f32[8,128]{1,0:T(8,128)S(1)} %get-tuple-element.128.refs_0_, s32[2]{0:T(128)S(1)} %get-tuple-element.209.refs_1_, bf16[256,1024]{1,0:T(8,128)(2,1)} %collective-permute-done.6.refs_2_, bf16[256,1024]{1,0:T(8,128)(2,1)S(1)} %collective-permute-done.7.refs_3_, ...), custom_call_target="tpu_custom_call" | custom-call | flops 3758096384 | bytes 14680064 | tf_op jit(solution)/shard_map/gate_up/pallas_call | solution.py:63
  56.0 1.8 collective-permute-start.8
  58.6 6.5 %collective-permute-done.9.refs_2_ = bf16[256,1024]{1,0:T(8,128)(2,1)S(1)} collective-permute-done((bf16[256,1024]{1,0:T(8,128)(2,1)}, bf16[256,1024]{1,0:T(8,128)(2,1)S(1)}, u32[]{:S(2)}, u32[]{:S(2)}) %collective-permute-start.9) | collective-permute-done | bytes 524320 | tf_op jit(solution)/shard_map/ppermute | solution.py:446
  65.1 1.8 collective-permute-start.10
  66.9 6.7 %down_back.4 = (f32[256,1792]{1,0:T(8,128)}, f32[8,128]{1,0:T(8,128)S(1)}) custom-call(f32[8,128]{1,0:T(8,128)S(1)} %get-tuple-element.141.refs_0_, s32[2]{0:T(128)S(1)} %get-tuple-element.209.refs_1_, bf16[272,1024]{1,0:T(8,128)(2,1)S(1)} %collective-permute-done.4.refs_2_, bf16[272,1024]{1,0:T(8,128)(2,1)S(1)} %collective-permute-done.5.refs_3_, ...), custom_call_target="tpu_custom_call" | custom-call | flops 1879048192 | bytes 7340032 | tf_op jit(solution)/shard_map/down_back/pallas_call | solution.py:63
  73.7 3.0 %collective-permute-done.8.refs_3_ = bf16[272,1024]{1,0:T(8,128)(2,1)S(1)} collective-permute-done((bf16[272,1024]{1,0:T(8,128)(2,1)S(1)}, bf16[272,1024]{1,0:T(8,128)(2,1)S(1)}, u32[]{:S(2)}, u32[]{:S(2)}) %collective-permute-start.8) | collective-permute-done | bytes 557088 | tf_op jit(solution)/shard_map/ppermute | solution.py:446
  76.6 2.2 %collective-permute-start.14 = (bf16[272,1024]{1,0:T(8,128)(2,1)S(1)}, bf16[272,1024]{1,0:T(8,128)(2,1)S(1)}, u32[]{:S(2)}, u32[]{:S(2)}) collective-permute-start(bf16[272,1024]{1,0:T(8,128)(2,1)S(1)} %collective-permute-done.8.refs_3_), channel_id=1, source_target_pairs={{0,1},{1,0},{2,3},{3,2},{4,5},{5,4},{6,7},{7,6},{8,9},{9,8},{10,11... | collective-permute-start | bytes 1671176 | tf_op jit(solution)/shard_map/ppermute | solution.py:449
  78.8 10.9 %gate_up.6 = (f32[256,1792]{1,0:T(8,128)}, f32[256,1792]{1,0:T(8,128)}, f32[8,128]{1,0:T(8,128)S(1)}) custom-call(f32[8,128]{1,0:T(8,128)S(1)} %get-tuple-element.149.refs_0_, s32[2]{0:T(128)S(1)} %get-tuple-element.212.refs_1_, bf16[256,1024]{1,0:T(8,128)(2,1)S(1)} %collective-permute-done.9.refs_2_, bf16[256,1024]{1,0:T(8,128)(2,1)} %collective-permute-done.11.refs_3_, ...), custom_call_target="tpu_custom_call" | custom-call | flops 3758096384 | bytes 14680064 | tf_op jit(solution)/shard_map/gate_up/pallas_call | solution.py:63
  89.7 8.3 %gate_up.7 = (f32[256,1792]{1,0:T(8,128)}, f32[256,1792]{1,0:T(8,128)}, bf16[256,1792]{1,0:T(8,128)(2,1)}, f32[2,128,64]{2,1,0:T(8,128)S(1)}, f32[8,128]{1,0:T(8,128)S(1)}) custom-call(f32[8,128]{1,0:T(8,128)S(1)} %get-tuple-element.155.refs_0_, s32[1]{0:T(128)} %bitcast.9.refs_1_, s32[2]{0:T(128)S(1)} %copy-done.16, ...), custom_call_target="tpu_custom_call" | custom-call | flops 1879048192 | bytes 7340032 | tf_op jit(solution)/shard_map/gate_up/pallas_call | solution.py:63
  100.1 3.0 %collective-permute-done.12 = f32[2,128,64]{2,1,0:T(8,128)S(1)} collective-permute-done((f32[2,128,64]{2,1,0:T(8,128)S(1)}, f32[2,128,64]{2,1,0:T(8,128)S(1)}, u32[]{:S(2)}, u32[]{:S(2)}) %collective-permute-start.12) | collective-permute-done | bytes 65568 | tf_op jit(solution)/shard_map/ppermute | solution.py:449
  103.2 2.0 %copy-done.5 = bf16[16,1792,64]{1,2,0:T(8,128)(2,1)S(1)} copy-done((bf16[16,1792,64]{1,2,0:T(8,128)(2,1)S(1)}, bf16[16,1792,64]{1,2,0:T(8,128)(2,1)}, u32[]{:S(2)}) %copy-start.5) | copy-done | bytes 3670040
  108.4 7.8 %down_back.5 = (bf16[256,1792]{1,0:T(8,128)(2,1)S(1)}, bf16[256,1792]{1,0:T(8,128)(2,1)S(1)}, f32[8,128]{1,0:T(8,128)S(1)}) custom-call(f32[8,128]{1,0:T(8,128)S(1)} %get-tuple-element.164.refs_0_, s32[3]{0:T(128)S(1)} %pad_add_fusion.2.refs_1_, s32[2]{0:T(128)S(1)} %copy-done.16, bf16[272,1024]{1,0:T(8,128)(2,1)S(1)} %copy-done.10, ...), custom_call_target="tpu_custom_call" | custom-call | flops 2818572288 | bytes 11010048 | tf_op jit(solution)/shard_map/down_back/pallas_call | solution.py:63
  116.2 4.8 %input_parts.5 = (bf16[256,1024]{1,0:T(8,128)(2,1)S(1)}, f32[8,128]{1,0:T(8,128)S(1)}) custom-call(f32[8,128]{1,0:T(8,128)S(1)} %get-tuple-element.171.refs_0_, s32[1]{0:T(128)} %bitcast.6.refs_1_, bf16[256,1792]{1,0:T(8,128)(2,1)S(1)} %get-tuple-element.172.refs_2_, bf16[256,1792]{1,0:T(8,128)(2,1)S(1)} %get-tuple-element.173.refs_3_, ...), custom_call_target="tpu_custom_call" | custom-call | flops 1879048192 | bytes 7340032 | tf_op jit(solution)/shard_map/input_parts/pallas_call | solution.py:63
  121.6 5.6 %collective-permute-done.16 = f32[2,128,64]{2,1,0:T(8,128)S(1)} collective-permute-done((f32[2,128,64]{2,1,0:T(8,128)S(1)}, f32[2,128,64]{2,1,0:T(8,128)S(1)}, u32[]{:S(2)}, u32[]{:S(2)}) %collective-permute-start.16) | collective-permute-done | bytes 65568 | tf_op jit(solution)/shard_map/ppermute | solution.py:449
  127.2 1.6 collective-permute-start.17
  128.8 8.8 %input_parts.6 = (f32[256,1024]{1,0:T(8,128)S(1)}, bf16[256,1024]{1,0:T(8,128)(2,1)}, f32[8,128]{1,0:T(8,128)S(1)}) custom-call(f32[8,128]{1,0:T(8,128)S(1)} %get-tuple-element.180.refs_0_, s32[2]{0:T(128)S(1)} %get-tuple-element.211.refs_1_, bf16[256,1792]{1,0:T(8,128)(2,1)S(1)} %get-tuple-element.172.refs_2_, ...), custom_call_target="tpu_custom_call" | custom-call | flops 3758096384 | bytes 14680064 | tf_op jit(solution)/shard_map/input_parts/pallas_call | solution.py:63
  139.9 2.0 %collective-permute-start.18 = (bf16[256,1024]{1,0:T(8,128)(2,1)}, bf16[256,1024]{1,0:T(8,128)(2,1)}, u32[]{:S(2)}, u32[]{:S(2)}) collective-permute-start(bf16[256,1024]{1,0:T(8,128)(2,1)} %add_convert_fusion.3), channel_id=1, source_target_pairs={{0,2},{1,3},{2,4},{3,5},{4,6},{5,7},{6,0},{7,1},{8,10},{9,11},{10,... | collective-permute-start | bytes 1572872 | tf_op jit(solution)/shard_map/ppermute | solution.py:446
  144.4 8.3 %input_parts.7 = (f32[256,1024]{1,0:T(8,128)S(1)}, bf16[256,1024]{1,0:T(8,128)(2,1)S(1)}, f32[8,128]{1,0:T(8,128)S(1)}) custom-call(f32[8,128]{1,0:T(8,128)S(1)} %get-tuple-element.190.refs_0_, s32[2]{0:T(128)S(1)} %get-tuple-element.210.refs_1_, bf16[256,1792]{1,0:T(8,128)(2,1)S(1)} %get-tuple-element.172.refs_2_, ...), custom_call_target="tpu_custom_call" | custom-call | flops 3758096384 | bytes 14680064 | tf_op jit(solution)/shard_map/input_parts/pallas_call | solution.py:63
  156.5 8.3 %input_parts.8 = (f32[256,1024]{1,0:T(8,128)S(1)}, bf16[256,1024]{1,0:T(8,128)(2,1)S(1)}, f32[8,128]{1,0:T(8,128)S(1)}) custom-call(f32[8,128]{1,0:T(8,128)S(1)} %get-tuple-element.196.refs_0_, s32[2]{0:T(128)S(1)} %pad_add_fusion.5.refs_1_, bf16[256,1792]{1,0:T(8,128)(2,1)S(1)} %get-tuple-element.172.refs_2_, ...), custom_call_target="tpu_custom_call" | custom-call | flops 3758096384 | bytes 14680064 | tf_op jit(solution)/shard_map/input_parts/pallas_call | solution.py:63
  164.7 1.8 collective-permute-start.23
  167.1 3.7 %collective-permute-done.20 = bf16[256,1024]{1,0:T(8,128)(2,1)S(1)} collective-permute-done((bf16[256,1024]{1,0:T(8,128)(2,1)S(1)}, bf16[256,1024]{1,0:T(8,128)(2,1)S(1)}, u32[]{:S(2)}, u32[]{:S(2)}) %collective-permute-start.20) | collective-permute-done | bytes 524320 | tf_op jit(solution)/shard_map/ppermute | solution.py:446
  171.3 4.1 %by_tenant.2 = f32[16,64,1792]{2,1,0:T(8,128)} custom-call(s32[4]{0:T(128)S(1)} %broadcast_select_fusion.1.labels_ref, f32[4]{0:T(128)S(1)} %broadcast_6_scales_ref.2.scales_ref, bf16[4,64,1792]{2,1,0:T(8,128)(2,1)S(1)} %maximum_select_fusion.parts_ref), custom_call_target="tpu_custom_call" | custom-call | bytes 7340032 | tf_op jit(solution)/shard_map/by_tenant/pallas_call | solution.py:407
  175.5 3.2 %by_tenant.3 = f32[16,64,1024]{2,1,0:T(8,128)} custom-call(s32[4]{0:T(128)S(1)} %broadcast_select_fusion.1.labels_ref, f32[4]{0:T(128)S(1)} %gather_fusion.3, bf16[4,64,1024]{2,1,0:T(8,128)(2,1)S(1)} %maximum_select_fusion.1.parts_ref), custom_call_target="tpu_custom_call" | custom-call | bytes 4194304 | tf_op jit(solution)/shard_map/by_tenant/pallas_call | solution.py:407
  178.7 5.6 %input_parts.9 = (f32[256,1024]{1,0:T(8,128)S(1)}, f32[8,128]{1,0:T(8,128)}) custom-call(f32[8,128]{1,0:T(8,128)S(1)} %get-tuple-element.202.refs_0_, s32[1]{0:T(128)} %bitcast.2.refs_1_, bf16[256,1792]{1,0:T(8,128)(2,1)S(1)} %get-tuple-element.172.refs_2_, bf16[256,1792]{1,0:T(8,128)(2,1)S(1)} %copy-done.3, bf16[8192,1792]{1,0:T(8,128)(2,1)} %refs_4_.17, ...), custom_call_target="tpu_custom_call" | custom-call | flops 1879048192 | bytes 7340032 | tf_op jit(solution)/shard_map/input_parts/pallas_call | solution.py:63
  184.4 1.8 collective-permute-done.22
  (110 shorter events, 28.5 us)
Async XLA Ops:
  0.6 21.4 %copy-start.15 = (bf16[256,1024]{1,0:T(8,128)(2,1)S(1)}, bf16[256,1024]{1,0:T(8,128)(2,1)}, u32[]{:S(2)}) copy-start(bf16[256,1024]{1,0:T(8,128)(2,1)} %refs_2_.3) | copy-start | bytes 1572868
  0.7 11.8 %copy-start.16 = (s32[2]{0:T(128)S(1)}, s32[2]{0:T(128)}, u32[]{:S(2)}) copy-start(s32[2]{0:T(128)} %refs_2_.5) | copy-start | bytes 28
  0.7 18.2 %collective-permute-start.2 = (bf16[256,1024]{1,0:T(8,128)(2,1)}, bf16[256,1024]{1,0:T(8,128)(2,1)}, u32[]{:S(2)}, u32[]{:S(2)}) collective-permute-start(bf16[256,1024]{1,0:T(8,128)(2,1)} %refs_2_.3), channel_id=1, source_target_pairs={{0,2},{1,3},{2,4},{3,5},{4,6},{5,7},{6,0},{7,1},{8,10},{9,11},{10,... | collective-permute-start | bytes 1572872 | tf_op jit(solution)/shard_map/ppermute | solution.py:446
  3.8 15.2 %collective-permute-start.3 = (bf16[256,1024]{1,0:T(8,128)(2,1)}, bf16[256,1024]{1,0:T(8,128)(2,1)}, u32[]{:S(2)}, u32[]{:S(2)}) collective-permute-start(bf16[256,1024]{1,0:T(8,128)(2,1)} %refs_2_.3), channel_id=1, source_target_pairs={{0,1},{1,0},{2,3},{3,2},{4,5},{5,4},{6,7},{7,6},{8,9},{9,8},{10,11... | collective-permute-start | bytes 1572872 | tf_op jit(solution)/shard_map/ppermute | solution.py:449
  10.3 24.1 %collective-permute-start = (bf16[272,1024]{1,0:T(8,128)(2,1)S(1)}, bf16[272,1024]{1,0:T(8,128)(2,1)S(1)}, u32[]{:S(2)}, u32[]{:S(2)}) collective-permute-start(bf16[272,1024]{1,0:T(8,128)(2,1)S(1)} %constant_dynamic-update-slice_fusion.refs_2_), channel_id=1, source_target_pairs={{0,2},{1,3},{2,4},{3,5},{4,6},{5,7},{6,0},{7,1},{8,10},{9,11},{10,... | collective-permute-start | bytes 1671176 | tf_op jit(solution)/shard_map/ppermute | solution.py:446
  11.9 22.5 %collective-permute-start.1 = (bf16[272,1024]{1,0:T(8,128)(2,1)S(1)}, bf16[272,1024]{1,0:T(8,128)(2,1)S(1)}, u32[]{:S(2)}, u32[]{:S(2)}) collective-permute-start(bf16[272,1024]{1,0:T(8,128)(2,1)S(1)} %constant_dynamic-update-slice_fusion.refs_2_), channel_id=1, source_target_pairs={{0,1},{1,0},{2,3},{3,2},{4,5},{5,4},{6,7},{7,6},{8,9},{9,8},{10,11... | collective-permute-start | bytes 1671176 | tf_op jit(solution)/shard_map/ppermute | solution.py:449
  12.5 109.1 %collective-permute-start.24 = (s32[2]{0:T(128)S(1)}, s32[2]{0:T(128)S(1)}, u32[]{:S(2)}, u32[]{:S(2)}) collective-permute-start(s32[2]{0:T(128)S(1)} %copy-done.16), channel_id=1, source_target_pairs={{0,8},{8,0},{1,9},{9,1},{2,10},{10,2},{3,11},{11,3},{4,12},{12,4},... | collective-permute-start | bytes 32 | tf_op jit(solution)/shard_map/ppermute | solution.py:452
  18.9 25.2 %collective-permute-start.6 = (bf16[256,1024]{1,0:T(8,128)(2,1)}, bf16[256,1024]{1,0:T(8,128)(2,1)}, u32[]{:S(2)}, u32[]{:S(2)}) collective-permute-start(bf16[256,1024]{1,0:T(8,128)(2,1)} %collective-permute-done.2.refs_3_), channel_id=1, source_target_pairs={{0,2},{1,3},{2,4},{3,5},{4,6},{5,7},{6,0},{7,1},{8,10},{9,11},{10,... | collective-permute-start | bytes 1572872 | tf_op jit(solution)/shard_map/ppermute | solution.py:446
  20.5 23.6 %collective-permute-start.7 = (bf16[256,1024]{1,0:T(8,128)(2,1)}, bf16[256,1024]{1,0:T(8,128)(2,1)S(1)}, u32[]{:S(2)}, u32[]{:S(2)}) collective-permute-start(bf16[256,1024]{1,0:T(8,128)(2,1)} %collective-permute-done.2.refs_3_), channel_id=1, source_target_pairs={{0,1},{1,0},{2,3},{3,2},{4,5},{5,4},{6,7},{7,6},{8,9},{9,8},{10,11... | collective-permute-start | bytes 1572872 | tf_op jit(solution)/shard_map/ppermute | solution.py:449
  34.4 21.5 %collective-permute-start.4 = (bf16[272,1024]{1,0:T(8,128)(2,1)S(1)}, bf16[272,1024]{1,0:T(8,128)(2,1)S(1)}, u32[]{:S(2)}, u32[]{:S(2)}) collective-permute-start(bf16[272,1024]{1,0:T(8,128)(2,1)S(1)} %collective-permute-done.refs_3_), channel_id=1, source_target_pairs={{0,2},{1,3},{2,4},{3,5},{4,6},{5,7},{6,0},{7,1},{8,10},{9,11},{10,... | collective-permute-start | bytes 1671176 | tf_op jit(solution)/shard_map/ppermute | solution.py:446
  36.1 19.9 %collective-permute-start.5 = (bf16[272,1024]{1,0:T(8,128)(2,1)S(1)}, bf16[272,1024]{1,0:T(8,128)(2,1)S(1)}, u32[]{:S(2)}, u32[]{:S(2)}) collective-permute-start(bf16[272,1024]{1,0:T(8,128)(2,1)S(1)} %collective-permute-done.refs_3_), channel_id=1, source_target_pairs={{0,1},{1,0},{2,3},{3,2},{4,5},{5,4},{6,7},{7,6},{8,9},{9,8},{10,11... | collective-permute-start | bytes 1671176 | tf_op jit(solution)/shard_map/ppermute | solution.py:449
  44.1 21.0 %collective-permute-start.9 = (bf16[256,1024]{1,0:T(8,128)(2,1)}, bf16[256,1024]{1,0:T(8,128)(2,1)S(1)}, u32[]{:S(2)}, u32[]{:S(2)}) collective-permute-start(bf16[256,1024]{1,0:T(8,128)(2,1)} %collective-permute-done.6.refs_2_), channel_id=1, source_target_pairs={{0,2},{1,3},{2,4},{3,5},{4,6},{5,7},{6,0},{7,1},{8,10},{9,11},{10,... | collective-permute-start | bytes 1572872 | tf_op jit(solution)/shard_map/ppermute | solution.py:446
  44.4 29.2 %collective-permute-start.11 = (bf16[256,1024]{1,0:T(8,128)(2,1)}, bf16[256,1024]{1,0:T(8,128)(2,1)}, u32[]{:S(2)}, u32[]{:S(2)}) collective-permute-start(bf16[256,1024]{1,0:T(8,128)(2,1)} %collective-permute-done.6.refs_2_), channel_id=1, source_target_pairs={{0,1},{1,0},{2,3},{3,2},{4,5},{5,4},{6,7},{7,6},{8,9},{9,8},{10,11... | collective-permute-start | bytes 1572872 | tf_op jit(solution)/shard_map/ppermute | solution.py:449
  45.9 11.9 %copy-start.17 = (s32[16]{0:T(128)S(1)}, s32[16]{0:T(128)}, u32[]{:S(2)}) copy-start(s32[16]{0:T(128)} %param.17) | copy-start | bytes 196
  56.0 20.6 %collective-permute-start.8 = (bf16[272,1024]{1,0:T(8,128)(2,1)S(1)}, bf16[272,1024]{1,0:T(8,128)(2,1)S(1)}, u32[]{:S(2)}, u32[]{:S(2)}) collective-permute-start(bf16[272,1024]{1,0:T(8,128)(2,1)S(1)} %collective-permute-done.4.refs_2_), channel_id=1, source_target_pairs={{0,2},{1,3},{2,4},{3,5},{4,6},{5,7},{6,0},{7,1},{8,10},{9,11},{10,... | collective-permute-start | bytes 1671176 | tf_op jit(solution)/shard_map/ppermute | solution.py:446
  65.1 24.6 %collective-permute-start.10 = (bf16[256,1024]{1,0:T(8,128)(2,1)S(1)}, bf16[256,1024]{1,0:T(8,128)(2,1)S(1)}, u32[]{:S(2)}, u32[]{:S(2)}) collective-permute-start(bf16[256,1024]{1,0:T(8,128)(2,1)S(1)} %collective-permute-done.9.refs_2_), channel_id=1, source_target_pairs={{0,1},{1,0},{2,3},{3,2},{4,5},{5,4},{6,7},{7,6},{8,9},{9,8},{10,11... | collective-permute-start | bytes 1572872 | tf_op jit(solution)/shard_map/ppermute | solution.py:449
  73.6 24.7 %collective-permute-start.13 = (bf16[272,1024]{1,0:T(8,128)(2,1)S(1)}, bf16[272,1024]{1,0:T(8,128)(2,1)S(1)}, u32[]{:S(2)}, u32[]{:S(2)}) collective-permute-start(bf16[272,1024]{1,0:T(8,128)(2,1)S(1)} %collective-permute-done.5.refs_3_), channel_id=1, source_target_pairs={{0,2},{1,3},{2,4},{3,5},{4,6},{5,7},{6,0},{7,1},{8,10},{9,11},{10,... | collective-permute-start | bytes 1671176 | tf_op jit(solution)/shard_map/ppermute | solution.py:446
  76.6 21.7 %copy-start.9 = (bf16[272,1024]{1,0:T(8,128)(2,1)}, bf16[272,1024]{1,0:T(8,128)(2,1)S(1)}, u32[]{:S(2)}) copy-start(bf16[272,1024]{1,0:T(8,128)(2,1)S(1)} %collective-permute-done.8.refs_3_) | copy-start | bytes 1671172
  76.6 21.7 %collective-permute-start.14 = (bf16[272,1024]{1,0:T(8,128)(2,1)S(1)}, bf16[272,1024]{1,0:T(8,128)(2,1)S(1)}, u32[]{:S(2)}, u32[]{:S(2)}) collective-permute-start(bf16[272,1024]{1,0:T(8,128)(2,1)S(1)} %collective-permute-done.8.refs_3_), channel_id=1, source_target_pairs={{0,1},{1,0},{2,3},{3,2},{4,5},{5,4},{6,7},{7,6},{8,9},{9,8},{10,11... | collective-permute-start | bytes 1671176 | tf_op jit(solution)/shard_map/ppermute | solution.py:449
  98.1 5.0 %collective-permute-start.12 = (f32[2,128,64]{2,1,0:T(8,128)S(1)}, f32[2,128,64]{2,1,0:T(8,128)S(1)}, u32[]{:S(2)}, u32[]{:S(2)}) collective-permute-start(f32[2,128,64]{2,1,0:T(8,128)S(1)} %broadcast_multiply_fusion), channel_id=1, source_target_pairs={{0,1},{1,0},{2,3},{3,2},{4,5},{5,4},{6,7},{7,6},{8,9},{9,8},{10,11... | collective-permute-start | bytes 196616 | tf_op jit(solution)/shard_map/ppermute | solution.py:449
  116.1 40.3 %copy-start.2 = (bf16[256,1792]{1,0:T(8,128)(2,1)}, bf16[256,1792]{1,0:T(8,128)(2,1)S(1)}, u32[]{:S(2)}) copy-start(bf16[256,1792]{1,0:T(8,128)(2,1)S(1)} %get-tuple-element.173.refs_3_) | copy-start | bytes 2752516
  121.0 18.0 %collective-permute-start.15 = (bf16[256,1024]{1,0:T(8,128)(2,1)S(1)}, bf16[256,1024]{1,0:T(8,128)(2,1)S(1)}, u32[]{:S(2)}, u32[]{:S(2)}) collective-permute-start(bf16[256,1024]{1,0:T(8,128)(2,1)S(1)} %get-tuple-element.174), channel_id=1, source_target_pairs={{0,1},{1,0},{2,3},{3,2},{4,5},{5,4},{6,7},{7,6},{8,9},{9,8},{10,11... | collective-permute-start | bytes 1572872 | tf_op jit(solution)/shard_map/ppermute | solution.py:449
  121.4 5.8 %collective-permute-start.16 = (f32[2,128,64]{2,1,0:T(8,128)S(1)}, f32[2,128,64]{2,1,0:T(8,128)S(1)}, u32[]{:S(2)}, u32[]{:S(2)}) collective-permute-start(f32[2,128,64]{2,1,0:T(8,128)S(1)} %add.245), channel_id=1, source_target_pairs={{0,2},{1,3},{2,0},{3,1},{4,6},{5,7},{6,4},{7,5},{8,10},{9,11},{10,... | collective-permute-start | bytes 196616 | tf_op jit(solution)/shard_map/ppermute | solution.py:449
  127.2 11.8 %collective-permute-start.17 = (f32[2,128,64]{2,1,0:T(8,128)S(1)}, f32[2,128,64]{2,1,0:T(8,128)S(1)}, u32[]{:S(2)}, u32[]{:S(2)}) collective-permute-start(f32[2,128,64]{2,1,0:T(8,128)S(1)} %add.246), channel_id=1, source_target_pairs={{0,4},{1,5},{2,6},{3,7},{4,0},{5,1},{6,2},{7,3},{8,12},{9,13},{10,... | collective-permute-start | bytes 196616 | tf_op jit(solution)/shard_map/ppermute | solution.py:449
  137.6 15.6 %collective-permute-start.19 = (bf16[256,1024]{1,0:T(8,128)(2,1)}, bf16[256,1024]{1,0:T(8,128)(2,1)}, u32[]{:S(2)}, u32[]{:S(2)}) collective-permute-start(bf16[256,1024]{1,0:T(8,128)(2,1)} %get-tuple-element.184), channel_id=1, source_target_pairs={{0,1},{1,0},{2,3},{3,2},{4,5},{5,4},{6,7},{7,6},{8,9},{9,8},{10,11... | collective-permute-start | bytes 1572872 | tf_op jit(solution)/shard_map/ppermute | solution.py:449
  139.9 13.3 %collective-permute-start.18 = (bf16[256,1024]{1,0:T(8,128)(2,1)}, bf16[256,1024]{1,0:T(8,128)(2,1)}, u32[]{:S(2)}, u32[]{:S(2)}) collective-permute-start(bf16[256,1024]{1,0:T(8,128)(2,1)} %add_convert_fusion.3), channel_id=1, source_target_pairs={{0,2},{1,3},{2,4},{3,5},{4,6},{5,7},{6,0},{7,1},{8,10},{9,11},{10,... | collective-permute-start | bytes 1572872 | tf_op jit(solution)/shard_map/ppermute | solution.py:446
  144.3 11.4 %collective-permute-start.25 = (bf16[2,64,1792]{2,1,0:T(8,128)(2,1)S(1)}, bf16[2,64,1792]{2,1,0:T(8,128)(2,1)S(1)}, u32[]{:S(2)}, u32[]{:S(2)}) collective-permute-start(bf16[2,64,1792]{2,1,0:T(8,128)(2,1)S(1)} %block_products.2), channel_id=1, source_target_pairs={{0,8},{8,0},{1,9},{9,1},{2,10},{10,2},{3,11},{11,3},{4,12},{12,4},... | collective-permute-start | bytes 1376264 | tf_op jit(solution)/shard_map/ppermute | solution.py:452
  152.7 14.4 %collective-permute-start.21 = (bf16[256,1024]{1,0:T(8,128)(2,1)S(1)}, bf16[256,1024]{1,0:T(8,128)(2,1)S(1)}, u32[]{:S(2)}, u32[]{:S(2)}) collective-permute-start(bf16[256,1024]{1,0:T(8,128)(2,1)S(1)} %get-tuple-element.195), channel_id=1, source_target_pairs={{0,1},{1,0},{2,3},{3,2},{4,5},{5,4},{6,7},{7,6},{8,9},{9,8},{10,11... | collective-permute-start | bytes 1572872 | tf_op jit(solution)/shard_map/ppermute | solution.py:449
  154.7 16.1 %collective-permute-start.20 = (bf16[256,1024]{1,0:T(8,128)(2,1)S(1)}, bf16[256,1024]{1,0:T(8,128)(2,1)S(1)}, u32[]{:S(2)}, u32[]{:S(2)}) collective-permute-start(bf16[256,1024]{1,0:T(8,128)(2,1)S(1)} %add_convert_fusion.2), channel_id=1, source_target_pairs={{0,2},{1,3},{2,4},{3,5},{4,6},{5,7},{6,0},{7,1},{8,10},{9,11},{10,... | collective-permute-start | bytes 1572872 | tf_op jit(solution)/shard_map/ppermute | solution.py:446
  156.2 19.3 %collective-permute-start.26 = (bf16[2,64,1024]{2,1,0:T(8,128)(2,1)S(1)}, bf16[2,64,1024]{2,1,0:T(8,128)(2,1)S(1)}, u32[]{:S(2)}, u32[]{:S(2)}) collective-permute-start(bf16[2,64,1024]{2,1,0:T(8,128)(2,1)S(1)} %block_products.3), channel_id=1, source_target_pairs={{0,8},{8,0},{1,9},{9,1},{2,10},{10,2},{3,11},{11,3},{4,12},{12,4},... | collective-permute-start | bytes 786440 | tf_op jit(solution)/shard_map/ppermute | solution.py:452
  164.7 19.6 %collective-permute-start.23 = (bf16[256,1024]{1,0:T(8,128)(2,1)S(1)}, bf16[256,1024]{1,0:T(8,128)(2,1)S(1)}, u32[]{:S(2)}, u32[]{:S(2)}) collective-permute-start(bf16[256,1024]{1,0:T(8,128)(2,1)S(1)} %get-tuple-element.201), channel_id=1, source_target_pairs={{0,1},{1,0},{2,3},{3,2},{4,5},{5,4},{6,7},{7,6},{8,9},{9,8},{10,11... | collective-permute-start | bytes 1572872 | tf_op jit(solution)/shard_map/ppermute | solution.py:449
  171.1 15.1 %collective-permute-start.22 = (bf16[256,1024]{1,0:T(8,128)(2,1)S(1)}, bf16[256,1024]{1,0:T(8,128)(2,1)S(1)}, u32[]{:S(2)}, u32[]{:S(2)}) collective-permute-start(bf16[256,1024]{1,0:T(8,128)(2,1)S(1)} %add_convert_fusion.1), channel_id=1, source_target_pairs={{0,2},{1,3},{2,4},{3,5},{4,6},{5,7},{6,0},{7,1},{8,10},{9,11},{10,... | collective-permute-start | bytes 1572872 | tf_op jit(solution)/shard_map/ppermute | solution.py:446
  (13 other events, 48.5 us)

commit v2 on v1

--- a/solution.py
+++ b/solution.py
@@ -92,17 +92,26 @@
         self.copy(n).wait()
 
 
-def tiles(steps, inward, *phases):
-    most = max([f.slots for f in inward])
-    for n in range(most):
+def tiles(steps, whole, inward, *phases):
+    for i in range(max(len(whole), len(inward))):
+        for f in whole[i : i + 1] + inward[i : i + 1]:
+            f.start(0)
+    for n in range(1, steps):
         for f in inward:
-            if n < min(f.slots, steps):
+            if n < f.slots:
                 f.start(n)
     share = steps // len(phases)
+
     for p, (outward, compute) in enumerate(phases):
 
         def step(k, carry, base=p * share, outward=outward, compute=compute):
             n = base + k
+
+            @pl.when(n == 0)
+            def _():
+                for f in whole:
+                    f.wait(0)
+
             for f in inward:
                 f.wait(n)
             for f in outward:
@@ -111,7 +120,11 @@
                 def _():
                     f.wait(k - f.slots)
 
-            compute(n, [f.close(n) for f in inward], [f.close(k) for f in outward])
+            compute(
+                [f.close(0) for f in whole],
+                [f.close(n) for f in inward],
+                [f.close(k) for f in outward],
+            )
             for f in outward:
                 f.start(k)
             for f in inward:
@@ -161,8 +174,9 @@
     length = 0 if low is None else rows // blocks
     rank = 0 if low is None else low[1].shape[1]
     scalars = [places] + ([] if low is None else [low[0]])
-    far = [*chunks, in_hbm(gate), in_hbm(up)] + ([] if sums is None else [in_hbm(t) for t in sums])
+    far = [*chunks, gate, up] + ([] if sums is None else list(sums))
     far += [] if low is None else [low[1]]
+    far = [in_hbm(f) for f in far]
     types = [f32, f32] if low is None else [f32, f32, bf16]
     outs = [pltpu.HBM((rows, hid), t) for t in types]
     if low is not None:
@@ -200,25 +214,20 @@
         )
         o = flows([lambda n, r=r: r.at[:, at(n, tile)] for r in out_far], take(2 * len(out_far)), True)
         l = flows([lambda n, r=r: r for r in low_far], take(2 * len(low_far)), True)
-        for f in x:
-            f.start(0)
         for f in l:
             f.close(0)[...] = jnp.zeros((blocks, length, rank), f32)
 
-        def compute(n, got, put):
-            @pl.when(n == 0)
-            def _():
-                for f in x:
-                    f.wait(0)
-
+        def compute(x, got, put):
             found = []
             for which in range(2):
-                total = None if sums is None else got[2 * count + which][...]
+                total = None
                 for c in range(count):
                     term = jnp.dot(
-                        x[c].close(0)[...], got[which * count + c][...], preferred_element_type=f32
+                        x[c][...], got[which * count + c][...], preferred_element_type=f32
                     )
                     total = term if total is None else total + term
+                if sums is not None:
+                    total = total + got[2 * count + which][...]
                 found.append(total)
             if low is None:
                 put[0][...], put[1][...] = found
@@ -235,7 +244,7 @@
                     hidden[b * length : (b + 1) * length], got[len(got) - blocks + b][...]
                 )
 
-        tiles(hid // tile, w, (o, compute))
+        tiles(hid // tile, x, w, (o, compute))
         for f in l:
             f.start(0)
             f.wait(0)
@@ -253,8 +262,9 @@
     length = 0 if last is None else rows // blocks
     rank = 0 if last is None else last[1].shape[1]
     scalars = [places] + ([] if last is None else [last[0]])
-    far = [*chunks, in_hbm(down)] + ([] if total is None else [in_hbm(total)])
-    far += [] if last is None else [*last[1:3], in_hbm(last[3]), in_hbm(last[4])]
+    far = [*chunks, down] + ([] if total is None else [total])
+    far += [] if last is None else list(last[1:])
+    far = [in_hbm(f) for f in far]
     types = [f32] if last is None else [bf16, bf16]
     scratch = buffers(1, *[((rows, depth), bf16)] * count)
     scratch += buffers(slots, *[((tile, depth), bf16)] * count)
@@ -289,32 +299,27 @@
         )
         w += flows([lambda n, r=r: r.at[:, at(n, tile)] for r in factors], take(2 * len(factors)))
         o = flows([lambda n, r=r: r.at[:, at(n, tile)] for r in out_far], take(2 * len(out_far)), True)
-        for f in x:
-            f.start(0)
-
-        def compute(n, got, put):
-            @pl.when(n == 0)
-            def _():
-                for f in x:
-                    f.wait(0)
-
-            value = None if total is None else got[count][...]
+        def compute(x, got, put):
+            value = None
             for c in range(count):
-                term = contract_trailing_axis(x[c].close(0)[...], got[c][...])
+                term = contract_trailing_axis(x[c][...], got[c][...])
                 value = term if value is None else value + term
+            if total is not None:
+                value = value + got[count][...]
             if last is None:
                 put[0][...] = value
                 return
             *adapters, act, slope = got[len(got) - blocks - 2 :]
+            back = x[count]
             for b in range(blocks):
                 span = slice(b * length, (b + 1) * length)
                 grad = value[span] + jnp.dot(
-                    x[count].close(0)[b], adapters[b][...], preferred_element_type=f32
+                    back[b], adapters[b][...], preferred_element_type=f32
                 )
                 put[0][span] = (grad * slope[span]).astype(bf16)
                 put[1][span] = (grad * act[span]).astype(bf16)
 
-        tiles(hid // tile, w, (o, compute))
+        tiles(hid // tile, x, w, (o, compute))
 
     if last is None:
         outs = [pltpu.HBM((rows, hid), f32)]
@@ -325,13 +330,12 @@
     return call(body, "down_back", mark, scalars, far, outs, scratch, 24, estimate)
 
 
-def input_parts(mark, places, grads, gate, up, width, dtypes, tile=256, slots=4):
+def input_parts(mark, places, grads, gate, up, width, count, tile=256, slots=4):
     rows, hid = grads[0].shape
-    count = len(dtypes)
     share = width // tile
     scratch = buffers(1, *[((rows, hid), bf16)] * 2)
     scratch += buffers(slots, *[((tile, hid), bf16)] * 2)
-    scratch += buffers(2, *[((rows, tile), t) for t in dtypes])
+    scratch += buffers(2, *[((rows, tile), bf16)] * count)
 
     def body(*refs):
         take = Refs(refs)
@@ -344,23 +348,15 @@
         x = flows([lambda n, r=r: r for r in x_far], take(4))
         w = flows([lambda n, r=r: r.at[tile_at(n), :] for r in weights], take(4))
         o = flows([lambda n, r=r: r.at[:, at(n, tile)] for r in out_far], take(2 * count), True)
-        for f in x:
-            f.start(0)
-
-        def compute(n, got, put):
-            @pl.when(n == 0)
-            def _():
-                for f in x:
-                    f.wait(0)
-
+        def compute(x, got, put):
             put[0][...] = (
-                contract_trailing_axis(x[0].close(0)[...], got[0][...])
-                + contract_trailing_axis(x[1].close(0)[...], got[1][...])
-            ).astype(put[0].dtype)
-
-        tiles(count * share, w, *[([f], compute) for f in o])
-
-    outs = [jax.ShapeDtypeStruct((rows, width), t) for t in dtypes]
+                contract_trailing_axis(x[0][...], got[0][...])
+                + contract_trailing_axis(x[1][...], got[1][...])
+            ).astype(bf16)
+
+        tiles(count * share, x, w, *[([f], compute) for f in o])
+
+    outs = [jax.ShapeDtypeStruct((rows, width), bf16)] * count
     work = count * rows * width * hid
     estimate = cost(4 * work, 4 * work // rows)
     far = [*grads, in_hbm(gate), in_hbm(up)]
@@ -458,16 +454,15 @@
 
     adapter = adapter_a.transpose(0, 2, 1)
     ranks_of = ranks[tenant]
-    mask = (lax.broadcasted_iota(jnp.int32, (blocks, 1, rank), 2) < ranks_of[:, None, None]).astype(f32)
+    mask_of = (lax.broadcasted_iota(jnp.int32, (blocks, 1, rank), 2) < ranks_of[:, None, None]).astype(f32)
     scales = adapter_alpha_factor / ranks.astype(f32)
     scale_of = scales[tenant]
 
     cot_blocks = cotangent.reshape(blocks, length, depth)
     back = jnp.einsum("bnd,brd->bnr", cot_blocks, adapter_b[tenant], preferred_element_type=f32)
-    back = (back * mask).astype(bf16).reshape(rows * rank // depth, depth)
+    back = (back * mask_of).astype(bf16).reshape(rows * rank // depth, depth)
 
     held = {"T00": tokens, "C00": jnp.concatenate([cotangent, back])}
-    slots = []
     mark = jnp.zeros(MARK.shape, MARK.dtype)
 
     def passed(*values):
@@ -475,23 +470,20 @@
         *values, mark = together((*values, mark))
         return values
 
-    def start(i):
-        sent = []
-        for plan, send, side in ((RING_PLAN, ring_on, 0), (PAIR_PLAN, swap, 1)):
-            name, source = plan[i]
+    def start(i, *sides):
+        for side in sides or (0, 1):
+            name, source = (RING_PLAN, PAIR_PLAN)[side][i]
             value = held[source]
             if i >= 2:
-                gate = slots[i - 2][side]
+                gate = (RING_PLAN, PAIR_PLAN)[side][i - 2][0]
                 if gate == source:
                     (value,) = passed(value)
                 else:
                     value, held[gate] = passed(value, held[gate])
-            held[name] = send(value)
-            sent.append(name)
-        slots.append(sent)
+            held[name] = (ring_on, swap)[side](value)
 
     def landed(i):
-        names = slots[i]
+        names = (RING_PLAN[i][0], PAIR_PLAN[i][0])
         for n, v in zip(names, passed(*[held[n] for n in names])):
             held[n] = v
 
@@ -521,55 +513,59 @@
     start(4)
     sums = add_up(["T20", "T11"], sums)
     landed(3)
-    start(5)
+    start(5, 0)
     (total,) = add_down(["C20", "C11"], total)
     landed(4)
-    start(6)
+    start(5, 1)
+    start(6, 0)
     sums = add_up(["T30", "T21"], sums)
     landed(5)
+    start(6, 1)
     act, slope, hidden, low = add_up(["T31"], sums, (tenant, adapter))
-    low = low * mask
-    got_low = swap(low)
+    low = low * mask_of
+    got_low = swap(low, PAIR)
     landed(6)
     back = sum(held[f"C{k}{j}"][rows:].astype(f32) for k in range(RING) for j in range(PAIR))
-    back = back.reshape(blocks, length, rank)
-    back = (back * scale_of[:, None, None]).astype(bf16)
+    back = back * jnp.repeat(scale_of, length * rank // depth)[:, None]
+    back = back.astype(bf16).reshape(blocks, length, rank)
+    grads = add_down(["C30", "C21", "C31"], total, (tenant, adapter, back, act, slope))
+
+    def parts(*blocks_of):
+        nonlocal mark
+        where = jnp.stack([place(k, j) for k, j in blocks_of]).astype(jnp.int32)
+        count = len(blocks_of)
+        *out, mark = input_parts(mark, where, grads, gate_weight, up_weight, depth, count)
+        return out
+
+    def add(*terms):
+        return sum(t.astype(f32) for t in terms).astype(bf16)
+
     low, got_low = passed(low, got_low)
     low = low + got_low
-    got_low = swap(low, PAIR)
-    grads = add_down(["C30", "C21", "C31"], total, (tenant, adapter, back, act, slope))
-
-    def parts(blocks_of, dtypes):
-        nonlocal mark
-        where = jnp.stack([place(k, j) for k, j in blocks_of]).astype(jnp.int32)
-        *out, mark = input_parts(mark, where, grads, gate_weight, up_weight, depth, dtypes)
-        return out
-
-    def add(*terms):
-        return sum(t.astype(f32) for t in terms).astype(bf16)
-
-    (out0,) = parts([(1, 1)], [bf16])
+    (out0,) = parts((1, 1))
+    got0 = swap(out0)
+    (low,) = passed(low)
+    got_low = swap(low, 2 * PAIR)
+    own0, out1 = parts((1, 0), (2, 1))
     low, got_low = passed(low, got_low)
     low = low + got_low
-    got_low = swap(low, 2 * PAIR)
-    got0 = swap(out0)
-    own0, out1 = parts([(1, 0), (2, 1)], [f32, bf16])
+    got_low = swap(low)
     got1 = swap(out1)
-    got0, got_low = passed(got0, got_low)
+    (got0,) = passed(got0)
     ring0 = ring_on(add(got0, own0))
+    own1, out2 = parts((2, 0), (3, 1))
+    got2 = swap(out2)
+    ring0, got1 = passed(ring0, got1)
+    ring1 = ring_on(add(ring0, got1, own1))
     hidden, back = passed(hidden, back)
     block_a = block_products(back, hidden)
     other_a = other_core(block_a)
     (block_a,) = passed(block_a)
-    own1, out2 = parts([(2, 0), (3, 1)], [f32, bf16])
-    got2 = swap(out2)
-    ring0, got1 = passed(ring0, got1)
-    ring1 = ring_on(add(ring0, got1, own1))
-    own2, out3 = parts([(3, 0), (0, 1)], [f32, bf16])
+    own2, out3 = parts((3, 0), (0, 1))
     got3 = swap(out3)
     ring1, got2 = passed(ring1, got2)
     ring2 = ring_on(add(ring1, got2, own2))
-    (own3,) = parts([(0, 0)], [f32])
+    (own3,) = parts((0, 0))
 
     low = (low + got_low).astype(bf16)
     low, block_a, other_a = passed(low, block_a, other_a)

time: 188 us -> 172 us (0.915)
  waiting for transfers between devices: 30.4 us -> 12.4 us
  local copies, waits for them, and re-layouts: 12.2 us -> 5.18 us
  Pallas kernels: 108 us -> 113 us
  starting transfers between devices: 28.9 us -> 32.6 us
    ppermute x10, waiting for transfers between devices: 21.2 us -> 11 us  [ring_on(): lax.ppermute(value, 'tensor', [(i, (i + PAIR) % devices) for i in range(d...]
    ppermute x14, waiting for transfers between devices: 9.19 us -> 1.43 us  [swap(): return lax.ppermute(value, 'tensor', [(i, i ^ bit) for i in range(devices)])]
    unnamed x37 -> x39, local copies, waits for them, and re-layouts: 8.08 us -> 0.91 us
    pallas_call x12, Pallas kernels: 99.4 us -> 105 us  [call(): pl.pallas_call(marked, in_specs=[ANYWHERE] + [SCALARS] * len(scalars) + [...]
    ppermute x14, starting transfers between devices: 15.5 us -> 17.7 us  [swap(): return lax.ppermute(value, 'tensor', [(i, i ^ bit) for i in range(devices)])]
  transfers between devices with their start and end apart: 27 -> 27, of which waited for: 9 -> 7; matrix products, arithmetic and copies ran while one was open for 5% -> 6% of each run, Pallas kernels for 58% -> 66%
where the time goes in v2:
time: 172 us
  Pallas kernels  113 us (66%)
  starting transfers between devices  32.6 us (19%)
  waiting for transfers between devices  12.4 us (7%)
  other arithmetic  6.38 us (4%)
  local copies, waits for them, and re-layouts  5.18 us (3%)
    pallas_call x12, Pallas kernels, call(): pl.pallas_call(marked, in_specs=[ANYWHERE] + [SCALARS] * len(scalars) + [...  105 us
    ppermute x14, starting transfers between devices, swap(): return lax.ppermute(value, 'tensor', [(i, i ^ bit) for i in range(devices)])  17.7 us
    ppermute x10, starting transfers between devices, ring_on(): lax.ppermute(value, 'tensor', [(i, (i + PAIR) % devices) for i in range(d...  14.6 us
    ppermute x10, waiting for transfers between devices, ring_on(): lax.ppermute(value, 'tensor', [(i, (i + PAIR) % devices) for i in range(d...  11 us
    pallas_call x2, Pallas kernels, by_tenant(): pl.pallas_call(body, grid=(tenants // at_once,), in_specs=[SCALARS, SCALA...  7.21 us
    convert_element_type x4, other arithmetic, add(): return sum((t.astype(f32) for t in terms)).astype(bf16)  3.78 us
  transfers between devices with their start and end apart: 27, of which 7 were waited for; matrix products, arithmetic and copies ran while one was open for 6% of the time, Pallas kernels for 66%

profile of v2, /device:TPU:0, one launch (start us, length us, event | category | flops | bytes accessed | tf_op | source)
XLA Modules:
  0.0 171.7 jit_solution(2845025234738718906)
XLA Ops:
  0.7 3.1 %collective-permute-start.2 = (bf16[256,1024]{1,0:T(8,128)(2,1)}, bf16[256,1024]{1,0:T(8,128)(2,1)}, u32[]{:S(2)}, u32[]{:S(2)}) collective-permute-start(bf16[256,1024]{1,0:T(8,128)(2,1)} %refs_2_.3), channel_id=1, source_target_pairs={{0,2},{1,3},{2,4},{3,5},{4,6},{5,7},{6,0},{7,1},{8,10},{9,11},{10,... | collective-permute-start | bytes 1572872 | tf_op jit(solution)/shard_map/ppermute | solution.py:442
  3.7 1.5 collective-permute-start.3
  9.5 1.6 collective-permute-start
  11.8 7.0 %collective-permute-done.2.refs_3_ = bf16[256,1024]{1,0:T(8,128)(2,1)} collective-permute-done((bf16[256,1024]{1,0:T(8,128)(2,1)}, bf16[256,1024]{1,0:T(8,128)(2,1)}, u32[]{:S(2)}, u32[]{:S(2)}) %collective-permute-start.2) | collective-permute-done | bytes 524320 | tf_op jit(solution)/shard_map/ppermute | solution.py:442
  18.9 1.6 collective-permute-start.6
  20.5 1.5 collective-permute-start.7
  22.0 12.5 %gate_up.4 = (f32[256,1792]{1,0:T(8,128)}, f32[256,1792]{1,0:T(8,128)}, f32[8,128]{1,0:T(8,128)S(1)}) custom-call(f32[8,128]{1,0:T(8,128)S(1)} %broadcast_in_dim.14.refs_0_, s32[3]{0:T(128)S(1)} %pad_add_fusion.refs_1_, bf16[256,1024]{1,0:T(8,128)(2,1)} %refs_2_.3, bf16[256,1024]{1,0:T(8,128)(2,1)} %collective-permute-done.2.refs_3_, ...), custom_call_target="tpu_custom_call" | custom-call | flops 5637144576 | bytes 22020096 | tf_op jit(solution)/shard_map/gate_up/pallas_call | solution.py:63
  34.6 1.6 collective-permute-start.4
  36.7 8.8 %down_back.3 = (f32[256,1792]{1,0:T(8,128)}, f32[8,128]{1,0:T(8,128)S(1)}) custom-call(f32[8,128]{1,0:T(8,128)S(1)} %get-tuple-element.121.refs_0_, s32[3]{0:T(128)S(1)} %pad_add_fusion.refs_1_, bf16[272,1024]{1,0:T(8,128)(2,1)} %copy-done.7, bf16[272,1024]{1,0:T(8,128)(2,1)} %copy-done.10, bf16[272,1024]{1,0:T(8,128)(2,1)} %copy-done.11, ...), custom_call_target="tpu_custom_call" | custom-call | flops 2818572288 | bytes 11010048 | tf_op jit(solution)/shard_map/down_back/pallas_call | solution.py:63
  47.4 10.8 %gate_up.5 = (f32[256,1792]{1,0:T(8,128)}, f32[256,1792]{1,0:T(8,128)}, f32[8,128]{1,0:T(8,128)S(1)}) custom-call(f32[8,128]{1,0:T(8,128)S(1)} %get-tuple-element.128.refs_0_, s32[2]{0:T(128)S(1)} %get-tuple-element.209.refs_1_, bf16[256,1024]{1,0:T(8,128)(2,1)} %copy-done.15, bf16[256,1024]{1,0:T(8,128)(2,1)} %copy-done.18, bf16[8192,1792]{1,0:T(8,128)(2,1)} %refs_4_.17, ...), custom_call_target="tpu_custom_call" | custom-call | flops 3758096384 | bytes 14680064 | tf_op jit(solution)/shard_map/gate_up/pallas_call | solution.py:63
  58.2 1.8 %collective-permute-start.8 = (bf16[272,1024]{1,0:T(8,128)(2,1)S(1)}, bf16[272,1024]{1,0:T(8,128)(2,1)S(1)}, u32[]{:S(2)}, u32[]{:S(2)}) collective-permute-start(bf16[272,1024]{1,0:T(8,128)(2,1)S(1)} %collective-permute-done.4.refs_2_), channel_id=1, source_target_pairs={{0,2},{1,3},{2,4},{3,5},{4,6},{5,7},{6,0},{7,1},{8,10},{9,11},{10,... | collective-permute-start | bytes 1671176 | tf_op jit(solution)/shard_map/ppermute | solution.py:442
  60.0 7.8 %down_back.4 = (f32[256,1792]{1,0:T(8,128)}, f32[8,128]{1,0:T(8,128)S(1)}) custom-call(f32[8,128]{1,0:T(8,128)S(1)} %get-tuple-element.138.refs_0_, s32[2]{0:T(128)S(1)} %get-tuple-element.209.refs_1_, bf16[272,1024]{1,0:T(8,128)(2,1)} %copy-done.8, bf16[272,1024]{1,0:T(8,128)(2,1)} %copy-done.9, bf16[1792,8192]{1,0:T(8,128)(2,1)} %refs_6_.3, ...), custom_call_target="tpu_custom_call" | custom-call | flops 1879048192 | bytes 7340032 | tf_op jit(solution)/shard_map/down_back/pallas_call | solution.py:63
  69.1 1.6 collective-permute-start.13
  70.6 10.8 %gate_up.6 = (f32[256,1792]{1,0:T(8,128)}, f32[256,1792]{1,0:T(8,128)}, f32[8,128]{1,0:T(8,128)S(1)}) custom-call(f32[8,128]{1,0:T(8,128)S(1)} %get-tuple-element.147.refs_0_, s32[2]{0:T(128)S(1)} %get-tuple-element.212.refs_1_, bf16[256,1024]{1,0:T(8,128)(2,1)} %collective-permute-done.9.refs_2_, bf16[256,1024]{1,0:T(8,128)(2,1)} %copy-done.17, ...), custom_call_target="tpu_custom_call" | custom-call | flops 3758096384 | bytes 14680064 | tf_op jit(solution)/shard_map/gate_up/pallas_call | solution.py:63
  81.4 1.6 collective-permute-start.14
  84.0 10.2 %gate_up.7 = (f32[256,1792]{1,0:T(8,128)}, f32[256,1792]{1,0:T(8,128)}, bf16[256,1792]{1,0:T(8,128)(2,1)}, f32[2,128,64]{2,1,0:T(8,128)S(1)}, f32[8,128]{1,0:T(8,128)S(1)}) custom-call(f32[8,128]{1,0:T(8,128)S(1)} %get-tuple-element.155.refs_0_, s32[1]{0:T(128)} %bitcast.9.refs_1_, s32[2]{0:T(128)S(1)} %copy-done.5, bf16[256,1024]{1,0:T(8,128)(2,1)} %copy-done.16, ...), custom_call_target="tpu_custom_call" | custom-call | flops 1879048192 | bytes 7340032 | tf_op jit(solution)/shard_map/gate_up/pallas_call | solution.py:63
  94.2 1.6 collective-permute-start.12
  98.0 9.6 %down_back.5 = (bf16[256,1792]{1,0:T(8,128)(2,1)S(1)}, bf16[256,1792]{1,0:T(8,128)(2,1)S(1)}, f32[8,128]{1,0:T(8,128)S(1)}) custom-call(f32[8,128]{1,0:T(8,128)S(1)} %get-tuple-element.163.refs_0_, s32[3]{0:T(128)S(1)} %pad_add_fusion.2.refs_1_, s32[2]{0:T(128)S(1)} %copy-done.5, bf16[272,1024]{1,0:T(8,128)(2,1)} %copy-done.12, ...), custom_call_target="tpu_custom_call" | custom-call | flops 2818572288 | bytes 11010048 | tf_op jit(solution)/shard_map/down_back/pallas_call | solution.py:63
  107.6 4.7 %input_parts.5 = (bf16[256,1024]{1,0:T(8,128)(2,1)S(1)}, f32[8,128]{1,0:T(8,128)S(1)}) custom-call(f32[8,128]{1,0:T(8,128)S(1)} %get-tuple-element.170.refs_0_, s32[1]{0:T(128)} %bitcast.6.refs_1_, bf16[256,1792]{1,0:T(8,128)(2,1)S(1)} %get-tuple-element.171.refs_2_, bf16[256,1792]{1,0:T(8,128)(2,1)S(1)} %get-tuple-element.172.refs_3_, ...), custom_call_target="tpu_custom_call" | custom-call | flops 1879048192 | bytes 7340032 | tf_op jit(solution)/shard_map/input_parts/pallas_call | solution.py:63
  112.3 1.6 collective-permute-start.15
  114.1 1.9 %collective-permute-start.16 = (f32[2,128,64]{2,1,0:T(8,128)S(1)}, f32[2,128,64]{2,1,0:T(8,128)S(1)}, u32[]{:S(2)}, u32[]{:S(2)}) collective-permute-start(f32[2,128,64]{2,1,0:T(8,128)S(1)} %add.245), channel_id=1, source_target_pairs={{0,4},{1,5},{2,6},{3,7},{4,0},{5,1},{6,2},{7,3},{8,12},{9,13},{10,... | collective-permute-start | bytes 196616 | tf_op jit(solution)/shard_map/ppermute | solution.py:445
  116.0 8.0 %input_parts.6 = (bf16[256,1024]{1,0:T(8,128)(2,1)S(1)}, bf16[256,1024]{1,0:T(8,128)(2,1)S(1)}, f32[8,128]{1,0:T(8,128)S(1)}) custom-call(f32[8,128]{1,0:T(8,128)S(1)} %get-tuple-element.178.refs_0_, s32[2]{0:T(128)S(1)} %get-tuple-element.211.refs_1_, bf16[256,1792]{1,0:T(8,128)(2,1)S(1)} %get-tuple-element.171.refs_2_, ...), custom_call_target="tpu_custom_call" | custom-call | flops 3758096384 | bytes 14680064 | tf_op jit(solution)/shard_map/input_parts/pallas_call | solution.py:63
  126.6 2.2 %collective-permute-start.17 = (bf16[256,1024]{1,0:T(8,128)(2,1)}, bf16[256,1024]{1,0:T(8,128)(2,1)}, u32[]{:S(2)}, u32[]{:S(2)}) collective-permute-start(bf16[256,1024]{1,0:T(8,128)(2,1)} %add_convert_fusion.3), channel_id=1, source_target_pairs={{0,2},{1,3},{2,4},{3,5},{4,6},{5,7},{6,0},{7,1},{8,10},{9,11},{10,... | collective-permute-start | bytes 1572872 | tf_op jit(solution)/shard_map/ppermute | solution.py:442
  129.6 2.5 %collective-permute-start.24 = (f32[2,128,64]{2,1,0:T(8,128)S(1)}, f32[2,128,64]{2,1,0:T(8,128)S(1)}, u32[]{:S(2)}, u32[]{:S(2)}) collective-permute-start(f32[2,128,64]{2,1,0:T(8,128)S(1)} %add.253), channel_id=1, source_target_pairs={{0,1},{1,0},{2,3},{3,2},{4,5},{5,4},{6,7},{7,6},{8,9},{9,8},{10,11... | collective-permute-start | bytes 196616 | tf_op jit(solution)/shard_map/ppermute | solution.py:445
  132.1 8.1 %input_parts.7 = (bf16[256,1024]{1,0:T(8,128)(2,1)S(1)}, bf16[256,1024]{1,0:T(8,128)(2,1)S(1)}, f32[8,128]{1,0:T(8,128)S(1)}) custom-call(f32[8,128]{1,0:T(8,128)S(1)} %get-tuple-element.184.refs_0_, s32[2]{0:T(128)S(1)} %get-tuple-element.210.refs_1_, bf16[256,1792]{1,0:T(8,128)(2,1)S(1)} %get-tuple-element.171.refs_2_, ...), custom_call_target="tpu_custom_call" | custom-call | flops 3758096384 | bytes 14680064 | tf_op jit(solution)/shard_map/input_parts/pallas_call | solution.py:63
  143.6 8.1 %input_parts.8 = (bf16[256,1024]{1,0:T(8,128)(2,1)S(1)}, bf16[256,1024]{1,0:T(8,128)(2,1)S(1)}, f32[8,128]{1,0:T(8,128)S(1)}) custom-call(f32[8,128]{1,0:T(8,128)S(1)} %get-tuple-element.195.refs_0_, s32[2]{0:T(128)S(1)} %pad_add_fusion.5.refs_1_, bf16[256,1792]{1,0:T(8,128)(2,1)S(1)} %get-tuple-element.171.refs_2_, ...), custom_call_target="tpu_custom_call" | custom-call | flops 3758096384 | bytes 14680064 | tf_op jit(solution)/shard_map/input_parts/pallas_call | solution.py:63
  151.7 2.0 %collective-permute-start.22 = (bf16[256,1024]{1,0:T(8,128)(2,1)S(1)}, bf16[256,1024]{1,0:T(8,128)(2,1)S(1)}, u32[]{:S(2)}, u32[]{:S(2)}) collective-permute-start(bf16[256,1024]{1,0:T(8,128)(2,1)S(1)} %get-tuple-element.200), channel_id=1, source_target_pairs={{0,1},{1,0},{2,3},{3,2},{4,5},{5,4},{6,7},{7,6},{8,9},{9,8},{10,11... | collective-permute-start | bytes 1572872 | tf_op jit(solution)/shard_map/ppermute | solution.py:445
  154.4 1.6 collective-permute-done.19
  156.5 4.1 %by_tenant.2 = f32[16,64,1792]{2,1,0:T(8,128)} custom-call(s32[4]{0:T(128)S(1)} %broadcast_select_fusion.1.labels_ref, f32[4]{0:T(128)S(1)} %broadcast_6_scales_ref.2.scales_ref, bf16[4,64,1792]{2,1,0:T(8,128)(2,1)S(1)} %maximum_select_fusion.parts_ref), custom_call_target="tpu_custom_call" | custom-call | bytes 7340032 | tf_op jit(solution)/shard_map/by_tenant/pallas_call | solution.py:403
  160.6 5.3 %input_parts.9 = (bf16[256,1024]{1,0:T(8,128)(2,1)S(1)}, f32[8,128]{1,0:T(8,128)}) custom-call(f32[8,128]{1,0:T(8,128)S(1)} %get-tuple-element.201.refs_0_, s32[1]{0:T(128)} %bitcast.2.refs_1_, bf16[256,1792]{1,0:T(8,128)(2,1)S(1)} %get-tuple-element.171.refs_2_, bf16[256,1792]{1,0:T(8,128)(2,1)S(1)} %get-tuple-element.172.refs_3_, ...), custom_call_target="tpu_custom_call" | custom-call | flops 1879048192 | bytes 7340032 | tf_op jit(solution)/shard_map/input_parts/pallas_call | solution.py:63
  166.0 3.1 %by_tenant.3 = f32[16,64,1024]{2,1,0:T(8,128)} custom-call(s32[4]{0:T(128)S(1)} %broadcast_select_fusion.1.labels_ref, f32[4]{0:T(128)S(1)} %gather_fusion.3, bf16[4,64,1024]{2,1,0:T(8,128)(2,1)S(1)} %maximum_select_fusion.1.parts_ref), custom_call_target="tpu_custom_call" | custom-call | bytes 4194304 | tf_op jit(solution)/shard_map/by_tenant/pallas_call | solution.py:403
  169.1 1.6 collective-permute-done.21
  (113 shorter events, 20.8 us)
Async XLA Ops:
  0.6 8.8 %copy-start.2 = (bf16[256,1024]{1,0:T(8,128)(2,1)S(1)}, bf16[256,1024]{1,0:T(8,128)(2,1)}, u32[]{:S(2)}) copy-start(bf16[256,1024]{1,0:T(8,128)(2,1)} %r.1) | copy-start | bytes 1572868
  0.7 18.2 %collective-permute-start.2 = (bf16[256,1024]{1,0:T(8,128)(2,1)}, bf16[256,1024]{1,0:T(8,128)(2,1)}, u32[]{:S(2)}, u32[]{:S(2)}) collective-permute-start(bf16[256,1024]{1,0:T(8,128)(2,1)} %refs_2_.3), channel_id=1, source_target_pairs={{0,2},{1,3},{2,4},{3,5},{4,6},{5,7},{6,0},{7,1},{8,10},{9,11},{10,... | collective-permute-start | bytes 1572872 | tf_op jit(solution)/shard_map/ppermute | solution.py:442
  3.7 15.2 %collective-permute-start.3 = (bf16[256,1024]{1,0:T(8,128)(2,1)}, bf16[256,1024]{1,0:T(8,128)(2,1)}, u32[]{:S(2)}, u32[]{:S(2)}) collective-permute-start(bf16[256,1024]{1,0:T(8,128)(2,1)} %refs_2_.3), channel_id=1, source_target_pairs={{0,1},{1,0},{2,3},{3,2},{4,5},{5,4},{6,7},{7,6},{8,9},{9,8},{10,11... | collective-permute-start | bytes 1572872 | tf_op jit(solution)/shard_map/ppermute | solution.py:445
  9.5 25.0 %copy-start.7 = (bf16[272,1024]{1,0:T(8,128)(2,1)}, bf16[272,1024]{1,0:T(8,128)(2,1)S(1)}, u32[]{:S(2)}) copy-start(bf16[272,1024]{1,0:T(8,128)(2,1)S(1)} %constant_dynamic-update-slice_fusion.refs_2_) | copy-start | bytes 1671172
  9.5 25.0 %collective-permute-start = (bf16[272,1024]{1,0:T(8,128)(2,1)S(1)}, bf16[272,1024]{1,0:T(8,128)(2,1)S(1)}, u32[]{:S(2)}, u32[]{:S(2)}) collective-permute-start(bf16[272,1024]{1,0:T(8,128)(2,1)S(1)} %constant_dynamic-update-slice_fusion.refs_2_), channel_id=1, source_target_pairs={{0,2},{1,3},{2,4},{3,5},{4,6},{5,7},{6,0},{7,1},{8,10},{9,11},{10,... | collective-permute-start | bytes 1671176 | tf_op jit(solution)/shard_map/ppermute | solution.py:442
  11.2 23.4 %collective-permute-start.1 = (bf16[272,1024]{1,0:T(8,128)(2,1)S(1)}, bf16[272,1024]{1,0:T(8,128)(2,1)S(1)}, u32[]{:S(2)}, u32[]{:S(2)}) collective-permute-start(bf16[272,1024]{1,0:T(8,128)(2,1)S(1)} %constant_dynamic-update-slice_fusion.refs_2_), channel_id=1, source_target_pairs={{0,1},{1,0},{2,3},{3,2},{4,5},{5,4},{6,7},{7,6},{8,9},{9,8},{10,11... | collective-permute-start | bytes 1671176 | tf_op jit(solution)/shard_map/ppermute | solution.py:445
  18.9 26.7 %collective-permute-start.6 = (bf16[256,1024]{1,0:T(8,128)(2,1)}, bf16[256,1024]{1,0:T(8,128)(2,1)S(1)}, u32[]{:S(2)}, u32[]{:S(2)}) collective-permute-start(bf16[256,1024]{1,0:T(8,128)(2,1)} %collective-permute-done.2.refs_3_), channel_id=1, source_target_pairs={{0,2},{1,3},{2,4},{3,5},{4,6},{5,7},{6,0},{7,1},{8,10},{9,11},{10,... | collective-permute-start | bytes 1572872 | tf_op jit(solution)/shard_map/ppermute | solution.py:442
  20.5 25.1 %collective-permute-start.7 = (bf16[256,1024]{1,0:T(8,128)(2,1)}, bf16[256,1024]{1,0:T(8,128)(2,1)S(1)}, u32[]{:S(2)}, u32[]{:S(2)}) collective-permute-start(bf16[256,1024]{1,0:T(8,128)(2,1)} %collective-permute-done.2.refs_3_), channel_id=1, source_target_pairs={{0,1},{1,0},{2,3},{3,2},{4,5},{5,4},{6,7},{7,6},{8,9},{9,8},{10,11... | collective-permute-start | bytes 1572872 | tf_op jit(solution)/shard_map/ppermute | solution.py:445
  34.6 23.6 %collective-permute-start.4 = (bf16[272,1024]{1,0:T(8,128)(2,1)S(1)}, bf16[272,1024]{1,0:T(8,128)(2,1)S(1)}, u32[]{:S(2)}, u32[]{:S(2)}) collective-permute-start(bf16[272,1024]{1,0:T(8,128)(2,1)S(1)} %collective-permute-done.refs_3_), channel_id=1, source_target_pairs={{0,2},{1,3},{2,4},{3,5},{4,6},{5,7},{6,0},{7,1},{8,10},{9,11},{10,... | collective-permute-start | bytes 1671176 | tf_op jit(solution)/shard_map/ppermute | solution.py:442
  36.2 22.0 %collective-permute-start.5 = (bf16[272,1024]{1,0:T(8,128)(2,1)S(1)}, bf16[272,1024]{1,0:T(8,128)(2,1)S(1)}, u32[]{:S(2)}, u32[]{:S(2)}) collective-permute-start(bf16[272,1024]{1,0:T(8,128)(2,1)S(1)} %collective-permute-done.refs_3_), channel_id=1, source_target_pairs={{0,1},{1,0},{2,3},{3,2},{4,5},{5,4},{6,7},{7,6},{8,9},{9,8},{10,11... | collective-permute-start | bytes 1671176 | tf_op jit(solution)/shard_map/ppermute | solution.py:445
  45.6 22.2 %collective-permute-start.9 = (bf16[256,1024]{1,0:T(8,128)(2,1)S(1)}, bf16[256,1024]{1,0:T(8,128)(2,1)}, u32[]{:S(2)}, u32[]{:S(2)}) collective-permute-start(bf16[256,1024]{1,0:T(8,128)(2,1)S(1)} %collective-permute-done.6.refs_2_), channel_id=1, source_target_pairs={{0,2},{1,3},{2,4},{3,5},{4,6},{5,7},{6,0},{7,1},{8,10},{9,11},{10,... | collective-permute-start | bytes 1572872 | tf_op jit(solution)/shard_map/ppermute | solution.py:442
  46.2 21.7 %collective-permute-start.10 = (bf16[256,1024]{1,0:T(8,128)(2,1)S(1)}, bf16[256,1024]{1,0:T(8,128)(2,1)S(1)}, u32[]{:S(2)}, u32[]{:S(2)}) collective-permute-start(bf16[256,1024]{1,0:T(8,128)(2,1)S(1)} %collective-permute-done.6.refs_2_), channel_id=1, source_target_pairs={{0,1},{1,0},{2,3},{3,2},{4,5},{5,4},{6,7},{7,6},{8,9},{9,8},{10,11... | collective-permute-start | bytes 1572872 | tf_op jit(solution)/shard_map/ppermute | solution.py:445
  58.2 23.2 %collective-permute-start.8 = (bf16[272,1024]{1,0:T(8,128)(2,1)S(1)}, bf16[272,1024]{1,0:T(8,128)(2,1)S(1)}, u32[]{:S(2)}, u32[]{:S(2)}) collective-permute-start(bf16[272,1024]{1,0:T(8,128)(2,1)S(1)} %collective-permute-done.4.refs_2_), channel_id=1, source_target_pairs={{0,2},{1,3},{2,4},{3,5},{4,6},{5,7},{6,0},{7,1},{8,10},{9,11},{10,... | collective-permute-start | bytes 1671176 | tf_op jit(solution)/shard_map/ppermute | solution.py:442
  60.0 8.9 %copy-start.5 = (s32[2]{0:T(128)S(1)}, s32[2]{0:T(128)}, u32[]{:S(2)}) copy-start(s32[2]{0:T(128)} %refs_2_.5) | copy-start | bytes 28
  68.6 12.8 %collective-permute-start.11 = (bf16[256,1024]{1,0:T(8,128)(2,1)}, bf16[256,1024]{1,0:T(8,128)(2,1)S(1)}, u32[]{:S(2)}, u32[]{:S(2)}) collective-permute-start(bf16[256,1024]{1,0:T(8,128)(2,1)} %collective-permute-done.9.refs_2_), channel_id=1, source_target_pairs={{0,1},{1,0},{2,3},{3,2},{4,5},{5,4},{6,7},{7,6},{8,9},{9,8},{10,11... | collective-permute-start | bytes 1572872 | tf_op jit(solution)/shard_map/ppermute | solution.py:445
  69.0 45.1 %collective-permute-start.23 = (s32[2]{0:T(128)S(1)}, s32[2]{0:T(128)S(1)}, u32[]{:S(2)}, u32[]{:S(2)}) collective-permute-start(s32[2]{0:T(128)S(1)} %copy-done.5), channel_id=1, source_target_pairs={{0,8},{8,0},{1,9},{9,1},{2,10},{10,2},{3,11},{11,3},{4,12},{12,4},... | collective-permute-start | bytes 32 | tf_op jit(solution)/shard_map/ppermute | solution.py:448
  69.1 26.8 %collective-permute-start.13 = (bf16[272,1024]{1,0:T(8,128)(2,1)}, bf16[272,1024]{1,0:T(8,128)(2,1)S(1)}, u32[]{:S(2)}, u32[]{:S(2)}) collective-permute-start(bf16[272,1024]{1,0:T(8,128)(2,1)} %copy-done.9), channel_id=1, source_target_pairs={{0,2},{1,3},{2,4},{3,5},{4,6},{5,7},{6,0},{7,1},{8,10},{9,11},{10,... | collective-permute-start | bytes 1671176 | tf_op jit(solution)/shard_map/ppermute | solution.py:442
  70.6 12.5 %copy-start.6 = (s32[16]{0:T(128)S(1)}, s32[16]{0:T(128)}, u32[]{:S(2)}) copy-start(s32[16]{0:T(128)} %param.17) | copy-start | bytes 196
  81.4 14.9 %copy-start.12 = (bf16[272,1024]{1,0:T(8,128)(2,1)}, bf16[272,1024]{1,0:T(8,128)(2,1)S(1)}, u32[]{:S(2)}) copy-start(bf16[272,1024]{1,0:T(8,128)(2,1)S(1)} %collective-permute-done.8.refs_3_) | copy-start | bytes 1671172
  81.4 14.8 %collective-permute-start.14 = (bf16[272,1024]{1,0:T(8,128)(2,1)S(1)}, bf16[272,1024]{1,0:T(8,128)(2,1)S(1)}, u32[]{:S(2)}, u32[]{:S(2)}) collective-permute-start(bf16[272,1024]{1,0:T(8,128)(2,1)S(1)} %collective-permute-done.8.refs_3_), channel_id=1, source_target_pairs={{0,1},{1,0},{2,3},{3,2},{4,5},{5,4},{6,7},{7,6},{8,9},{9,8},{10,11... | collective-permute-start | bytes 1671176 | tf_op jit(solution)/shard_map/ppermute | solution.py:445
  94.2 13.4 %collective-permute-start.12 = (f32[2,128,64]{2,1,0:T(8,128)S(1)}, f32[2,128,64]{2,1,0:T(8,128)S(1)}, u32[]{:S(2)}, u32[]{:S(2)}) collective-permute-start(f32[2,128,64]{2,1,0:T(8,128)S(1)} %broadcast_multiply_fusion), channel_id=1, source_target_pairs={{0,2},{1,3},{2,0},{3,1},{4,6},{5,7},{6,4},{7,5},{8,10},{9,11},{10,... | collective-permute-start | bytes 196616 | tf_op jit(solution)/shard_map/ppermute | solution.py:445
  112.3 13.3 %collective-permute-start.15 = (bf16[256,1024]{1,0:T(8,128)(2,1)S(1)}, bf16[256,1024]{1,0:T(8,128)(2,1)S(1)}, u32[]{:S(2)}, u32[]{:S(2)}) collective-permute-start(bf16[256,1024]{1,0:T(8,128)(2,1)S(1)} %get-tuple-element.173), channel_id=1, source_target_pairs={{0,1},{1,0},{2,3},{3,2},{4,5},{5,4},{6,7},{7,6},{8,9},{9,8},{10,11... | collective-permute-start | bytes 1572872 | tf_op jit(solution)/shard_map/ppermute | solution.py:445
  114.1 10.6 %collective-permute-start.16 = (f32[2,128,64]{2,1,0:T(8,128)S(1)}, f32[2,128,64]{2,1,0:T(8,128)S(1)}, u32[]{:S(2)}, u32[]{:S(2)}) collective-permute-start(f32[2,128,64]{2,1,0:T(8,128)S(1)} %add.245), channel_id=1, source_target_pairs={{0,4},{1,5},{2,6},{3,7},{4,0},{5,1},{6,2},{7,3},{8,12},{9,13},{10,... | collective-permute-start | bytes 196616 | tf_op jit(solution)/shard_map/ppermute | solution.py:445
  124.1 16.2 %collective-permute-start.18 = (bf16[256,1024]{1,0:T(8,128)(2,1)S(1)}, bf16[256,1024]{1,0:T(8,128)(2,1)}, u32[]{:S(2)}, u32[]{:S(2)}) collective-permute-start(bf16[256,1024]{1,0:T(8,128)(2,1)S(1)} %get-tuple-element.183), channel_id=1, source_target_pairs={{0,1},{1,0},{2,3},{3,2},{4,5},{5,4},{6,7},{7,6},{8,9},{9,8},{10,11... | collective-permute-start | bytes 1572872 | tf_op jit(solution)/shard_map/ppermute | solution.py:445
  126.6 14.4 %collective-permute-start.17 = (bf16[256,1024]{1,0:T(8,128)(2,1)}, bf16[256,1024]{1,0:T(8,128)(2,1)}, u32[]{:S(2)}, u32[]{:S(2)}) collective-permute-start(bf16[256,1024]{1,0:T(8,128)(2,1)} %add_convert_fusion.3), channel_id=1, source_target_pairs={{0,2},{1,3},{2,4},{3,5},{4,6},{5,7},{6,0},{7,1},{8,10},{9,11},{10,... | collective-permute-start | bytes 1572872 | tf_op jit(solution)/shard_map/ppermute | solution.py:442
  129.6 14.0 %collective-permute-start.24 = (f32[2,128,64]{2,1,0:T(8,128)S(1)}, f32[2,128,64]{2,1,0:T(8,128)S(1)}, u32[]{:S(2)}, u32[]{:S(2)}) collective-permute-start(f32[2,128,64]{2,1,0:T(8,128)S(1)} %add.253), channel_id=1, source_target_pairs={{0,1},{1,0},{2,3},{3,2},{4,5},{5,4},{6,7},{7,6},{8,9},{9,8},{10,11... | collective-permute-start | bytes 196616 | tf_op jit(solution)/shard_map/ppermute | solution.py:445
  140.2 14.2 %collective-permute-start.20 = (bf16[256,1024]{1,0:T(8,128)(2,1)S(1)}, bf16[256,1024]{1,0:T(8,128)(2,1)S(1)}, u32[]{:S(2)}, u32[]{:S(2)}) collective-permute-start(bf16[256,1024]{1,0:T(8,128)(2,1)S(1)} %get-tuple-element.189), channel_id=1, source_target_pairs={{0,1},{1,0},{2,3},{3,2},{4,5},{5,4},{6,7},{7,6},{8,9},{9,8},{10,11... | collective-permute-start | bytes 1572872 | tf_op jit(solution)/shard_map/ppermute | solution.py:445
  142.6 13.4 %collective-permute-start.19 = (bf16[256,1024]{1,0:T(8,128)(2,1)S(1)}, bf16[256,1024]{1,0:T(8,128)(2,1)S(1)}, u32[]{:S(2)}, u32[]{:S(2)}) collective-permute-start(bf16[256,1024]{1,0:T(8,128)(2,1)S(1)} %add_convert_fusion.2), channel_id=1, source_target_pairs={{0,2},{1,3},{2,4},{3,5},{4,6},{5,7},{6,0},{7,1},{8,10},{9,11},{10,... | collective-permute-start | bytes 1572872 | tf_op jit(solution)/shard_map/ppermute | solution.py:442
  143.5 10.2 %collective-permute-start.25 = (bf16[2,64,1792]{2,1,0:T(8,128)(2,1)S(1)}, bf16[2,64,1792]{2,1,0:T(8,128)(2,1)S(1)}, u32[]{:S(2)}, u32[]{:S(2)}) collective-permute-start(bf16[2,64,1792]{2,1,0:T(8,128)(2,1)S(1)} %block_products.2), channel_id=1, source_target_pairs={{0,8},{8,0},{1,9},{9,1},{2,10},{10,2},{3,11},{11,3},{4,12},{12,4},... | collective-permute-start | bytes 1376264 | tf_op jit(solution)/shard_map/ppermute | solution.py:448
  151.7 17.4 %collective-permute-start.22 = (bf16[256,1024]{1,0:T(8,128)(2,1)S(1)}, bf16[256,1024]{1,0:T(8,128)(2,1)S(1)}, u32[]{:S(2)}, u32[]{:S(2)}) collective-permute-start(bf16[256,1024]{1,0:T(8,128)(2,1)S(1)} %get-tuple-element.200), channel_id=1, source_target_pairs={{0,1},{1,0},{2,3},{3,2},{4,5},{5,4},{6,7},{7,6},{8,9},{9,8},{10,11... | collective-permute-start | bytes 1572872 | tf_op jit(solution)/shard_map/ppermute | solution.py:445
  154.1 11.7 %collective-permute-start.26 = (bf16[2,64,1024]{2,1,0:T(8,128)(2,1)S(1)}, bf16[2,64,1024]{2,1,0:T(8,128)(2,1)S(1)}, u32[]{:S(2)}, u32[]{:S(2)}) collective-permute-start(bf16[2,64,1024]{2,1,0:T(8,128)(2,1)S(1)} %block_products.3), channel_id=1, source_target_pairs={{0,8},{8,0},{1,9},{9,1},{2,10},{10,2},{3,11},{11,3},{4,12},{12,4},... | collective-permute-start | bytes 786440 | tf_op jit(solution)/shard_map/ppermute | solution.py:448
  156.3 14.4 %collective-permute-start.21 = (bf16[256,1024]{1,0:T(8,128)(2,1)S(1)}, bf16[256,1024]{1,0:T(8,128)(2,1)S(1)}, u32[]{:S(2)}, u32[]{:S(2)}) collective-permute-start(bf16[256,1024]{1,0:T(8,128)(2,1)S(1)} %add_convert_fusion.1), channel_id=1, source_target_pairs={{0,2},{1,3},{2,4},{3,5},{4,6},{5,7},{6,0},{7,1},{8,10},{9,11},{10,... | collective-permute-start | bytes 1572872 | tf_op jit(solution)/shard_map/ppermute | solution.py:442
  (14 other events, 35.6 us)

commit v3 on v2

--- a/solution.py
+++ b/solution.py
@@ -184,7 +184,7 @@
     scratch = buffers(1, *[((rows, depth), bf16)] * count)
     scratch += buffers(slots, *[((depth, tile), bf16)] * (2 * count))
     scratch += buffers(slots, *[((rows, tile), f32)] * (0 if sums is None else 2))
-    scratch += buffers(2, *[((rank, tile), bf16)] * blocks)
+    scratch += buffers(slots, *[((rank, tile), bf16)] * blocks)
     scratch += buffers(2, *[((rows, tile), t) for t in types])
     scratch += [] if low is None else buffers(1, ((blocks, length, rank), f32))
 
@@ -363,11 +363,11 @@
     return call(body, "input_parts", mark, [places], far, outs, scratch, 16, estimate)
 
 
-def block_products(left, right):
+def block_products(mark, left, right):
     blocks, length, rank = left.shape
     width = right.shape[1]
 
-    def body(l, r, out):
+    def body(_, l, r, out):
         out[0] = lax.dot_general(
             l[0], r[...], (((0,), (0,)), ((), ())), preferred_element_type=f32
         ).astype(bf16)
@@ -376,6 +376,7 @@
         body,
         grid=(blocks,),
         in_specs=[
+            ANYWHERE,
             pl.BlockSpec((1, length, rank), lambda b: (b, 0, 0)),
             pl.BlockSpec((length, width), lambda b: (b, 0)),
         ],
@@ -384,13 +385,13 @@
         compiler_params=pltpu.CompilerParams(vmem_limit_bytes=16 << 20),
         cost_estimate=cost(2 * blocks * length * rank * width, left.size * 2 + right.size * 2),
         name="block_products",
-    )(left, right)
-
-
-def by_tenant(labels, scales, parts, tenants, at_once=4):
+    )(mark, left, right)
+
+
+def by_tenant(mark, labels, scales, parts, tenants, at_once=4):
     count, rank, width = parts.shape
 
-    def body(labels_ref, scales_ref, parts_ref, out):
+    def body(_, labels_ref, scales_ref, parts_ref, out):
         first = pl.program_id(0) * at_once
         out[...] = jnp.zeros_like(out)
         for c in range(count):
@@ -403,13 +404,13 @@
     return pl.pallas_call(
         body,
         grid=(tenants // at_once,),
-        in_specs=[SCALARS, SCALARS, pl.BlockSpec((count, rank, width), lambda t: (0, 0, 0))],
+        in_specs=[ANYWHERE, SCALARS, SCALARS, pl.BlockSpec((count, rank, width), lambda t: (0, 0, 0))],
         out_specs=pl.BlockSpec((at_once, rank, width), lambda t: (t, 0, 0)),
         out_shape=jax.ShapeDtypeStruct((tenants, rank, width), f32),
         compiler_params=pltpu.CompilerParams(vmem_limit_bytes=16 << 20),
         cost_estimate=cost(0, 4 * tenants * rank * width),
         name="by_tenant",
-    )(labels, scales, parts)
+    )(mark, labels, scales, parts)
 
 
 def ringed(
@@ -518,10 +519,10 @@
     landed(4)
     start(5, 1)
     start(6, 0)
-    sums = add_up(["T30", "T21"], sums)
+    sums = add_up(["T30"], sums)
     landed(5)
     start(6, 1)
-    act, slope, hidden, low = add_up(["T31"], sums, (tenant, adapter))
+    act, slope, hidden, low = add_up(["T21", "T31"], sums, (tenant, adapter))
     low = low * mask_of
     got_low = swap(low, PAIR)
     landed(6)
@@ -555,25 +556,22 @@
     ring0 = ring_on(add(got0, own0))
     own1, out2 = parts((2, 0), (3, 1))
     got2 = swap(out2)
-    ring0, got1 = passed(ring0, got1)
+    ring0, got1, low, got_low = passed(ring0, got1, low, got_low)
     ring1 = ring_on(add(ring0, got1, own1))
     hidden, back = passed(hidden, back)
-    block_a = block_products(back, hidden)
-    other_a = other_core(block_a)
-    (block_a,) = passed(block_a)
+    block_a = block_products(mark, back, hidden)
+    block_b = block_products(mark, (low + got_low).astype(bf16), cotangent)
+    other_a, other_b = other_core(block_a), other_core(block_b)
+    block_a, block_b = passed(block_a, block_b)
     own2, out3 = parts((3, 0), (0, 1))
     got3 = swap(out3)
-    ring1, got2 = passed(ring1, got2)
+    ring1, got2, other_a, other_b = passed(ring1, got2, other_a, other_b)
     ring2 = ring_on(add(ring1, got2, own2))
     (own3,) = parts((0, 0))
 
-    low = (low + got_low).astype(bf16)
-    low, block_a, other_a = passed(low, block_a, other_a)
-    block_b = block_products(low, cotangent)
-    other_b = other_core(block_b)
     ones = jnp.ones_like(label_scales)
-    grad_a = by_tenant(labels, ones, both_cores(block_a, other_a), tenants)
-    grad_b = by_tenant(labels, label_scales, both_cores(block_b, other_b), tenants)
+    grad_a = by_tenant(mark, labels, ones, both_cores(block_a, other_a), tenants)
+    grad_b = by_tenant(mark, labels, label_scales, both_cores(block_b, other_b), tenants)
     return add(ring2, got3, own3), grad_a.transpose(0, 2, 1), grad_b
 
 

time: 172 us -> 168 us (0.977)
  starting transfers between devices: 32.6 us -> 29.2 us
  Pallas kernels: 113 us -> 110 us
    ppermute x14, starting transfers between devices: 17.7 us -> 14.8 us  [swap(): return lax.ppermute(value, 'tensor', [(i, i ^ bit) for i in range(devices)])]
    pallas_call x12, Pallas kernels: 105 us -> 102 us  [call(): pl.pallas_call(marked, in_specs=[ANYWHERE] + [SCALARS] * len(scalars) + [...]
    ppermute x14, waiting for transfers between devices: 1.43 us -> 3.3 us  [swap(): return lax.ppermute(value, 'tensor', [(i, i ^ bit) for i in range(devices)])]
  transfers between devices with their start and end apart: 27 -> 27, of which waited for: 7 -> 6; matrix products, arithmetic and copies ran while one was open for 6% -> 7% of each run, Pallas kernels for 66% -> 66%
where the time goes in v3:
time: 168 us; the launch traced here: 167 us
  Pallas kernels  110 us (65%)
  starting transfers between devices  29.2 us (17%)
  waiting for transfers between devices  12.9 us (8%)
  other arithmetic  6.4 us (4%)
  local copies, waits for them, and re-layouts  6.03 us (4%)
    pallas_call x12, Pallas kernels, call(): pl.pallas_call(marked, in_specs=[ANYWHERE] + [SCALARS] * len(scalars) + [...  102 us
    ppermute x14, starting transfers between devices, swap(): return lax.ppermute(value, 'tensor', [(i, i ^ bit) for i in range(devices)])  14.8 us
    ppermute x10, starting transfers between devices, ring_on(): lax.ppermute(value, 'tensor', [(i, (i + PAIR) % devices) for i in range(d...  13.7 us
    ppermute x10, waiting for transfers between devices, ring_on(): lax.ppermute(value, 'tensor', [(i, (i + PAIR) % devices) for i in range(d...  9.62 us
    pallas_call x2, Pallas kernels, by_tenant(): pl.pallas_call(body, grid=(tenants // at_once,), in_specs=[ANYWHERE, SCAL...  7.15 us
    convert_element_type x4, other arithmetic, add(): return sum((t.astype(f32) for t in terms)).astype(bf16)  3.79 us
  transfers between devices with their start and end apart: 27, of which 6 were waited for; matrix products, arithmetic and copies ran while one was open for 7% of the time, Pallas kernels for 66%

profile of v3, /device:TPU:0, one launch (start us, length us, event | category | flops | bytes accessed | tf_op | source)
XLA Modules:
  0.0 167.4 jit_solution(7924121299046178531)
XLA Ops:
  0.7 3.1 %collective-permute-start.2 = (bf16[256,1024]{1,0:T(8,128)(2,1)}, bf16[256,1024]{1,0:T(8,128)(2,1)}, u32[]{:S(2)}, u32[]{:S(2)}) collective-permute-start(bf16[256,1024]{1,0:T(8,128)(2,1)} %refs_2_.3), channel_id=1, source_target_pairs={{0,2},{1,3},{2,4},{3,5},{4,6},{5,7},{6,0},{7,1},{8,10},{9,11},{10,... | collective-permute-start | bytes 1572872 | tf_op jit(solution)/shard_map/ppermute | solution.py:443
  3.7 1.5 collective-permute-start.3
  6.5 1.3 gather_fusion.1
  7.9 1.4 fusion.1
  9.6 1.6 collective-permute-start
  11.9 7.0 %collective-permute-done.2.refs_3_ = bf16[256,1024]{1,0:T(8,128)(2,1)} collective-permute-done((bf16[256,1024]{1,0:T(8,128)(2,1)}, bf16[256,1024]{1,0:T(8,128)(2,1)}, u32[]{:S(2)}, u32[]{:S(2)}) %collective-permute-start.2) | collective-permute-done | bytes 524320 | tf_op jit(solution)/shard_map/ppermute | solution.py:443
  18.9 1.6 collective-permute-start.6
  20.5 1.5 collective-permute-start.7
  22.0 12.5 %gate_up.4 = (f32[256,1792]{1,0:T(8,128)}, f32[256,1792]{1,0:T(8,128)}, f32[8,128]{1,0:T(8,128)S(1)}) custom-call(f32[8,128]{1,0:T(8,128)S(1)} %broadcast_in_dim.14.refs_0_, s32[3]{0:T(128)S(1)} %pad_add_fusion.refs_1_, bf16[256,1024]{1,0:T(8,128)(2,1)} %refs_2_.3, bf16[256,1024]{1,0:T(8,128)(2,1)} %collective-permute-done.2.refs_3_, ...), custom_call_target="tpu_custom_call" | custom-call | flops 5637144576 | bytes 22020096 | tf_op jit(solution)/shard_map/gate_up/pallas_call | solution.py:63
  34.6 1.6 collective-permute-start.4
  36.7 8.8 %down_back.3 = (f32[256,1792]{1,0:T(8,128)}, f32[8,128]{1,0:T(8,128)S(1)}) custom-call(f32[8,128]{1,0:T(8,128)S(1)} %get-tuple-element.125.refs_0_, s32[3]{0:T(128)S(1)} %pad_add_fusion.refs_1_, bf16[272,1024]{1,0:T(8,128)(2,1)} %copy-done.7, bf16[272,1024]{1,0:T(8,128)(2,1)} %copy-done.10, bf16[272,1024]{1,0:T(8,128)(2,1)} %copy-done.11, ...), custom_call_target="tpu_custom_call" | custom-call | flops 2818572288 | bytes 11010048 | tf_op jit(solution)/shard_map/down_back/pallas_call | solution.py:63
  47.4 10.8 %gate_up.5 = (f32[256,1792]{1,0:T(8,128)}, f32[256,1792]{1,0:T(8,128)}, f32[8,128]{1,0:T(8,128)S(1)}) custom-call(f32[8,128]{1,0:T(8,128)S(1)} %get-tuple-element.132.refs_0_, s32[2]{0:T(128)S(1)} %get-tuple-element.217.refs_1_, bf16[256,1024]{1,0:T(8,128)(2,1)} %copy-done.16, bf16[256,1024]{1,0:T(8,128)(2,1)} %copy-done.18, bf16[8192,1792]{1,0:T(8,128)(2,1)} %refs_4_.15, ...), custom_call_target="tpu_custom_call" | custom-call | flops 3758096384 | bytes 14680064 | tf_op jit(solution)/shard_map/gate_up/pallas_call | solution.py:63
  58.2 1.8 %collective-permute-start.8 = (bf16[272,1024]{1,0:T(8,128)(2,1)S(1)}, bf16[272,1024]{1,0:T(8,128)(2,1)S(1)}, u32[]{:S(2)}, u32[]{:S(2)}) collective-permute-start(bf16[272,1024]{1,0:T(8,128)(2,1)S(1)} %collective-permute-done.4.refs_2_), channel_id=1, source_target_pairs={{0,2},{1,3},{2,4},{3,5},{4,6},{5,7},{6,0},{7,1},{8,10},{9,11},{10,... | collective-permute-start | bytes 1671176 | tf_op jit(solution)/shard_map/ppermute | solution.py:443
  60.1 7.8 %down_back.4 = (f32[256,1792]{1,0:T(8,128)}, f32[8,128]{1,0:T(8,128)S(1)}) custom-call(f32[8,128]{1,0:T(8,128)S(1)} %get-tuple-element.142.refs_0_, s32[2]{0:T(128)S(1)} %get-tuple-element.217.refs_1_, bf16[272,1024]{1,0:T(8,128)(2,1)} %copy-done.8, bf16[272,1024]{1,0:T(8,128)(2,1)} %copy-done.9, bf16[1792,8192]{1,0:T(8,128)(2,1)} %refs_6_.5, ...), custom_call_target="tpu_custom_call" | custom-call | flops 1879048192 | bytes 7340032 | tf_op jit(solution)/shard_map/down_back/pallas_call | solution.py:63
  69.9 1.6 collective-permute-start.13
  71.5 7.4 %gate_up.6 = (f32[256,1792]{1,0:T(8,128)}, f32[256,1792]{1,0:T(8,128)}, f32[8,128]{1,0:T(8,128)S(1)}) custom-call(f32[8,128]{1,0:T(8,128)S(1)} %get-tuple-element.151.refs_0_, s32[1]{0:T(128)} %bitcast.7.refs_1_, bf16[256,1024]{1,0:T(8,128)(2,1)} %collective-permute-done.9.refs_2_, bf16[8192,1792]{1,0:T(8,128)(2,1)} %refs_4_.15, ...), custom_call_target="tpu_custom_call" | custom-call | flops 1879048192 | bytes 7340032 | tf_op jit(solution)/shard_map/gate_up/pallas_call | solution.py:63
  79.8 1.5 collective-permute-start.14
  81.4 11.9 %gate_up.7 = (f32[256,1792]{1,0:T(8,128)}, f32[256,1792]{1,0:T(8,128)}, bf16[256,1792]{1,0:T(8,128)(2,1)}, f32[2,128,64]{2,1,0:T(8,128)S(1)}, f32[8,128]{1,0:T(8,128)S(1)}) custom-call(f32[8,128]{1,0:T(8,128)S(1)} %get-tuple-element.159.refs_0_, s32[2]{0:T(128)S(1)} %get-tuple-element.219.refs_1_, s32[2]{0:T(128)S(1)} %copy-done.5, ...), custom_call_target="tpu_custom_call" | custom-call | flops 3758096384 | bytes 14680064 | tf_op jit(solution)/shard_map/gate_up/pallas_call | solution.py:63
  93.3 1.6 collective-permute-start.12
  96.7 9.6 %down_back.5 = (bf16[256,1792]{1,0:T(8,128)(2,1)S(1)}, bf16[256,1792]{1,0:T(8,128)(2,1)S(1)}, f32[8,128]{1,0:T(8,128)S(1)}) custom-call(f32[8,128]{1,0:T(8,128)S(1)} %get-tuple-element.168.refs_0_, s32[3]{0:T(128)S(1)} %pad_add_fusion.3.refs_1_, s32[2]{0:T(128)S(1)} %copy-done.5, bf16[272,1024]{1,0:T(8,128)(2,1)} %copy-done.12, ...), custom_call_target="tpu_custom_call" | custom-call | flops 2818572288 | bytes 11010048 | tf_op jit(solution)/shard_map/down_back/pallas_call | solution.py:63
  106.3 4.7 %input_parts.5 = (bf16[256,1024]{1,0:T(8,128)(2,1)S(1)}, f32[8,128]{1,0:T(8,128)S(1)}) custom-call(f32[8,128]{1,0:T(8,128)S(1)} %get-tuple-element.175.refs_0_, s32[1]{0:T(128)} %bitcast.6.refs_1_, bf16[256,1792]{1,0:T(8,128)(2,1)S(1)} %get-tuple-element.176.refs_2_, bf16[256,1792]{1,0:T(8,128)(2,1)S(1)} %get-tuple-element.177.refs_3_, ...), custom_call_target="tpu_custom_call" | custom-call | flops 1879048192 | bytes 7340032 | tf_op jit(solution)/shard_map/input_parts/pallas_call | solution.py:63
  111.8 1.2 collective-permute-start.16
  113.0 8.1 %input_parts.6 = (bf16[256,1024]{1,0:T(8,128)(2,1)S(1)}, bf16[256,1024]{1,0:T(8,128)(2,1)S(1)}, f32[8,128]{1,0:T(8,128)S(1)}) custom-call(f32[8,128]{1,0:T(8,128)S(1)} %get-tuple-element.183.refs_0_, s32[2]{0:T(128)S(1)} %get-tuple-element.220.refs_1_, bf16[256,1792]{1,0:T(8,128)(2,1)S(1)} %get-tuple-element.176.refs_2_, ...), custom_call_target="tpu_custom_call" | custom-call | flops 3758096384 | bytes 14680064 | tf_op jit(solution)/shard_map/input_parts/pallas_call | solution.py:63
  121.1 1.8 %collective-permute-start.18 = (bf16[256,1024]{1,0:T(8,128)(2,1)S(1)}, bf16[256,1024]{1,0:T(8,128)(2,1)}, u32[]{:S(2)}, u32[]{:S(2)}) collective-permute-start(bf16[256,1024]{1,0:T(8,128)(2,1)S(1)} %get-tuple-element.188), channel_id=1, source_target_pairs={{0,1},{1,0},{2,3},{3,2},{4,5},{5,4},{6,7},{7,6},{8,9},{9,8},{10,11... | collective-permute-start | bytes 1572872 | tf_op jit(solution)/shard_map/ppermute | solution.py:446
  126.8 8.0 %input_parts.7 = (bf16[256,1024]{1,0:T(8,128)(2,1)S(1)}, bf16[256,1024]{1,0:T(8,128)(2,1)S(1)}, f32[8,128]{1,0:T(8,128)S(1)}) custom-call(f32[8,128]{1,0:T(8,128)S(1)} %get-tuple-element.191.refs_0_, s32[2]{0:T(128)S(1)} %get-tuple-element.218.refs_1_, bf16[256,1792]{1,0:T(8,128)(2,1)S(1)} %get-tuple-element.176.refs_2_, ...), custom_call_target="tpu_custom_call" | custom-call | flops 3758096384 | bytes 14680064 | tf_op jit(solution)/shard_map/input_parts/pallas_call | solution.py:63
  135.8 2.5 %collective-permute-done.19 = f32[2,128,64]{2,1,0:T(8,128)S(1)} collective-permute-done((f32[2,128,64]{2,1,0:T(8,128)S(1)}, f32[2,128,64]{2,1,0:T(8,128)S(1)}, u32[]{:S(2)}, u32[]{:S(2)}) %collective-permute-start.19) | collective-permute-done | bytes 65568 | tf_op jit(solution)/shard_map/ppermute | solution.py:446
  138.2 1.5 add_convert_fusion.2
  142.2 8.1 %input_parts.8 = (bf16[256,1024]{1,0:T(8,128)(2,1)S(1)}, bf16[256,1024]{1,0:T(8,128)(2,1)S(1)}, f32[8,128]{1,0:T(8,128)S(1)}) custom-call(f32[8,128]{1,0:T(8,128)S(1)} %get-tuple-element.204._.refs_0_, s32[2]{0:T(128)S(1)} %pad_add_fusion.5.refs_1_, bf16[256,1792]{1,0:T(8,128)(2,1)S(1)} %get-tuple-element.176.refs_2_, ...), custom_call_target="tpu_custom_call" | custom-call | flops 3758096384 | bytes 14680064 | tf_op jit(solution)/shard_map/input_parts/pallas_call | solution.py:63
  151.3 4.7 %input_parts.9 = (bf16[256,1024]{1,0:T(8,128)(2,1)S(1)}, f32[8,128]{1,0:T(8,128)S(1)}) custom-call(f32[8,128]{1,0:T(8,128)S(1)} %get-tuple-element.210.refs_0_, s32[1]{0:T(128)} %bitcast.2.refs_1_, bf16[256,1792]{1,0:T(8,128)(2,1)S(1)} %get-tuple-element.176.refs_2_, bf16[256,1792]{1,0:T(8,128)(2,1)S(1)} %get-tuple-element.177.refs_3_, ...), custom_call_target="tpu_custom_call" | custom-call | flops 1879048192 | bytes 7340032 | tf_op jit(solution)/shard_map/input_parts/pallas_call | solution.py:63
  156.1 4.0 %by_tenant.2 = f32[16,64,1792]{2,1,0:T(8,128)} custom-call(f32[8,128]{1,0:T(8,128)S(1)} %get-tuple-element.212._, s32[4]{0:T(128)S(1)} %broadcast_select_fusion.1.labels_ref, f32[4]{0:T(128)S(1)} %broadcast_6_scales_ref.2.scales_ref, bf16[4,64,1792]{2,1,0:T(8,128)(2,1)S(1)} %maximum_select_fusion.parts_ref), custom_call_target="tpu_custom_call" | custom-call | bytes 7340032 | tf_op jit(solution)/shard_map/by_tenant/pallas_call | solution.py:404
  160.3 3.1 %by_tenant.3 = f32[16,64,1024]{2,1,0:T(8,128)} custom-call(f32[8,128]{1,0:T(8,128)S(1)} %get-tuple-element.212._, s32[4]{0:T(128)S(1)} %broadcast_select_fusion.1.labels_ref, f32[4]{0:T(128)S(1)} %gather_fusion.3, bf16[4,64,1024]{2,1,0:T(8,128)(2,1)S(1)} %maximum_select_fusion.1.parts_ref), custom_call_target="tpu_custom_call" | custom-call | bytes 4194304 | tf_op jit(solution)/shard_map/by_tenant/pallas_call | solution.py:404
  164.1 2.2 %collective-permute-done.24 = bf16[256,1024]{1,0:T(8,128)(2,1)S(1)} collective-permute-done((bf16[256,1024]{1,0:T(8,128)(2,1)S(1)}, bf16[256,1024]{1,0:T(8,128)(2,1)S(1)}, u32[]{:S(2)}, u32[]{:S(2)}) %collective-permute-start.24) | collective-permute-done | bytes 524320 | tf_op jit(solution)/shard_map/ppermute | solution.py:443
  (113 shorter events, 20.6 us)
Async XLA Ops:
  0.6 11.0 %copy-start.5 = (s32[2]{0:T(128)S(1)}, s32[2]{0:T(128)}, u32[]{:S(2)}) copy-start(s32[2]{0:T(128)} %refs_2_.5) | copy-start | bytes 28
  0.7 8.8 %copy-start.2 = (bf16[256,1024]{1,0:T(8,128)(2,1)S(1)}, bf16[256,1024]{1,0:T(8,128)(2,1)}, u32[]{:S(2)}) copy-start(bf16[256,1024]{1,0:T(8,128)(2,1)} %r.1) | copy-start | bytes 1572868
  0.7 18.2 %collective-permute-start.2 = (bf16[256,1024]{1,0:T(8,128)(2,1)}, bf16[256,1024]{1,0:T(8,128)(2,1)}, u32[]{:S(2)}, u32[]{:S(2)}) collective-permute-start(bf16[256,1024]{1,0:T(8,128)(2,1)} %refs_2_.3), channel_id=1, source_target_pairs={{0,2},{1,3},{2,4},{3,5},{4,6},{5,7},{6,0},{7,1},{8,10},{9,11},{10,... | collective-permute-start | bytes 1572872 | tf_op jit(solution)/shard_map/ppermute | solution.py:443
  3.7 15.2 %collective-permute-start.3 = (bf16[256,1024]{1,0:T(8,128)(2,1)}, bf16[256,1024]{1,0:T(8,128)(2,1)}, u32[]{:S(2)}, u32[]{:S(2)}) collective-permute-start(bf16[256,1024]{1,0:T(8,128)(2,1)} %refs_2_.3), channel_id=1, source_target_pairs={{0,1},{1,0},{2,3},{3,2},{4,5},{5,4},{6,7},{7,6},{8,9},{9,8},{10,11... | collective-permute-start | bytes 1572872 | tf_op jit(solution)/shard_map/ppermute | solution.py:446
  9.5 25.0 %copy-start.7 = (bf16[272,1024]{1,0:T(8,128)(2,1)}, bf16[272,1024]{1,0:T(8,128)(2,1)S(1)}, u32[]{:S(2)}) copy-start(bf16[272,1024]{1,0:T(8,128)(2,1)S(1)} %constant_dynamic-update-slice_fusion.refs_2_) | copy-start | bytes 1671172
  9.6 25.0 %collective-permute-start = (bf16[272,1024]{1,0:T(8,128)(2,1)S(1)}, bf16[272,1024]{1,0:T(8,128)(2,1)S(1)}, u32[]{:S(2)}, u32[]{:S(2)}) collective-permute-start(bf16[272,1024]{1,0:T(8,128)(2,1)S(1)} %constant_dynamic-update-slice_fusion.refs_2_), channel_id=1, source_target_pairs={{0,2},{1,3},{2,4},{3,5},{4,6},{5,7},{6,0},{7,1},{8,10},{9,11},{10,... | collective-permute-start | bytes 1671176 | tf_op jit(solution)/shard_map/ppermute | solution.py:443
  11.2 23.4 %collective-permute-start.1 = (bf16[272,1024]{1,0:T(8,128)(2,1)S(1)}, bf16[272,1024]{1,0:T(8,128)(2,1)S(1)}, u32[]{:S(2)}, u32[]{:S(2)}) collective-permute-start(bf16[272,1024]{1,0:T(8,128)(2,1)S(1)} %constant_dynamic-update-slice_fusion.refs_2_), channel_id=1, source_target_pairs={{0,1},{1,0},{2,3},{3,2},{4,5},{5,4},{6,7},{7,6},{8,9},{9,8},{10,11... | collective-permute-start | bytes 1671176 | tf_op jit(solution)/shard_map/ppermute | solution.py:446
  11.7 100.0 %collective-permute-start.26 = (s32[2]{0:T(128)S(1)}, s32[2]{0:T(128)S(1)}, u32[]{:S(2)}, u32[]{:S(2)}) collective-permute-start(s32[2]{0:T(128)S(1)} %copy-done.5), channel_id=1, source_target_pairs={{0,8},{8,0},{1,9},{9,1},{2,10},{10,2},{3,11},{11,3},{4,12},{12,4},... | collective-permute-start | bytes 32 | tf_op jit(solution)/shard_map/ppermute | solution.py:449
  18.9 26.7 %collective-permute-start.6 = (bf16[256,1024]{1,0:T(8,128)(2,1)}, bf16[256,1024]{1,0:T(8,128)(2,1)S(1)}, u32[]{:S(2)}, u32[]{:S(2)}) collective-permute-start(bf16[256,1024]{1,0:T(8,128)(2,1)} %collective-permute-done.2.refs_3_), channel_id=1, source_target_pairs={{0,2},{1,3},{2,4},{3,5},{4,6},{5,7},{6,0},{7,1},{8,10},{9,11},{10,... | collective-permute-start | bytes 1572872 | tf_op jit(solution)/shard_map/ppermute | solution.py:443
  20.5 25.1 %collective-permute-start.7 = (bf16[256,1024]{1,0:T(8,128)(2,1)}, bf16[256,1024]{1,0:T(8,128)(2,1)S(1)}, u32[]{:S(2)}, u32[]{:S(2)}) collective-permute-start(bf16[256,1024]{1,0:T(8,128)(2,1)} %collective-permute-done.2.refs_3_), channel_id=1, source_target_pairs={{0,1},{1,0},{2,3},{3,2},{4,5},{5,4},{6,7},{7,6},{8,9},{9,8},{10,11... | collective-permute-start | bytes 1572872 | tf_op jit(solution)/shard_map/ppermute | solution.py:446
  34.6 23.6 %collective-permute-start.4 = (bf16[272,1024]{1,0:T(8,128)(2,1)S(1)}, bf16[272,1024]{1,0:T(8,128)(2,1)S(1)}, u32[]{:S(2)}, u32[]{:S(2)}) collective-permute-start(bf16[272,1024]{1,0:T(8,128)(2,1)S(1)} %collective-permute-done.refs_3_), channel_id=1, source_target_pairs={{0,2},{1,3},{2,4},{3,5},{4,6},{5,7},{6,0},{7,1},{8,10},{9,11},{10,... | collective-permute-start | bytes 1671176 | tf_op jit(solution)/shard_map/ppermute | solution.py:443
  36.2 22.0 %collective-permute-start.5 = (bf16[272,1024]{1,0:T(8,128)(2,1)S(1)}, bf16[272,1024]{1,0:T(8,128)(2,1)S(1)}, u32[]{:S(2)}, u32[]{:S(2)}) collective-permute-start(bf16[272,1024]{1,0:T(8,128)(2,1)S(1)} %collective-permute-done.refs_3_), channel_id=1, source_target_pairs={{0,1},{1,0},{2,3},{3,2},{4,5},{5,4},{6,7},{7,6},{8,9},{9,8},{10,11... | collective-permute-start | bytes 1671176 | tf_op jit(solution)/shard_map/ppermute | solution.py:446
  45.6 22.2 %collective-permute-start.9 = (bf16[256,1024]{1,0:T(8,128)(2,1)S(1)}, bf16[256,1024]{1,0:T(8,128)(2,1)}, u32[]{:S(2)}, u32[]{:S(2)}) collective-permute-start(bf16[256,1024]{1,0:T(8,128)(2,1)S(1)} %collective-permute-done.6.refs_2_), channel_id=1, source_target_pairs={{0,2},{1,3},{2,4},{3,5},{4,6},{5,7},{6,0},{7,1},{8,10},{9,11},{10,... | collective-permute-start | bytes 1572872 | tf_op jit(solution)/shard_map/ppermute | solution.py:443
  46.2 21.7 %collective-permute-start.10 = (bf16[256,1024]{1,0:T(8,128)(2,1)S(1)}, bf16[256,1024]{1,0:T(8,128)(2,1)S(1)}, u32[]{:S(2)}, u32[]{:S(2)}) collective-permute-start(bf16[256,1024]{1,0:T(8,128)(2,1)S(1)} %collective-permute-done.6.refs_2_), channel_id=1, source_target_pairs={{0,1},{1,0},{2,3},{3,2},{4,5},{5,4},{6,7},{7,6},{8,9},{9,8},{10,11... | collective-permute-start | bytes 1572872 | tf_op jit(solution)/shard_map/ppermute | solution.py:446
  58.2 20.7 %collective-permute-start.8 = (bf16[272,1024]{1,0:T(8,128)(2,1)S(1)}, bf16[272,1024]{1,0:T(8,128)(2,1)S(1)}, u32[]{:S(2)}, u32[]{:S(2)}) collective-permute-start(bf16[272,1024]{1,0:T(8,128)(2,1)S(1)} %collective-permute-done.4.refs_2_), channel_id=1, source_target_pairs={{0,2},{1,3},{2,4},{3,5},{4,6},{5,7},{6,0},{7,1},{8,10},{9,11},{10,... | collective-permute-start | bytes 1671176 | tf_op jit(solution)/shard_map/ppermute | solution.py:443
  60.1 8.9 %copy-start.6 = (s32[16]{0:T(128)S(1)}, s32[16]{0:T(128)}, u32[]{:S(2)}) copy-start(s32[16]{0:T(128)} %param.17) | copy-start | bytes 196
  68.7 10.3 %collective-permute-start.11 = (bf16[256,1024]{1,0:T(8,128)(2,1)}, bf16[256,1024]{1,0:T(8,128)(2,1)S(1)}, u32[]{:S(2)}, u32[]{:S(2)}) collective-permute-start(bf16[256,1024]{1,0:T(8,128)(2,1)} %collective-permute-done.9.refs_2_), channel_id=1, source_target_pairs={{0,1},{1,0},{2,3},{3,2},{4,5},{5,4},{6,7},{7,6},{8,9},{9,8},{10,11... | collective-permute-start | bytes 1572872 | tf_op jit(solution)/shard_map/ppermute | solution.py:446
  69.9 25.0 %collective-permute-start.13 = (bf16[272,1024]{1,0:T(8,128)(2,1)}, bf16[272,1024]{1,0:T(8,128)(2,1)S(1)}, u32[]{:S(2)}, u32[]{:S(2)}) collective-permute-start(bf16[272,1024]{1,0:T(8,128)(2,1)} %copy-done.9), channel_id=1, source_target_pairs={{0,2},{1,3},{2,4},{3,5},{4,6},{5,7},{6,0},{7,1},{8,10},{9,11},{10,... | collective-permute-start | bytes 1671176 | tf_op jit(solution)/shard_map/ppermute | solution.py:443
  78.9 16.0 %copy-start.12 = (bf16[272,1024]{1,0:T(8,128)(2,1)}, bf16[272,1024]{1,0:T(8,128)(2,1)S(1)}, u32[]{:S(2)}) copy-start(bf16[272,1024]{1,0:T(8,128)(2,1)S(1)} %collective-permute-done.8.refs_3_) | copy-start | bytes 1671172
  79.8 15.1 %collective-permute-start.14 = (bf16[272,1024]{1,0:T(8,128)(2,1)S(1)}, bf16[272,1024]{1,0:T(8,128)(2,1)S(1)}, u32[]{:S(2)}, u32[]{:S(2)}) collective-permute-start(bf16[272,1024]{1,0:T(8,128)(2,1)S(1)} %collective-permute-done.8.refs_3_), channel_id=1, source_target_pairs={{0,1},{1,0},{2,3},{3,2},{4,5},{5,4},{6,7},{7,6},{8,9},{9,8},{10,11... | collective-permute-start | bytes 1671176 | tf_op jit(solution)/shard_map/ppermute | solution.py:446
  93.3 13.0 %collective-permute-start.12 = (f32[2,128,64]{2,1,0:T(8,128)S(1)}, f32[2,128,64]{2,1,0:T(8,128)S(1)}, u32[]{:S(2)}, u32[]{:S(2)}) collective-permute-start(f32[2,128,64]{2,1,0:T(8,128)S(1)} %broadcast_multiply_fusion), channel_id=1, source_target_pairs={{0,2},{1,3},{2,0},{3,1},{4,6},{5,7},{6,4},{7,5},{8,10},{9,11},{10,... | collective-permute-start | bytes 196616 | tf_op jit(solution)/shard_map/ppermute | solution.py:446
  111.0 11.9 %collective-permute-start.15 = (bf16[256,1024]{1,0:T(8,128)(2,1)S(1)}, bf16[256,1024]{1,0:T(8,128)(2,1)S(1)}, u32[]{:S(2)}, u32[]{:S(2)}) collective-permute-start(bf16[256,1024]{1,0:T(8,128)(2,1)S(1)} %get-tuple-element.178), channel_id=1, source_target_pairs={{0,1},{1,0},{2,3},{3,2},{4,5},{5,4},{6,7},{7,6},{8,9},{9,8},{10,11... | collective-permute-start | bytes 1572872 | tf_op jit(solution)/shard_map/ppermute | solution.py:446
  111.8 11.1 %collective-permute-start.16 = (f32[2,128,64]{2,1,0:T(8,128)S(1)}, f32[2,128,64]{2,1,0:T(8,128)S(1)}, u32[]{:S(2)}, u32[]{:S(2)}) collective-permute-start(f32[2,128,64]{2,1,0:T(8,128)S(1)} %add.245), channel_id=1, source_target_pairs={{0,4},{1,5},{2,6},{3,7},{4,0},{5,1},{6,2},{7,3},{8,12},{9,13},{10,... | collective-permute-start | bytes 196616 | tf_op jit(solution)/shard_map/ppermute | solution.py:446
  121.1 17.2 %collective-permute-start.18 = (bf16[256,1024]{1,0:T(8,128)(2,1)S(1)}, bf16[256,1024]{1,0:T(8,128)(2,1)}, u32[]{:S(2)}, u32[]{:S(2)}) collective-permute-start(bf16[256,1024]{1,0:T(8,128)(2,1)S(1)} %get-tuple-element.188), channel_id=1, source_target_pairs={{0,1},{1,0},{2,3},{3,2},{4,5},{5,4},{6,7},{7,6},{8,9},{9,8},{10,11... | collective-permute-start | bytes 1572872 | tf_op jit(solution)/shard_map/ppermute | solution.py:446
  123.8 14.4 %collective-permute-start.17 = (bf16[256,1024]{1,0:T(8,128)(2,1)}, bf16[256,1024]{1,0:T(8,128)(2,1)}, u32[]{:S(2)}, u32[]{:S(2)}) collective-permute-start(bf16[256,1024]{1,0:T(8,128)(2,1)} %add_convert_fusion.3), channel_id=1, source_target_pairs={{0,2},{1,3},{2,4},{3,5},{4,6},{5,7},{6,0},{7,1},{8,10},{9,11},{10,... | collective-permute-start | bytes 1572872 | tf_op jit(solution)/shard_map/ppermute | solution.py:443
  125.5 12.7 %collective-permute-start.19 = (f32[2,128,64]{2,1,0:T(8,128)S(1)}, f32[2,128,64]{2,1,0:T(8,128)S(1)}, u32[]{:S(2)}, u32[]{:S(2)}) collective-permute-start(f32[2,128,64]{2,1,0:T(8,128)S(1)} %add.247), channel_id=1, source_target_pairs={{0,1},{1,0},{2,3},{3,2},{4,5},{5,4},{6,7},{7,6},{8,9},{9,8},{10,11... | collective-permute-start | bytes 196616 | tf_op jit(solution)/shard_map/ppermute | solution.py:446
  134.8 15.7 %collective-permute-start.21 = (bf16[256,1024]{1,0:T(8,128)(2,1)S(1)}, bf16[256,1024]{1,0:T(8,128)(2,1)S(1)}, u32[]{:S(2)}, u32[]{:S(2)}) collective-permute-start(bf16[256,1024]{1,0:T(8,128)(2,1)S(1)} %get-tuple-element.196), channel_id=1, source_target_pairs={{0,1},{1,0},{2,3},{3,2},{4,5},{5,4},{6,7},{7,6},{8,9},{9,8},{10,11... | collective-permute-start | bytes 1572872 | tf_op jit(solution)/shard_map/ppermute | solution.py:446
  139.7 11.2 %collective-permute-start.20 = (bf16[256,1024]{1,0:T(8,128)(2,1)S(1)}, bf16[256,1024]{1,0:T(8,128)(2,1)S(1)}, u32[]{:S(2)}, u32[]{:S(2)}) collective-permute-start(bf16[256,1024]{1,0:T(8,128)(2,1)S(1)} %add_convert_fusion.2), channel_id=1, source_target_pairs={{0,2},{1,3},{2,4},{3,5},{4,6},{5,7},{6,0},{7,1},{8,10},{9,11},{10,... | collective-permute-start | bytes 1572872 | tf_op jit(solution)/shard_map/ppermute | solution.py:443
  141.0 9.5 %collective-permute-start.22 = (bf16[2,64,1792]{2,1,0:T(8,128)(2,1)S(1)}, bf16[2,64,1792]{2,1,0:T(8,128)(2,1)S(1)}, u32[]{:S(2)}, u32[]{:S(2)}) collective-permute-start(bf16[2,64,1792]{2,1,0:T(8,128)(2,1)S(1)} %block_products.2), channel_id=1, source_target_pairs={{0,8},{8,0},{1,9},{9,1},{2,10},{10,2},{3,11},{11,3},{4,12},{12,4},... | collective-permute-start | bytes 1376264 | tf_op jit(solution)/shard_map/ppermute | solution.py:449
  141.6 8.9 %collective-permute-start.23 = (bf16[2,64,1024]{2,1,0:T(8,128)(2,1)S(1)}, bf16[2,64,1024]{2,1,0:T(8,128)(2,1)S(1)}, u32[]{:S(2)}, u32[]{:S(2)}) collective-permute-start(bf16[2,64,1024]{2,1,0:T(8,128)(2,1)S(1)} %block_products.3), channel_id=1, source_target_pairs={{0,8},{8,0},{1,9},{9,1},{2,10},{10,2},{3,11},{11,3},{4,12},{12,4},... | collective-permute-start | bytes 786440 | tf_op jit(solution)/shard_map/ppermute | solution.py:449
  150.2 13.9 %collective-permute-start.25 = (bf16[256,1024]{1,0:T(8,128)(2,1)S(1)}, bf16[256,1024]{1,0:T(8,128)(2,1)S(1)}, u32[]{:S(2)}, u32[]{:S(2)}) collective-permute-start(bf16[256,1024]{1,0:T(8,128)(2,1)S(1)} %get-tuple-element.209), channel_id=1, source_target_pairs={{0,1},{1,0},{2,3},{3,2},{4,5},{5,4},{6,7},{7,6},{8,9},{9,8},{10,11... | collective-permute-start | bytes 1572872 | tf_op jit(solution)/shard_map/ppermute | solution.py:446
  151.2 15.1 %collective-permute-start.24 = (bf16[256,1024]{1,0:T(8,128)(2,1)S(1)}, bf16[256,1024]{1,0:T(8,128)(2,1)S(1)}, u32[]{:S(2)}, u32[]{:S(2)}) collective-permute-start(bf16[256,1024]{1,0:T(8,128)(2,1)S(1)} %add_convert_fusion.1), channel_id=1, source_target_pairs={{0,2},{1,3},{2,4},{3,5},{4,6},{5,7},{6,0},{7,1},{8,10},{9,11},{10,... | collective-permute-start | bytes 1572872 | tf_op jit(solution)/shard_map/ppermute | solution.py:443
  (14 other events, 40.7 us)

commit v4 on v3

--- a/solution.py
+++ b/solution.py
@@ -550,7 +550,7 @@
     own0, out1 = parts((1, 0), (2, 1))
     low, got_low = passed(low, got_low)
     low = low + got_low
-    got_low = swap(low)
+    got_low = swap(low.astype(bf16))
     got1 = swap(out1)
     (got0,) = passed(got0)
     ring0 = ring_on(add(got0, own0))

time: 168 us -> 166 us (0.988)
    ppermute x10, waiting for transfers between devices: 9.62 us -> 12.7 us  [ring_on(): lax.ppermute(value, 'tensor', [(i, (i + PAIR) % devices) for i in range(d...]
    ppermute x14, waiting for transfers between devices: 3.3 us -> 0.22 us  [swap(): return lax.ppermute(value, 'tensor', [(i, i ^ bit) for i in range(devices)])]
  transfers between devices with their start and end apart: 27 -> 27, of which waited for: 6 -> 6; matrix products, arithmetic and copies ran while one was open for 7% -> 6% of each run, Pallas kernels for 66% -> 64%
where the time goes in v4:
time: 166 us
  Pallas kernels  111 us (67%)
  starting transfers between devices  28.4 us (17%)
  waiting for transfers between devices  12.9 us (8%)
  local copies, waits for them, and re-layouts  6.88 us (4%)
  other arithmetic  5.46 us (3%)
    pallas_call x12, Pallas kernels, call(): pl.pallas_call(marked, in_specs=[ANYWHERE] + [SCALARS] * len(scalars) + [...  102 us
    ppermute x14, starting transfers between devices, swap(): return lax.ppermute(value, 'tensor', [(i, i ^ bit) for i in range(devices)])  15.1 us
    ppermute x10, waiting for transfers between devices, ring_on(): lax.ppermute(value, 'tensor', [(i, (i + PAIR) % devices) for i in range(d...  12.7 us
    ppermute x10, starting transfers between devices, ring_on(): lax.ppermute(value, 'tensor', [(i, (i + PAIR) % devices) for i in range(d...  12.7 us
    pallas_call x2, Pallas kernels, by_tenant(): pl.pallas_call(body, grid=(tenants // at_once,), in_specs=[ANYWHERE, SCAL...  7.29 us
  transfers between devices with their start and end apart: 27, of which 6 were waited for; matrix products, arithmetic and copies ran while one was open for 6% of the time, Pallas kernels for 64%

profile of v4, /device:TPU:0, one launch (start us, length us, event | category | flops | bytes accessed | tf_op | source)
XLA Modules:
  0.0 165.7 jit_solution(11199157584661904079)
XLA Ops:
  0.7 3.1 %collective-permute-start.2 = (bf16[256,1024]{1,0:T(8,128)(2,1)}, bf16[256,1024]{1,0:T(8,128)(2,1)}, u32[]{:S(2)}, u32[]{:S(2)}) collective-permute-start(bf16[256,1024]{1,0:T(8,128)(2,1)} %refs_2_.3), channel_id=1, source_target_pairs={{0,2},{1,3},{2,4},{3,5},{4,6},{5,7},{6,0},{7,1},{8,10},{9,11},{10,... | collective-permute-start | bytes 1572872 | tf_op jit(solution)/shard_map/ppermute | solution.py:443
  3.8 1.5 collective-permute-start.3
  8.9 1.6 collective-permute-start
  11.2 7.7 %collective-permute-done.2.refs_3_ = bf16[256,1024]{1,0:T(8,128)(2,1)} collective-permute-done((bf16[256,1024]{1,0:T(8,128)(2,1)}, bf16[256,1024]{1,0:T(8,128)(2,1)}, u32[]{:S(2)}, u32[]{:S(2)}) %collective-permute-start.2) | collective-permute-done | bytes 524320 | tf_op jit(solution)/shard_map/ppermute | solution.py:443
  18.9 1.6 collective-permute-start.6
  20.5 1.5 collective-permute-start.7
  22.0 12.5 %gate_up.4 = (f32[256,1792]{1,0:T(8,128)}, f32[256,1792]{1,0:T(8,128)}, f32[8,128]{1,0:T(8,128)S(1)}) custom-call(f32[8,128]{1,0:T(8,128)S(1)} %broadcast_in_dim.14.refs_0_, s32[3]{0:T(128)S(1)} %pad_add_fusion.refs_1_, bf16[256,1024]{1,0:T(8,128)(2,1)} %refs_2_.3, bf16[256,1024]{1,0:T(8,128)(2,1)} %collective-permute-done.2.refs_3_, ...), custom_call_target="tpu_custom_call" | custom-call | flops 5637144576 | bytes 22020096 | tf_op jit(solution)/shard_map/gate_up/pallas_call | solution.py:63
  35.5 1.6 collective-permute-start.4
  37.6 8.9 %down_back.3 = (f32[256,1792]{1,0:T(8,128)}, f32[8,128]{1,0:T(8,128)S(1)}) custom-call(f32[8,128]{1,0:T(8,128)S(1)} %get-tuple-element.125.refs_0_, s32[3]{0:T(128)S(1)} %pad_add_fusion.refs_1_, bf16[272,1024]{1,0:T(8,128)(2,1)} %copy-done.7, bf16[272,1024]{1,0:T(8,128)(2,1)} %copy-done.10, bf16[272,1024]{1,0:T(8,128)(2,1)} %copy-done.11, ...), custom_call_target="tpu_custom_call" | custom-call | flops 2818572288 | bytes 11010048 | tf_op jit(solution)/shard_map/down_back/pallas_call | solution.py:63
  46.8 1.5 collective-permute-start.10
  48.2 10.8 %gate_up.5 = (f32[256,1792]{1,0:T(8,128)}, f32[256,1792]{1,0:T(8,128)}, f32[8,128]{1,0:T(8,128)S(1)}) custom-call(f32[8,128]{1,0:T(8,128)S(1)} %get-tuple-element.132.refs_0_, s32[2]{0:T(128)S(1)} %get-tuple-element.219.refs_1_, bf16[256,1024]{1,0:T(8,128)(2,1)} %copy-done.16, bf16[256,1024]{1,0:T(8,128)(2,1)} %copy-done.18, bf16[8192,1792]{1,0:T(8,128)(2,1)} %refs_4_.15, ...), custom_call_target="tpu_custom_call" | custom-call | flops 3758096384 | bytes 14680064 | tf_op jit(solution)/shard_map/gate_up/pallas_call | solution.py:63
  59.1 1.8 %collective-permute-start.8 = (bf16[272,1024]{1,0:T(8,128)(2,1)S(1)}, bf16[272,1024]{1,0:T(8,128)(2,1)S(1)}, u32[]{:S(2)}, u32[]{:S(2)}) collective-permute-start(bf16[272,1024]{1,0:T(8,128)(2,1)S(1)} %collective-permute-done.4.refs_2_), channel_id=1, source_target_pairs={{0,2},{1,3},{2,4},{3,5},{4,6},{5,7},{6,0},{7,1},{8,10},{9,11},{10,... | collective-permute-start | bytes 1671176 | tf_op jit(solution)/shard_map/ppermute | solution.py:443
  60.9 7.8 %down_back.4 = (f32[256,1792]{1,0:T(8,128)}, f32[8,128]{1,0:T(8,128)S(1)}) custom-call(f32[8,128]{1,0:T(8,128)S(1)} %get-tuple-element.142.refs_0_, s32[2]{0:T(128)S(1)} %get-tuple-element.219.refs_1_, bf16[272,1024]{1,0:T(8,128)(2,1)} %copy-done.8, bf16[272,1024]{1,0:T(8,128)(2,1)} %copy-done.9, bf16[1792,8192]{1,0:T(8,128)(2,1)} %refs_6_.5, ...), custom_call_target="tpu_custom_call" | custom-call | flops 1879048192 | bytes 7340032 | tf_op jit(solution)/shard_map/down_back/pallas_call | solution.py:63
  70.6 1.4 collective-permute-start.13
  72.0 7.4 %gate_up.6 = (f32[256,1792]{1,0:T(8,128)}, f32[256,1792]{1,0:T(8,128)}, f32[8,128]{1,0:T(8,128)S(1)}) custom-call(f32[8,128]{1,0:T(8,128)S(1)} %get-tuple-element.151.refs_0_, s32[1]{0:T(128)} %bitcast.7.refs_1_, bf16[256,1024]{1,0:T(8,128)(2,1)} %collective-permute-done.9.refs_2_, bf16[8192,1792]{1,0:T(8,128)(2,1)} %refs_4_.15, ...), custom_call_target="tpu_custom_call" | custom-call | flops 1879048192 | bytes 7340032 | tf_op jit(solution)/shard_map/gate_up/pallas_call | solution.py:63
  80.3 1.3 collective-permute-start.14
  81.6 11.9 %gate_up.7 = (f32[256,1792]{1,0:T(8,128)}, f32[256,1792]{1,0:T(8,128)}, bf16[256,1792]{1,0:T(8,128)(2,1)}, f32[2,128,64]{2,1,0:T(8,128)S(1)}, f32[8,128]{1,0:T(8,128)S(1)}) custom-call(f32[8,128]{1,0:T(8,128)S(1)} %get-tuple-element.159.refs_0_, s32[2]{0:T(128)S(1)} %get-tuple-element.221.refs_1_, s32[2]{0:T(128)S(1)} %copy-done.5, ...), custom_call_target="tpu_custom_call" | custom-call | flops 3758096384 | bytes 14680064 | tf_op jit(solution)/shard_map/gate_up/pallas_call | solution.py:63
  93.5 1.6 collective-permute-start.12
  96.9 9.6 %down_back.5 = (bf16[256,1792]{1,0:T(8,128)(2,1)S(1)}, bf16[256,1792]{1,0:T(8,128)(2,1)S(1)}, f32[8,128]{1,0:T(8,128)S(1)}) custom-call(f32[8,128]{1,0:T(8,128)S(1)} %get-tuple-element.168.refs_0_, s32[3]{0:T(128)S(1)} %pad_add_fusion.3.refs_1_, s32[2]{0:T(128)S(1)} %copy-done.5, bf16[272,1024]{1,0:T(8,128)(2,1)} %copy-done.12, ...), custom_call_target="tpu_custom_call" | custom-call | flops 2818572288 | bytes 11010048 | tf_op jit(solution)/shard_map/down_back/pallas_call | solution.py:63
  106.5 4.7 %input_parts.5 = (bf16[256,1024]{1,0:T(8,128)(2,1)S(1)}, f32[8,128]{1,0:T(8,128)S(1)}) custom-call(f32[8,128]{1,0:T(8,128)S(1)} %get-tuple-element.175.refs_0_, s32[1]{0:T(128)} %bitcast.6.refs_1_, bf16[256,1792]{1,0:T(8,128)(2,1)S(1)} %get-tuple-element.176.refs_2_, bf16[256,1792]{1,0:T(8,128)(2,1)S(1)} %get-tuple-element.177.refs_3_, ...), custom_call_target="tpu_custom_call" | custom-call | flops 1879048192 | bytes 7340032 | tf_op jit(solution)/shard_map/input_parts/pallas_call | solution.py:63
  112.7 1.5 collective-permute-start.16
  114.2 8.0 %input_parts.6 = (bf16[256,1024]{1,0:T(8,128)(2,1)S(1)}, bf16[256,1024]{1,0:T(8,128)(2,1)S(1)}, f32[8,128]{1,0:T(8,128)S(1)}) custom-call(f32[8,128]{1,0:T(8,128)S(1)} %get-tuple-element.183.refs_0_, s32[2]{0:T(128)S(1)} %get-tuple-element.222.refs_1_, bf16[256,1792]{1,0:T(8,128)(2,1)S(1)} %get-tuple-element.176.refs_2_, ...), custom_call_target="tpu_custom_call" | custom-call | flops 3758096384 | bytes 14680064 | tf_op jit(solution)/shard_map/input_parts/pallas_call | solution.py:63
  122.3 1.4 collective-permute-start.18
  123.7 1.2 add_convert_fusion.3
  126.8 8.1 %input_parts.7 = (bf16[256,1024]{1,0:T(8,128)(2,1)S(1)}, bf16[256,1024]{1,0:T(8,128)(2,1)S(1)}, f32[8,128]{1,0:T(8,128)S(1)}) custom-call(f32[8,128]{1,0:T(8,128)S(1)} %get-tuple-element.191.refs_0_, s32[2]{0:T(128)S(1)} %get-tuple-element.220.refs_1_, bf16[256,1792]{1,0:T(8,128)(2,1)S(1)} %get-tuple-element.176.refs_2_, ...), custom_call_target="tpu_custom_call" | custom-call | flops 3758096384 | bytes 14680064 | tf_op jit(solution)/shard_map/input_parts/pallas_call | solution.py:63
  134.9 1.4 collective-permute-start.21
  136.3 1.8 %collective-permute-done.17 = bf16[256,1024]{1,0:T(8,128)(2,1)S(1)} collective-permute-done((bf16[256,1024]{1,0:T(8,128)(2,1)S(1)}, bf16[256,1024]{1,0:T(8,128)(2,1)S(1)}, u32[]{:S(2)}, u32[]{:S(2)}) %collective-permute-start.17) | collective-permute-done | bytes 524320 | tf_op jit(solution)/shard_map/ppermute | solution.py:443
  140.2 8.1 %input_parts.8 = (bf16[256,1024]{1,0:T(8,128)(2,1)S(1)}, bf16[256,1024]{1,0:T(8,128)(2,1)S(1)}, f32[8,128]{1,0:T(8,128)S(1)}) custom-call(f32[8,128]{1,0:T(8,128)S(1)} %get-tuple-element.204._.refs_0_, s32[2]{0:T(128)S(1)} %pad_add_fusion.5.refs_1_, bf16[256,1792]{1,0:T(8,128)(2,1)S(1)} %get-tuple-element.176.refs_2_, ...), custom_call_target="tpu_custom_call" | custom-call | flops 3758096384 | bytes 14680064 | tf_op jit(solution)/shard_map/input_parts/pallas_call | solution.py:63
  149.9 4.7 %input_parts.9 = (bf16[256,1024]{1,0:T(8,128)(2,1)S(1)}, f32[8,128]{1,0:T(8,128)S(1)}) custom-call(f32[8,128]{1,0:T(8,128)S(1)} %get-tuple-element.210.refs_0_, s32[1]{0:T(128)} %bitcast.2.refs_1_, bf16[256,1792]{1,0:T(8,128)(2,1)S(1)} %get-tuple-element.176.refs_2_, bf16[256,1792]{1,0:T(8,128)(2,1)S(1)} %get-tuple-element.177.refs_3_, ...), custom_call_target="tpu_custom_call" | custom-call | flops 1879048192 | bytes 7340032 | tf_op jit(solution)/shard_map/input_parts/pallas_call | solution.py:63
  154.7 4.1 %by_tenant.2 = f32[16,64,1792]{2,1,0:T(8,128)} custom-call(f32[8,128]{1,0:T(8,128)S(1)} %get-tuple-element.212._, s32[4]{0:T(128)S(1)} %broadcast_select_fusion.1.labels_ref, f32[4]{0:T(128)S(1)} %broadcast_6_scales_ref.2.scales_ref, bf16[4,64,1792]{2,1,0:T(8,128)(2,1)S(1)} %maximum_select_fusion.parts_ref), custom_call_target="tpu_custom_call" | custom-call | bytes 7340032 | tf_op jit(solution)/shard_map/by_tenant/pallas_call | solution.py:404
  158.9 3.2 %by_tenant.3 = f32[16,64,1024]{2,1,0:T(8,128)} custom-call(f32[8,128]{1,0:T(8,128)S(1)} %get-tuple-element.212._, s32[4]{0:T(128)S(1)} %broadcast_select_fusion.1.labels_ref, f32[4]{0:T(128)S(1)} %gather_fusion.3, bf16[4,64,1024]{2,1,0:T(8,128)(2,1)S(1)} %maximum_select_fusion.1.parts_ref), custom_call_target="tpu_custom_call" | custom-call | bytes 4194304 | tf_op jit(solution)/shard_map/by_tenant/pallas_call | solution.py:404
  162.2 2.4 %collective-permute-done.24 = bf16[256,1024]{1,0:T(8,128)(2,1)S(1)} collective-permute-done((bf16[256,1024]{1,0:T(8,128)(2,1)S(1)}, bf16[256,1024]{1,0:T(8,128)(2,1)S(1)}, u32[]{:S(2)}, u32[]{:S(2)}) %collective-permute-start.24) | collective-permute-done | bytes 524320 | tf_op jit(solution)/shard_map/ppermute | solution.py:443
  (113 shorter events, 19.1 us)
Async XLA Ops:
  0.6 7.7 %copy-start.2 = (bf16[256,1024]{1,0:T(8,128)(2,1)S(1)}, bf16[256,1024]{1,0:T(8,128)(2,1)}, u32[]{:S(2)}) copy-start(bf16[256,1024]{1,0:T(8,128)(2,1)} %r.1) | copy-start | bytes 1572868
  0.7 10.4 %copy-start.5 = (s32[2]{0:T(128)S(1)}, s32[2]{0:T(128)}, u32[]{:S(2)}) copy-start(s32[2]{0:T(128)} %refs_2_.5) | copy-start | bytes 28
  0.7 6.9 %copy-start.6 = (s32[16]{0:T(128)S(1)}, s32[16]{0:T(128)}, u32[]{:S(2)}) copy-start(s32[16]{0:T(128)} %param.17) | copy-start | bytes 196
  0.7 18.2 %collective-permute-start.2 = (bf16[256,1024]{1,0:T(8,128)(2,1)}, bf16[256,1024]{1,0:T(8,128)(2,1)}, u32[]{:S(2)}, u32[]{:S(2)}) collective-permute-start(bf16[256,1024]{1,0:T(8,128)(2,1)} %refs_2_.3), channel_id=1, source_target_pairs={{0,2},{1,3},{2,4},{3,5},{4,6},{5,7},{6,0},{7,1},{8,10},{9,11},{10,... | collective-permute-start | bytes 1572872 | tf_op jit(solution)/shard_map/ppermute | solution.py:443
  3.8 15.2 %collective-permute-start.3 = (bf16[256,1024]{1,0:T(8,128)(2,1)}, bf16[256,1024]{1,0:T(8,128)(2,1)}, u32[]{:S(2)}, u32[]{:S(2)}) collective-permute-start(bf16[256,1024]{1,0:T(8,128)(2,1)} %refs_2_.3), channel_id=1, source_target_pairs={{0,1},{1,0},{2,3},{3,2},{4,5},{5,4},{6,7},{7,6},{8,9},{9,8},{10,11... | collective-permute-start | bytes 1572872 | tf_op jit(solution)/shard_map/ppermute | solution.py:446
  8.9 25.7 %copy-start.7 = (bf16[272,1024]{1,0:T(8,128)(2,1)}, bf16[272,1024]{1,0:T(8,128)(2,1)S(1)}, u32[]{:S(2)}) copy-start(bf16[272,1024]{1,0:T(8,128)(2,1)S(1)} %constant_dynamic-update-slice_fusion.refs_2_) | copy-start | bytes 1671172
  8.9 25.7 %collective-permute-start = (bf16[272,1024]{1,0:T(8,128)(2,1)S(1)}, bf16[272,1024]{1,0:T(8,128)(2,1)S(1)}, u32[]{:S(2)}, u32[]{:S(2)}) collective-permute-start(bf16[272,1024]{1,0:T(8,128)(2,1)S(1)} %constant_dynamic-update-slice_fusion.refs_2_), channel_id=1, source_target_pairs={{0,2},{1,3},{2,4},{3,5},{4,6},{5,7},{6,0},{7,1},{8,10},{9,11},{10,... | collective-permute-start | bytes 1671176 | tf_op jit(solution)/shard_map/ppermute | solution.py:443
  10.5 24.0 %collective-permute-start.1 = (bf16[272,1024]{1,0:T(8,128)(2,1)S(1)}, bf16[272,1024]{1,0:T(8,128)(2,1)S(1)}, u32[]{:S(2)}, u32[]{:S(2)}) collective-permute-start(bf16[272,1024]{1,0:T(8,128)(2,1)S(1)} %constant_dynamic-update-slice_fusion.refs_2_), channel_id=1, source_target_pairs={{0,1},{1,0},{2,3},{3,2},{4,5},{5,4},{6,7},{7,6},{8,9},{9,8},{10,11... | collective-permute-start | bytes 1671176 | tf_op jit(solution)/shard_map/ppermute | solution.py:446
  11.0 59.5 %collective-permute-start.26 = (s32[2]{0:T(128)S(1)}, s32[2]{0:T(128)S(1)}, u32[]{:S(2)}, u32[]{:S(2)}) collective-permute-start(s32[2]{0:T(128)S(1)} %copy-done.5), channel_id=1, source_target_pairs={{0,8},{8,0},{1,9},{9,1},{2,10},{10,2},{3,11},{11,3},{4,12},{12,4},... | collective-permute-start | bytes 32 | tf_op jit(solution)/shard_map/ppermute | solution.py:449
  18.9 27.5 %collective-permute-start.6 = (bf16[256,1024]{1,0:T(8,128)(2,1)}, bf16[256,1024]{1,0:T(8,128)(2,1)S(1)}, u32[]{:S(2)}, u32[]{:S(2)}) collective-permute-start(bf16[256,1024]{1,0:T(8,128)(2,1)} %collective-permute-done.2.refs_3_), channel_id=1, source_target_pairs={{0,2},{1,3},{2,4},{3,5},{4,6},{5,7},{6,0},{7,1},{8,10},{9,11},{10,... | collective-permute-start | bytes 1572872 | tf_op jit(solution)/shard_map/ppermute | solution.py:443
  20.5 25.9 %collective-permute-start.7 = (bf16[256,1024]{1,0:T(8,128)(2,1)}, bf16[256,1024]{1,0:T(8,128)(2,1)S(1)}, u32[]{:S(2)}, u32[]{:S(2)}) collective-permute-start(bf16[256,1024]{1,0:T(8,128)(2,1)} %collective-permute-done.2.refs_3_), channel_id=1, source_target_pairs={{0,1},{1,0},{2,3},{3,2},{4,5},{5,4},{6,7},{7,6},{8,9},{9,8},{10,11... | collective-permute-start | bytes 1572872 | tf_op jit(solution)/shard_map/ppermute | solution.py:446
  35.5 23.6 %collective-permute-start.4 = (bf16[272,1024]{1,0:T(8,128)(2,1)S(1)}, bf16[272,1024]{1,0:T(8,128)(2,1)S(1)}, u32[]{:S(2)}, u32[]{:S(2)}) collective-permute-start(bf16[272,1024]{1,0:T(8,128)(2,1)S(1)} %collective-permute-done.refs_3_), channel_id=1, source_target_pairs={{0,2},{1,3},{2,4},{3,5},{4,6},{5,7},{6,0},{7,1},{8,10},{9,11},{10,... | collective-permute-start | bytes 1671176 | tf_op jit(solution)/shard_map/ppermute | solution.py:443
  37.0 22.0 %collective-permute-start.5 = (bf16[272,1024]{1,0:T(8,128)(2,1)S(1)}, bf16[272,1024]{1,0:T(8,128)(2,1)S(1)}, u32[]{:S(2)}, u32[]{:S(2)}) collective-permute-start(bf16[272,1024]{1,0:T(8,128)(2,1)S(1)} %collective-permute-done.refs_3_), channel_id=1, source_target_pairs={{0,1},{1,0},{2,3},{3,2},{4,5},{5,4},{6,7},{7,6},{8,9},{9,8},{10,11... | collective-permute-start | bytes 1671176 | tf_op jit(solution)/shard_map/ppermute | solution.py:446
  46.5 22.2 %collective-permute-start.9 = (bf16[256,1024]{1,0:T(8,128)(2,1)S(1)}, bf16[256,1024]{1,0:T(8,128)(2,1)}, u32[]{:S(2)}, u32[]{:S(2)}) collective-permute-start(bf16[256,1024]{1,0:T(8,128)(2,1)S(1)} %collective-permute-done.6.refs_2_), channel_id=1, source_target_pairs={{0,2},{1,3},{2,4},{3,5},{4,6},{5,7},{6,0},{7,1},{8,10},{9,11},{10,... | collective-permute-start | bytes 1572872 | tf_op jit(solution)/shard_map/ppermute | solution.py:443
  46.8 21.9 %collective-permute-start.10 = (bf16[256,1024]{1,0:T(8,128)(2,1)S(1)}, bf16[256,1024]{1,0:T(8,128)(2,1)S(1)}, u32[]{:S(2)}, u32[]{:S(2)}) collective-permute-start(bf16[256,1024]{1,0:T(8,128)(2,1)S(1)} %collective-permute-done.6.refs_2_), channel_id=1, source_target_pairs={{0,1},{1,0},{2,3},{3,2},{4,5},{5,4},{6,7},{7,6},{8,9},{9,8},{10,11... | collective-permute-start | bytes 1572872 | tf_op jit(solution)/shard_map/ppermute | solution.py:446
  59.1 20.3 %collective-permute-start.8 = (bf16[272,1024]{1,0:T(8,128)(2,1)S(1)}, bf16[272,1024]{1,0:T(8,128)(2,1)S(1)}, u32[]{:S(2)}, u32[]{:S(2)}) collective-permute-start(bf16[272,1024]{1,0:T(8,128)(2,1)S(1)} %collective-permute-done.4.refs_2_), channel_id=1, source_target_pairs={{0,2},{1,3},{2,4},{3,5},{4,6},{5,7},{6,0},{7,1},{8,10},{9,11},{10,... | collective-permute-start | bytes 1671176 | tf_op jit(solution)/shard_map/ppermute | solution.py:443
  68.7 10.7 %collective-permute-start.11 = (bf16[256,1024]{1,0:T(8,128)(2,1)}, bf16[256,1024]{1,0:T(8,128)(2,1)S(1)}, u32[]{:S(2)}, u32[]{:S(2)}) collective-permute-start(bf16[256,1024]{1,0:T(8,128)(2,1)} %collective-permute-done.9.refs_2_), channel_id=1, source_target_pairs={{0,1},{1,0},{2,3},{3,2},{4,5},{5,4},{6,7},{7,6},{8,9},{9,8},{10,11... | collective-permute-start | bytes 1572872 | tf_op jit(solution)/shard_map/ppermute | solution.py:446
  70.6 24.5 %collective-permute-start.13 = (bf16[272,1024]{1,0:T(8,128)(2,1)}, bf16[272,1024]{1,0:T(8,128)(2,1)S(1)}, u32[]{:S(2)}, u32[]{:S(2)}) collective-permute-start(bf16[272,1024]{1,0:T(8,128)(2,1)} %copy-done.9), channel_id=1, source_target_pairs={{0,2},{1,3},{2,4},{3,5},{4,6},{5,7},{6,0},{7,1},{8,10},{9,11},{10,... | collective-permute-start | bytes 1671176 | tf_op jit(solution)/shard_map/ppermute | solution.py:443
  79.4 15.7 %copy-start.12 = (bf16[272,1024]{1,0:T(8,128)(2,1)}, bf16[272,1024]{1,0:T(8,128)(2,1)S(1)}, u32[]{:S(2)}) copy-start(bf16[272,1024]{1,0:T(8,128)(2,1)S(1)} %collective-permute-done.8.refs_3_) | copy-start | bytes 1671172
  80.3 14.9 %collective-permute-start.14 = (bf16[272,1024]{1,0:T(8,128)(2,1)S(1)}, bf16[272,1024]{1,0:T(8,128)(2,1)S(1)}, u32[]{:S(2)}, u32[]{:S(2)}) collective-permute-start(bf16[272,1024]{1,0:T(8,128)(2,1)S(1)} %collective-permute-done.8.refs_3_), channel_id=1, source_target_pairs={{0,1},{1,0},{2,3},{3,2},{4,5},{5,4},{6,7},{7,6},{8,9},{9,8},{10,11... | collective-permute-start | bytes 1671176 | tf_op jit(solution)/shard_map/ppermute | solution.py:446
  93.5 13.1 %collective-permute-start.12 = (f32[2,128,64]{2,1,0:T(8,128)S(1)}, f32[2,128,64]{2,1,0:T(8,128)S(1)}, u32[]{:S(2)}, u32[]{:S(2)}) collective-permute-start(f32[2,128,64]{2,1,0:T(8,128)S(1)} %broadcast_multiply_fusion), channel_id=1, source_target_pairs={{0,2},{1,3},{2,0},{3,1},{4,6},{5,7},{6,4},{7,5},{8,10},{9,11},{10,... | collective-permute-start | bytes 196616 | tf_op jit(solution)/shard_map/ppermute | solution.py:446
  111.2 12.5 %collective-permute-start.15 = (bf16[256,1024]{1,0:T(8,128)(2,1)S(1)}, bf16[256,1024]{1,0:T(8,128)(2,1)}, u32[]{:S(2)}, u32[]{:S(2)}) collective-permute-start(bf16[256,1024]{1,0:T(8,128)(2,1)S(1)} %get-tuple-element.178), channel_id=1, source_target_pairs={{0,1},{1,0},{2,3},{3,2},{4,5},{5,4},{6,7},{7,6},{8,9},{9,8},{10,11... | collective-permute-start | bytes 1572872 | tf_op jit(solution)/shard_map/ppermute | solution.py:446
  112.7 11.0 %collective-permute-start.16 = (f32[2,128,64]{2,1,0:T(8,128)S(1)}, f32[2,128,64]{2,1,0:T(8,128)S(1)}, u32[]{:S(2)}, u32[]{:S(2)}) collective-permute-start(f32[2,128,64]{2,1,0:T(8,128)S(1)} %add.245), channel_id=1, source_target_pairs={{0,4},{1,5},{2,6},{3,7},{4,0},{5,1},{6,2},{7,3},{8,12},{9,13},{10,... | collective-permute-start | bytes 196616 | tf_op jit(solution)/shard_map/ppermute | solution.py:446
  122.3 14.0 %collective-permute-start.18 = (bf16[256,1024]{1,0:T(8,128)(2,1)S(1)}, bf16[256,1024]{1,0:T(8,128)(2,1)S(1)}, u32[]{:S(2)}, u32[]{:S(2)}) collective-permute-start(bf16[256,1024]{1,0:T(8,128)(2,1)S(1)} %get-tuple-element.188), channel_id=1, source_target_pairs={{0,1},{1,0},{2,3},{3,2},{4,5},{5,4},{6,7},{7,6},{8,9},{9,8},{10,11... | collective-permute-start | bytes 1572872 | tf_op jit(solution)/shard_map/ppermute | solution.py:446
  125.0 13.1 %collective-permute-start.17 = (bf16[256,1024]{1,0:T(8,128)(2,1)S(1)}, bf16[256,1024]{1,0:T(8,128)(2,1)S(1)}, u32[]{:S(2)}, u32[]{:S(2)}) collective-permute-start(bf16[256,1024]{1,0:T(8,128)(2,1)S(1)} %add_convert_fusion.3), channel_id=1, source_target_pairs={{0,2},{1,3},{2,4},{3,5},{4,6},{5,7},{6,0},{7,1},{8,10},{9,11},{10,... | collective-permute-start | bytes 1572872 | tf_op jit(solution)/shard_map/ppermute | solution.py:443
  126.0 10.2 %collective-permute-start.19 = (bf16[2,128,64]{2,1,0:T(8,128)(2,1)S(1)}, bf16[2,128,64]{2,1,0:T(8,128)(2,1)S(1)}, u32[]{:S(2)}, u32[]{:S(2)}) collective-permute-start(bf16[2,128,64]{2,1,0:T(8,128)(2,1)S(1)} %get-tuple-element.217), channel_id=1, source_target_pairs={{0,1},{1,0},{2,3},{3,2},{4,5},{5,4},{6,7},{7,6},{8,9},{9,8},{10,11... | collective-permute-start | bytes 98312 | tf_op jit(solution)/shard_map/ppermute | solution.py:446
  134.9 13.8 %collective-permute-start.21 = (bf16[256,1024]{1,0:T(8,128)(2,1)S(1)}, bf16[256,1024]{1,0:T(8,128)(2,1)S(1)}, u32[]{:S(2)}, u32[]{:S(2)}) collective-permute-start(bf16[256,1024]{1,0:T(8,128)(2,1)S(1)} %get-tuple-element.196), channel_id=1, source_target_pairs={{0,1},{1,0},{2,3},{3,2},{4,5},{5,4},{6,7},{7,6},{8,9},{9,8},{10,11... | collective-permute-start | bytes 1572872 | tf_op jit(solution)/shard_map/ppermute | solution.py:446
  138.3 11.2 %collective-permute-start.20 = (bf16[256,1024]{1,0:T(8,128)(2,1)S(1)}, bf16[256,1024]{1,0:T(8,128)(2,1)S(1)}, u32[]{:S(2)}, u32[]{:S(2)}) collective-permute-start(bf16[256,1024]{1,0:T(8,128)(2,1)S(1)} %add_convert_fusion.2), channel_id=1, source_target_pairs={{0,2},{1,3},{2,4},{3,5},{4,6},{5,7},{6,0},{7,1},{8,10},{9,11},{10,... | collective-permute-start | bytes 1572872 | tf_op jit(solution)/shard_map/ppermute | solution.py:443
  139.1 9.6 %collective-permute-start.22 = (bf16[2,64,1792]{2,1,0:T(8,128)(2,1)S(1)}, bf16[2,64,1792]{2,1,0:T(8,128)(2,1)S(1)}, u32[]{:S(2)}, u32[]{:S(2)}) collective-permute-start(bf16[2,64,1792]{2,1,0:T(8,128)(2,1)S(1)} %block_products.2), channel_id=1, source_target_pairs={{0,8},{8,0},{1,9},{9,1},{2,10},{10,2},{3,11},{11,3},{4,12},{12,4},... | collective-permute-start | bytes 1376264 | tf_op jit(solution)/shard_map/ppermute | solution.py:449
  139.7 9.0 %collective-permute-start.23 = (bf16[2,64,1024]{2,1,0:T(8,128)(2,1)S(1)}, bf16[2,64,1024]{2,1,0:T(8,128)(2,1)S(1)}, u32[]{:S(2)}, u32[]{:S(2)}) collective-permute-start(bf16[2,64,1024]{2,1,0:T(8,128)(2,1)S(1)} %block_products.3), channel_id=1, source_target_pairs={{0,8},{8,0},{1,9},{9,1},{2,10},{10,2},{3,11},{11,3},{4,12},{12,4},... | collective-permute-start | bytes 786440 | tf_op jit(solution)/shard_map/ppermute | solution.py:449
  148.3 13.9 %collective-permute-start.25 = (bf16[256,1024]{1,0:T(8,128)(2,1)S(1)}, bf16[256,1024]{1,0:T(8,128)(2,1)S(1)}, u32[]{:S(2)}, u32[]{:S(2)}) collective-permute-start(bf16[256,1024]{1,0:T(8,128)(2,1)S(1)} %get-tuple-element.209), channel_id=1, source_target_pairs={{0,1},{1,0},{2,3},{3,2},{4,5},{5,4},{6,7},{7,6},{8,9},{9,8},{10,11... | collective-permute-start | bytes 1572872 | tf_op jit(solution)/shard_map/ppermute | solution.py:446
  149.8 14.8 %collective-permute-start.24 = (bf16[256,1024]{1,0:T(8,128)(2,1)S(1)}, bf16[256,1024]{1,0:T(8,128)(2,1)S(1)}, u32[]{:S(2)}, u32[]{:S(2)}) collective-permute-start(bf16[256,1024]{1,0:T(8,128)(2,1)S(1)} %add_convert_fusion.1), channel_id=1, source_target_pairs={{0,2},{1,3},{2,4},{3,5},{4,6},{5,7},{6,0},{7,1},{8,10},{9,11},{10,... | collective-permute-start | bytes 1572872 | tf_op jit(solution)/shard_map/ppermute | solution.py:443
  (14 other events, 37.0 us)
